TPU v7x, 32 devices: a whole 2x2x4 slice. The times are simulated.
32 devices in a mesh: igrp: 4 (over x, core), jgrp: 8 (over z, y).
Axes of the slice: x: 2, y: 2, z: 4, core: 2. Of those that a mesh axis runs over, the one named last changes fastest.
Arguments:
- t_start: bfloat16 [64, 64, 256, 256], P('igrp', 'jgrp'), may hold values from -2.390625 to 2.390625
- integrals: bfloat16 [64, 64, 256, 256], P('igrp', 'jgrp'), may hold values from -6 to 6
- weights: bfloat16 [64, 8, 256, 256], P('igrp'), may hold values from -0.125 to 0.125
- neighbours: int32 [64, 8], replicated, may hold values from 0 to 63, as said below
- eps_occ: float32 [64], replicated, may hold values from -2 to -0.5
- eps_vir: float32 [256], replicated, may hold values from 0.2 to 4
Outputs:
- amplitudes: float32 [64, 64, 256, 256], P('igrp', 'jgrp')
Inputs may be any that keep to these rules, and one draw needn't show every extreme that they name: `neighbours`: the entries of a row are distinct. For every block of 16 consecutive rows starting at a multiple of 16, and every block of 16 consecutive orbitals starting at a multiple of 16, exactly 2 distinct orbitals of that block appear in those rows.
All inputs are finite; a program needn't handle non-finite values.
Results may differ from a plain program's by a relative error of at most 0.0018.
Values may be sent and summed in bfloat16 or wider, within the bound.
No kernel may reach another device: no remote copies, remote signals or barrier semaphores. Data moves between devices by JAX's collectives and lax.ppermute only.
A program may use at most 256 MiB of HBM per device.

v0:
```python
import jax
import jax.numpy as jnp
from jax import lax
from jax.sharding import PartitionSpec as P

NNB = 8
CAP = 2
ITERS = 2


def first_true(flags, capacity):
    counted = flags.shape[1]
    ranking = jnp.cumsum(flags.astype(jnp.int32), axis=1) - 1
    offsets = jnp.arange(counted, dtype=jnp.int32)
    hits = flags[:, :, None] & (
        ranking[:, :, None] == jnp.arange(capacity, dtype=jnp.int32)[None, None, :]
    )
    return jnp.sum(offsets[None, :, None] * hits.astype(jnp.int32), axis=1)


def transposed(cycle_term):
    section_one = lax.all_to_all(cycle_term, "igrp", split_axis=2, concat_axis=0, tiled=True)
    section_two = lax.all_to_all(section_one, "jgrp", split_axis=0, concat_axis=1, tiled=True)
    section_three = lax.all_to_all(section_two, "igrp", split_axis=1, concat_axis=2, tiled=True)
    return section_three.transpose(1, 0, 3, 2)


def body(t_start, integrals, weights, neighbours, eps_occ, eps_vir):
    row_count = weights.shape[0]
    col_count = t_start.shape[1]
    capacity = CAP
    igroups = lax.axis_size("igrp")
    my_igrp = lax.axis_index("igrp")
    my_jgrp = lax.axis_index("jgrp")
    grouped = neighbours.reshape(igroups, row_count * NNB)
    own_orbitals = my_igrp * row_count + jnp.arange(row_count, dtype=jnp.int32)
    wanted = jnp.any(grouped[:, :, None] == own_orbitals[None, None, :], axis=1)
    send_choice = first_true(wanted, capacity).reshape(-1)
    my_rows = lax.dynamic_slice_in_dim(neighbours, my_igrp * row_count, row_count, 0)
    flat_list = my_rows.reshape(-1)
    all_blocks = jnp.arange(igroups * row_count, dtype=jnp.int32).reshape(igroups, row_count)
    needed = jnp.any(flat_list[None, None, :] == all_blocks[:, :, None], axis=2)
    recv_orbitals = (
        first_true(needed, capacity) + (jnp.arange(igroups, dtype=jnp.int32) * row_count)[:, None]
    ).reshape(-1)
    slot_index = jnp.sum(
        jnp.arange(igroups * capacity, dtype=jnp.int32)[None, None, :]
        * (my_rows[:, :, None] == recv_orbitals[None, None, :]).astype(jnp.int32),
        axis=2,
    )
    occ_rows = lax.dynamic_slice_in_dim(eps_occ, my_igrp * row_count, row_count, 0)
    occ_cols = lax.dynamic_slice_in_dim(eps_occ, my_jgrp * col_count, col_count, 0)
    denominator = (
        eps_vir[None, None, :, None]
        + eps_vir[None, None, None, :]
        - occ_rows[:, None, None, None]
        - occ_cols[None, :, None, None]
    )
    current = t_start
    updated = t_start.astype(jnp.float32)
    for sweep in range(ITERS):
        outgoing = jnp.take(current, send_choice, axis=0)
        received = lax.all_to_all(outgoing, "igrp", split_axis=0, concat_axis=0, tiled=True)

        def per_row(state_in, inputs):
            weight_rows, slot_rows = inputs
            picked = jnp.take(received, slot_rows, axis=0)
            product = jnp.einsum(
                "mac,mjcb->jab", weight_rows, picked, preferred_element_type=jnp.float32
            )
            return (state_in, product.astype(jnp.bfloat16))

        _, cycle_term = lax.scan(per_row, jnp.zeros((), jnp.int32), (weights, slot_index))
        flipped = transposed(cycle_term)
        updated = (
            integrals.astype(jnp.float32)
            + cycle_term.astype(jnp.float32)
            + flipped.astype(jnp.float32)
        ) / denominator
        current = updated.astype(jnp.bfloat16)
    return updated


def solution(mesh):
    placed = (
        P("igrp", "jgrp", None, None),
        P("igrp", "jgrp", None, None),
        P("igrp", None, None, None),
        P(),
        P(),
        P(),
    )
    return jax.shard_map(
        body, mesh=mesh, in_specs=placed, out_specs=P("igrp", "jgrp", None, None), check_vma=False
    )
```

profile of v0, /device:TPU:21, one launch (start us, length us, event | category | flops | bytes accessed | tf_op | source)
XLA Modules:
  0.0 2488.6 jit_solution(378374306922407759)
XLA Ops:
  1.7 10.6 gather_fusion.2
  12.3 7.7 broadcast_select_fusion.1
  27.4 91.2 %all-to-all-done = bf16[8,8,256,256]{3,2,1,0:T(8,128)(2,1)} async-done(((bf16[8,8,256,256]{3,2,1,0:T(8,128)(2,1)}), bf16[8,8,256,256]{3,2,1,0:T(8,128)(2,1)}, u32[]{:S(2)}, u32[]{:S(2)}) %all-to-all-start) | async-done | bytes 8388640 | tf_op jit(solution)/shard_map/all_to_all | solution.py:63
  124.5 248.7 %while.20 = (s32[]{:T(128)}, bf16[16,8,256,256]{2,3,1,0:T(8,128)(2,1)}, s32[16,8]{1,0:T(8,128)S(1)}, bf16[8,8,256,256]{3,2,1,0:T(8,128)(2,1)}, bf16[16,8,256,256]{3,2,1,0:T(8,128)(2,1)}, /*index=5*/s32[]{:T(128)}) while((s32[]{:T(128)}, bf16[16,8,256,256]{2,3,1,0:T(8,128)(2,1)}, s32[16,8]{1,0:T(8,128)S(1)}, ...), condition=%wide.region_8.11_spmd, body=%wide.region_7.10_spmd.sunk | while | flops 2152203264 | bytes 27268312 | solution.py:73
  124.5 8.2 gather_fusion
  140.1 8.2 gather_fusion
  148.3 7.3 fusion.47
  155.7 8.2 gather_fusion
  171.2 8.2 gather_fusion
  186.7 8.2 gather_fusion
  202.3 8.2 gather_fusion
  217.8 8.2 gather_fusion
  233.4 8.2 gather_fusion
  248.9 8.2 gather_fusion
  257.1 7.4 fusion.47
  264.5 8.2 gather_fusion
  280.0 8.2 gather_fusion
  295.6 8.2 gather_fusion
  311.1 8.2 gather_fusion
  319.3 7.3 fusion.47
  326.7 8.2 gather_fusion
  342.2 8.2 gather_fusion
  357.7 8.2 gather_fusion
  373.2 23.4 copy.64
  396.7 187.6 %all_to_all.100 = bf16[16,8,256,256]{3,1,0,2:T(8,128)(2,1)S(1)} all-to-all(bf16[16,8,256,256]{3,1,0,2:T(8,128)(2,1)} %copy.64), channel_id=1, replica_groups=mesh['igrp'=4,'jgrp'=8] {'igrp'}, dimensions={2} | all-to-all | bytes 33554432 | tf_op jit(solution)/shard_map/all_to_all | solution.py:22
  584.2 10.6 copy.66
  594.8 364.4 %all_to_all.101 = bf16[64,8,64,256]{3,2,1,0:T(8,128)(2,1)S(1)} all-to-all(bf16[64,8,64,256]{3,2,1,0:T(8,128)(2,1)S(1)} %bitcast.95), channel_id=1, replica_groups=mesh['igrp'=4,'jgrp'=8] {'jgrp'}, dimensions={0} | all-to-all | bytes 33554432 | tf_op jit(solution)/shard_map/all_to_all | solution.py:23
  968.0 8.9 all-to-all-start.3
  977.0 21.6 copy.57
  1001.1 158.0 %all-to-all-done.3 = bf16[8,64,64,256]{3,2,0,1:T(8,128)(2,1)} async-done(((bf16[8,64,64,256]{3,2,0,1:T(8,128)(2,1)}), bf16[8,64,64,256]{3,2,0,1:T(8,128)(2,1)}, u32[]{:S(2)}, u32[]{:S(2)}) %all-to-all-start.3) | async-done | bytes 16777248 | tf_op jit(solution)/shard_map/all_to_all | solution.py:24
  1159.1 14.2 copy.69
  1173.3 9.7 convert_bitcast_fusion.1
  1183.0 11.3 copy.70
  1194.3 29.2 %fusion.36 = bf16[16,8,256,256]{2,3,0,1:T(8,128)(2,1)} fusion(f32[8,16,4,64,256]{4,3,2,1,0:T(8,128)} %copy.70, bf16[16,8,256,256]{2,3,0,1:T(8,128)(2,1)} %copy.57, bf16[16,8,256,256]{2,3,1,0:T(8,128)(2,1)} %get-tuple-element.61, f32[8]{0:T(128)S(1)} %dynamic_slice.25, f32[16,256,256]{1,2,0:T(8,128)} %broadcast_subtract_fusion), kind=kLoop, calls=%fused_computation.44 | loop fusion | flops 58720256 | bytes 88080416 | tf_op jit(solution)/shard_map/convert_element_type | solution.py:80
  1223.5 10.7 gather_fusion.3
  1234.2 7.6 broadcast_select_fusion
  1241.9 100.4 %all_to_all.102 = bf16[8,8,256,256]{2,3,1,0:T(8,128)(2,1)} all-to-all(bf16[8,8,256,256]{2,3,1,0:T(8,128)(2,1)} %broadcast_select_fusion), channel_id=1, replica_groups=mesh['igrp'=4,'jgrp'=8] {'igrp'}, dimensions={0} | all-to-all | bytes 16777216 | tf_op jit(solution)/shard_map/all_to_all | solution.py:63
  1342.3 11.3 copy.72
  1359.5 256.6 %while.21 = (s32[]{:T(128)}, bf16[16,8,256,256]{2,3,1,0:T(8,128)(2,1)}, s32[16,8]{1,0:T(8,128)}, bf16[8,8,256,256]{3,2,1,0:T(8,128)(2,1)}, bf16[16,8,256,256]{3,2,1,0:T(8,128)(2,1)}, /*index=5*/s32[]{:T(128)}) while((s32[]{:T(128)}, bf16[16,8,256,256]{2,3,1,0:T(8,128)(2,1)}, s32[16,8]{1,0:T(8,128)}, bf16[8,8,256,256]{3,2,1,0:T(8,128)(2,1)}, ...), condition=%wide.region_10.13_spmd, body=%wide.region_9.12_spmd.sunk | while | flops 2152203264 | bytes 27268312 | solution.py:73
  1360.2 8.1 gather_fusion.1
  1376.3 8.1 gather_fusion.1
  1392.3 8.1 gather_fusion.1
  1408.4 8.1 gather_fusion.1
  1424.4 8.1 gather_fusion.1
  1440.4 8.1 gather_fusion.1
  1456.4 8.1 gather_fusion.1
  1472.5 8.1 gather_fusion.1
  1488.5 8.1 gather_fusion.1
  1504.6 8.1 gather_fusion.1
  1520.6 8.1 gather_fusion.1
  1536.7 8.1 gather_fusion.1
  1552.7 8.1 gather_fusion.1
  1568.7 8.1 gather_fusion.1
  1584.8 8.1 gather_fusion.1
  1600.9 8.1 gather_fusion.1
  1616.2 23.4 copy.74
  1639.6 187.7 %all_to_all.103 = bf16[16,8,256,256]{3,1,0,2:T(8,128)(2,1)S(1)} all-to-all(bf16[16,8,256,256]{3,1,0,2:T(8,128)(2,1)} %copy.74), channel_id=1, replica_groups=mesh['igrp'=4,'jgrp'=8] {'igrp'}, dimensions={2} | all-to-all | bytes 33554432 | tf_op jit(solution)/shard_map/all_to_all | solution.py:22
  1827.3 10.6 copy.76
  1837.9 365.6 %all_to_all.104 = bf16[64,8,64,256]{3,2,1,0:T(8,128)(2,1)S(1)} all-to-all(bf16[64,8,64,256]{3,2,1,0:T(8,128)(2,1)S(1)} %bitcast.99), channel_id=1, replica_groups=mesh['igrp'=4,'jgrp'=8] {'jgrp'}, dimensions={0} | all-to-all | bytes 33554432 | tf_op jit(solution)/shard_map/all_to_all | solution.py:23
  2207.6 186.5 %all_to_all.105 = bf16[8,64,64,256]{3,2,0,1:T(8,128)(2,1)S(1)} all-to-all(bf16[8,64,64,256]{3,2,0,1:T(8,128)(2,1)S(1)} %copy.78), channel_id=1, replica_groups=mesh['igrp'=4,'jgrp'=8] {'igrp'}, dimensions={1} | all-to-all | bytes 33554432 | tf_op jit(solution)/shard_map/all_to_all | solution.py:24
  2400.7 9.7 convert_bitcast_fusion
  2410.4 11.3 copy.80
  2421.7 35.0 %subtract_divide_fusion = f32[16,8,256,256]{2,3,0,1:T(8,128)} fusion(bf16[16,8,256,256]{2,3,0,1:T(8,128)(2,1)} %copy.57, f32[8,16,4,64,256]{4,3,2,1,0:T(8,128)} %copy.80, bf16[16,8,256,256]{2,3,1,0:T(8,128)(2,1)} %get-tuple-element.62, f32[8]{0:T(128)S(1)} %copy-done.7, f32[16,256,256]{1,2,0:T(8,128)} %broadcast_subtract_fusion), kind=kLoop, calls=%fused_computation.36 | loop fusion | flops 50331648 | bytes 104857632 | tf_op jit(solution)/shard_map/div | solution.py:75
  2456.7 31.9 %copy.81 = f32[16,8,256,256]{3,2,1,0:T(8,128)} copy(f32[16,8,256,256]{2,3,0,1:T(8,128)} %subtract_divide_fusion) | data formatting | bytes 67108864 | tf_op jit(solution)/shard_map/div | solution.py:75
  (151 shorter events, 265.4 us)
Async XLA Ops:
  1.6 18.3 copy-start.4
  1.7 18.3 copy-start.2
  12.3 14.0 copy-start.1
  20.0 98.6 %all-to-all-start = ((bf16[8,8,256,256]{3,2,1,0:T(8,128)(2,1)}), bf16[8,8,256,256]{3,2,1,0:T(8,128)(2,1)}, u32[]{:S(2)}, u32[]{:S(2)}) async-start(bf16[8,8,256,256]{3,2,1,0:T(8,128)(2,1)} %broadcast_select_fusion.1), calls=%async_computation | async-start | bytes 16777216 | tf_op jit(solution)/shard_map/all_to_all | solution.py:63
  373.2 23.4 copy-start
  968.0 8.9 copy-start.8
  968.0 191.1 %all-to-all-start.3 = ((bf16[8,64,64,256]{3,2,0,1:T(8,128)(2,1)}), bf16[8,64,64,256]{3,2,0,1:T(8,128)(2,1)}, u32[]{:S(2)}, u32[]{:S(2)}) async-start(bf16[8,64,64,256]{3,2,0,1:T(8,128)(2,1)} %copy.68), calls=%async_computation.3 | async-start | bytes 33554432 | tf_op jit(solution)/shard_map/all_to_all | solution.py:24
  977.0 217.3 %copy-start.6 = (f32[8]{0:T(128)}, f32[8]{0:T(128)S(1)}, u32[]{:S(2)}) copy-start(f32[8]{0:T(128)S(1)} %dynamic_slice.25) | copy-start | bytes 100
  977.0 21.6 copy-start.3
  1223.5 10.7 copy-start.5
  2410.4 11.3 copy-start.7
where the time goes:
time: 2500 us; the launch traced here: 2490 us
  blocking collectives  1390 us (56%)
  local copies, waits for them, and re-layouts  485 us (19%)
  waiting for transfers between devices  249 us (10%)
  matrix products  233 us (9%)
  other arithmetic  114 us (5%)
    all_to_all x2, blocking collectives, transposed(): lax.all_to_all(section_one, 'jgrp', split_axis=0, concat_axis=1, tiled=True)  730 us
    all_to_all x2, blocking collectives, transposed(): lax.all_to_all(cycle_term, 'igrp', split_axis=2, concat_axis=0, tiled=True)  375 us
    gather x32, local copies, waits for them, and re-layouts, per_row(): picked = jnp.take(received, slot_rows, axis=0)  261 us
    dot_general x32, matrix products, per_row(): jnp.einsum('mac,mjcb->jab', weight_rows, picked, preferred_element_type=j...  233 us
    all_to_all x1, blocking collectives, transposed(): lax.all_to_all(section_two, 'igrp', split_axis=1, concat_axis=2, tiled=True)  187 us
    all_to_all x1, waiting for transfers between devices, transposed(): lax.all_to_all(section_two, 'igrp', split_axis=1, concat_axis=2, tiled=True)  158 us
    all_to_all x1, blocking collectives, body(): lax.all_to_all(outgoing, 'igrp', split_axis=0, concat_axis=0, tiled=True)  100 us
    all_to_all x1, waiting for transfers between devices, body(): lax.all_to_all(outgoing, 'igrp', split_axis=0, concat_axis=0, tiled=True)  91.2 us
  transfers between devices with their start and end apart: 2, of which 2 were waited for; matrix products, arithmetic and copies ran while one was open for 1% of the time, Pallas kernels for 0%

commit v1 on v0

v1 whole, which is shorter than its diff:
```python
import functools

import jax
import jax.numpy as jnp
from jax import lax
from jax.experimental import pallas as pl
from jax.experimental.pallas import tpu as pltpu
from jax.sharding import PartitionSpec as P

CAP = 2
ITERS = 2
AXES = ("igrp", "jgrp")
VMEM = 56 * 2**20
F32, BF16, I32 = jnp.float32, jnp.bfloat16, jnp.int32


def params():
    return pltpu.CompilerParams(vmem_limit_bytes=VMEM)


def cost(flops, moved):
    return pl.CostEstimate(flops=flops, bytes_accessed=moved, transcendentals=0)


def resident(shape):
    return pl.BlockSpec(shape, lambda *_: (0,) * len(shape))


def listed_offsets(neighbours, groups, rows):
    named = neighbours.reshape(groups, -1)
    every = jnp.arange(groups * rows, dtype=I32)
    flags = jnp.any(named[:, :, None] == every[None, None, :], axis=1).reshape(groups, groups, rows)
    offsets = jnp.arange(rows, dtype=I32)
    before = (offsets[:, None] < offsets[None, :]).astype(I32)
    rank = jnp.sum(flags.astype(I32)[:, :, :, None] * before[None, None], axis=2)
    hits = flags[:, :, :, None] & (rank[:, :, :, None] == jnp.arange(CAP, dtype=I32))
    return jnp.sum(hits.astype(I32) * offsets[None, None, :, None], axis=2)


def relative_slots(neighbours, lists, groups, rows):
    group = jnp.arange(groups, dtype=I32)[:, None, None]
    block = jnp.arange(groups, dtype=I32)[None, :, None]
    orbital = block * rows + lists
    slot = (group ^ block) * CAP + jnp.arange(CAP, dtype=I32)[None, None, :]
    grouped = neighbours.reshape(groups, -1)
    hits = (grouped[:, :, None, None] == orbital[:, None]).astype(I32)
    return jnp.sum(hits * slot[:, None], axis=(2, 3)).reshape(neighbours.shape)


def pick_kernel(rows_ref, *refs):
    half = len(refs) // 2
    for source, target in zip(refs[:half], refs[half:]):
        target[:, 0] = source[0]


def pick_rows(t, rows, groups):
    _, cols, v, _ = t.shape
    return pl.pallas_call(
        pick_kernel,
        out_shape=[jax.ShapeDtypeStruct((cols, CAP, v, v), t.dtype)] * groups,
        grid_spec=pltpu.PrefetchScalarGridSpec(
            num_scalar_prefetch=1,
            grid=(CAP,),
            in_specs=[
                pl.BlockSpec((1, cols, v, v), lambda c, rows, s=s: (rows[s * CAP + c], 0, 0, 0))
                for s in range(groups)
            ],
            out_specs=[pl.BlockSpec((cols, 1, v, v), lambda c, rows: (0, c, 0, 0))] * groups,
        ),
        compiler_params=params(),
        cost_estimate=cost(0, 4 * groups * CAP * cols * v * v),
        name="pick_rows",
    )(rows, *[t] * groups)


def slotted_kernel(slots_ref, w_ref, o_ref):
    listed, v = w_ref.shape[1], w_ref.shape[2]
    row = pl.program_id(0) * listed
    if o_ref.shape[2] > listed * v:
        o_ref[...] = jnp.zeros_like(o_ref)
    for m in range(listed):
        start = pl.multiple_of(slots_ref[row + m] * v, v)
        o_ref[0, :, pl.ds(start, v)] = w_ref[0, m]


def slotted(w, slots, groups):
    rows, listed, v, _ = w.shape
    depth = groups * CAP * v
    return pl.pallas_call(
        slotted_kernel,
        out_shape=jax.ShapeDtypeStruct((rows, v, depth), w.dtype),
        grid_spec=pltpu.PrefetchScalarGridSpec(
            num_scalar_prefetch=1,
            grid=(rows,),
            in_specs=[pl.BlockSpec((1, listed, v, v), lambda i, slots: (i, 0, 0, 0))],
            out_specs=pl.BlockSpec((1, v, depth), lambda i, slots: (i, 0, 0)),
        ),
        compiler_params=params(),
        cost_estimate=cost(0, 4 * rows * v * depth),
        name="slotted",
    )(slots.reshape(-1), w)


def stacked(refs, at):
    v = refs[0].shape[-1]
    return jnp.concatenate([r[at].reshape(-1, v) for r in refs], axis=0)


def direct_kernel(taken, rows_ref, *refs):
    w_refs, t_refs, o_ref = refs[:taken], refs[taken:-1], refs[-1]
    cols, v = o_ref.shape[1], o_ref.shape[2]

    def column(j, carry):
        left = jnp.concatenate([w[0] for w in w_refs], axis=0)
        product = jnp.dot(left, stacked(t_refs, j), preferred_element_type=F32).astype(BF16)
        for q in range(taken):
            o_ref[q, j] = product[q * v : (q + 1) * v]
        return carry

    lax.fori_loop(0, cols, column, 0)


def direct(wp, rows, parts):
    cols, _, v, _ = parts[0].shape
    count, depth = rows.shape[0], wp.shape[2]
    taken = 4 if count % 4 == 0 else 1
    return pl.pallas_call(
        functools.partial(direct_kernel, taken),
        out_shape=jax.ShapeDtypeStruct((count, cols, v, v), BF16),
        grid_spec=pltpu.PrefetchScalarGridSpec(
            num_scalar_prefetch=1,
            grid=(count // taken,),
            in_specs=[
                pl.BlockSpec((1, v, depth), lambda n, rows, q=q: (rows[n * taken + q], 0, 0))
                for q in range(taken)
            ]
            + [resident(p.shape) for p in parts],
            out_specs=pl.BlockSpec((taken, cols, v, v), lambda n, rows: (n, 0, 0, 0)),
        ),
        compiler_params=params(),
        cost_estimate=cost(2 * count * cols * v * v * depth, 2 * count * v * (depth + cols * v)),
        name="direct",
    )(rows, *[wp] * taken, *parts)


def finish_kernel(halves, rows_ref, where_ref, occ_ref, w_ref, c_ref, k_ref, tall_ref, wide_ref, *refs):
    o_ref, base_ref = refs[-2], refs[-1]
    t_refs = refs[:-2]
    cols, v, depth = w_ref.shape
    row = rows_ref[pl.program_id(0)]
    base_ref[...] = tall_ref[...] + wide_ref[...] - occ_ref[where_ref[0] + row]
    taken = 4 if cols % 4 == 0 else 1
    by_half = [t_refs[h::halves] for h in range(halves)]

    def work(parts):
        right = stacked(parts, 0)
        for first in range(0, cols, taken):
            left = w_ref[first : first + taken].reshape(taken * v, depth)
            product = jnp.dot(left, right, preferred_element_type=F32).astype(BF16)
            for q in range(taken):
                j = first + q
                flipped = product[q * v : (q + 1) * v].astype(F32).T
                total = k_ref[0, j].astype(F32) + c_ref[0, j].astype(F32) + flipped
                value = (total / (base_ref[...] - occ_ref[where_ref[1] + j])).astype(o_ref.dtype)
                if o_ref.shape[0] == 1:
                    o_ref[0, j] = value
                else:
                    o_ref[j, 0] = value

    if halves == 1:
        work(by_half[0])
    else:
        here = (row // cols) ^ where_ref[2]
        for h in range(halves):
            pl.when(here == h)(functools.partial(work, by_half[h]))


def kept_kernel(halves, *refs):
    finish_kernel(halves, *refs[:8], *refs[9:])


def finish(wpj, c, c_first, k, tall, wide, occ, where, rows, far, out, into=None):
    cols, v, depth = wpj.shape
    halves, groups = len(far), len(far[0])
    parts = [far[h][s] for s in range(groups) for h in range(halves)]
    part = pl.BlockSpec((1, CAP, v, v), lambda n, rows, where: (rows[n] % cols, 0, 0, 0))
    one_row = (1, cols, v, v)
    by_row = pl.BlockSpec(one_row, lambda n, rows, where: (rows[n], 0, 0, 0))
    kept = [] if into is None else [into]
    return pl.pallas_call(
        functools.partial(finish_kernel if into is None else kept_kernel, halves),
        out_shape=out,
        grid_spec=pltpu.PrefetchScalarGridSpec(
            num_scalar_prefetch=2,
            grid=(rows.shape[0],),
            in_specs=[
                pl.BlockSpec(memory_space=pltpu.SMEM),
                resident(wpj.shape),
                by_row if c_first is None else pl.BlockSpec(one_row, lambda n, rows, where: (c_first + n, 0, 0, 0)),
                by_row,
                resident(tall.shape),
                resident(wide.shape),
            ]
            + [pl.BlockSpec(memory_space=pl.ANY)] * len(kept)
            + [part] * len(parts),
            out_specs=by_row
            if out.dtype == F32
            else pl.BlockSpec((cols, 1, v, v), lambda n, rows, where: (0, n, 0, 0)),
            scratch_shapes=[pltpu.VMEM((v, v), F32)],
        ),
        input_output_aliases={} if into is None else {8: 0},
        compiler_params=params(),
        cost_estimate=cost(2 * rows.shape[0] * cols * v * v * depth, 2 * cols * v * (depth + rows.shape[0] * v * 5)),
        name="finish",
    )(rows, where, occ, wpj, c, k, tall, wide, *kept, *parts)


def exchange(groups, ratio, jgroups, mine):
    near = [mine[0]] + [
        lax.ppermute(mine[s], "igrp", [(i, i ^ s) for i in range(groups)]) for s in range(1, groups)
    ]
    first = [
        lax.ppermute(
            mine[s],
            AXES,
            [
                (i * jgroups + z * ratio + y, z * jgroups + (i ^ s) * ratio + y)
                for i in range(groups)
                for z in range(groups)
                for y in range(ratio)
            ],
        )
        for s in range(groups)
    ]
    far = [first] + [
        [lax.ppermute(f, "jgrp", [(j, j ^ d) for j in range(jgroups)]) for f in first] for d in range(1, ratio)
    ]
    return near, far


def spread_weights(w, groups, ratio, jgroups, my_i, my_z):
    held = [0]
    bit = groups // 2
    while bit:
        pairs = [
            (((z ^ h) * jgroups + z * ratio + y), ((z ^ h ^ bit) * jgroups + z * ratio + y))
            for h in held
            for z in range(groups)
            for y in range(ratio)
        ]
        came = lax.ppermute(w, AXES, pairs)
        fresh = functools.reduce(jnp.logical_or, [(my_i ^ my_z) == (h ^ bit) for h in held])
        w = jnp.where(fresh, came, w)
        held = held + [h ^ bit for h in held]
        bit //= 2
    return w


def body(t_start, integrals, weights, neighbours, eps_occ, eps_vir):
    row_count, cols, v, _ = t_start.shape
    groups, jgroups = lax.axis_size("igrp"), lax.axis_size("jgrp")
    ratio = jgroups // groups
    my_i, my_j = lax.axis_index("igrp"), lax.axis_index("jgrp")
    my_z, my_half = my_j // ratio, my_j % ratio

    lists = listed_offsets(neighbours, groups, row_count)
    slots = relative_slots(neighbours, lists, groups, row_count)
    asked = lax.dynamic_slice_in_dim(lists, my_i, 1, 1)[:, 0]
    order = my_i ^ jnp.arange(groups, dtype=I32)
    rows = jnp.sum(
        asked[None] * (jnp.arange(groups, dtype=I32)[None, :, None] == order[:, None, None]).astype(I32), axis=1
    ).reshape(-1)
    every_row = jnp.arange(row_count, dtype=I32)
    where = jnp.stack([my_i * row_count, my_j * cols, my_half]).astype(I32)
    tall, wide = eps_vir.reshape(v, 1), eps_vir.reshape(1, v)

    mine = pick_rows(t_start, rows, groups)
    half_w = lax.dynamic_slice_in_dim(weights, my_half * cols, cols, 0)
    wj = spread_weights(half_w, groups, ratio, jgroups, my_i, my_z)
    wp = slotted(weights, lax.dynamic_slice_in_dim(slots, my_i * row_count, row_count, 0), groups)
    wpj = slotted(wj, lax.dynamic_slice_in_dim(slots, my_j * cols, cols, 0), groups)

    for sweep in range(ITERS - 1):
        near, far = exchange(groups, ratio, jgroups, mine)
        c = direct(wp, rows, near)
        mine = [
            finish(
                wpj, c, s * CAP, integrals, tall, wide, eps_occ, where, rows[s * CAP : (s + 1) * CAP], far,
                jax.ShapeDtypeStruct((cols, CAP, v, v), BF16),
            )
            for s in range(groups)
        ]
    near, far = exchange(groups, ratio, jgroups, mine)
    c = direct(wp, every_row, near)
    updated = None
    for d in range(ratio):
        half_rows = (my_half ^ d) * cols + jnp.arange(cols, dtype=I32)
        updated = finish(
            wpj, c, None, integrals, tall, wide, eps_occ, where, half_rows, far[d : d + 1],
            jax.ShapeDtypeStruct((row_count, cols, v, v), F32), updated,
        )
    return updated


def solution(mesh):
    placed = (
        P("igrp", "jgrp", None, None),
        P("igrp", "jgrp", None, None),
        P("igrp", None, None, None),
        P(),
        P(),
        P(),
    )
    return jax.shard_map(
        body, mesh=mesh, in_specs=placed, out_specs=P("igrp", "jgrp", None, None), check_vma=False
    )
```

time: 2500 us -> 878 us (0.35)
  blocking collectives: 1390 us -> 0 us
  local copies, waits for them, and re-layouts: 485 us -> 13.6 us
  matrix products: 233 us -> 0 us
  Pallas kernels: 0 us -> 221 us
  waiting for transfers between devices: 249 us -> 469 us
  starting transfers between devices: 15.2 us -> 154 us
  other arithmetic: 114 us -> 16.9 us
    all_to_all x6 -> x0, blocking collectives: 1390 us -> none  [the longest x2 730 us: transposed(): lax.all_to_all(section_one, 'jgrp', split_axis=0, concat_axis=1, tiled=True)]
    ppermute x0 -> x24, waiting for transfers between devices: none -> 469 us  [the longest x8 343 us: exchange(): lax.ppermute(mine[s], AXES, [(i * jgroups + z * ratio + y, z * jgroups +...]
    gather x34 -> x0, local copies, waits for them, and re-layouts: 282 us -> none  [the longest x32 261 us: per_row(): picked = jnp.take(received, slot_rows, axis=0)]
    all_to_all x2 -> x0, waiting for transfers between devices: 249 us -> none  [the longest x1 158 us: transposed(): lax.all_to_all(section_two, 'igrp', split_axis=1, concat_axis=2, tiled=True)]
    dot_general x32 -> x0, matrix products: 233 us -> none  [per_row(): jnp.einsum('mac,mjcb->jab', weight_rows, picked, preferred_element_type=j...]
    pallas_call x0 -> x11, Pallas kernels: none -> 221 us  [the longest x6 109 us: finish(): pl.pallas_call(functools.partial(finish_kernel if into is None else kept_...]
    ppermute x0 -> x24, starting transfers between devices: none -> 154 us  [the longest x8 130 us: exchange(): lax.ppermute(mine[s], AXES, [(i * jgroups + z * ratio + y, z * jgroups +...]
    while x4 -> x0, local copies, waits for them, and re-layouts: 58.2 us -> none  [body(): lax.scan(per_row, jnp.zeros((), jnp.int32), (weights, slot_index))]
  transfers between devices with their start and end apart: 2 -> 24, of which waited for: 2 -> 11; matrix products, arithmetic and copies ran while one was open for 1% -> 2% of each run, Pallas kernels for 0% -> 20%
where the time goes in v1:
time: 878 us; the launch traced here: 875 us
  waiting for transfers between devices  469 us (53%)
  Pallas kernels  221 us (25%)
  starting transfers between devices  154 us (18%)
  other arithmetic  16.9 us (2%)
  local copies, waits for them, and re-layouts  13.6 us (2%)
    ppermute x8, waiting for transfers between devices, exchange(): lax.ppermute(mine[s], AXES, [(i * jgroups + z * ratio + y, z * jgroups +...  343 us
    ppermute x8, starting transfers between devices, exchange(): lax.ppermute(mine[s], AXES, [(i * jgroups + z * ratio + y, z * jgroups +...  130 us
    pallas_call x6, Pallas kernels, finish(): pl.pallas_call(functools.partial(finish_kernel if into is None else kept_...  109 us
    ppermute x8, waiting for transfers between devices, exchange(): lax.ppermute(f, 'jgrp', [(j, j ^ d) for j in range(jgroups)])  107 us
    pallas_call x2, Pallas kernels, direct(): pl.pallas_call(functools.partial(direct_kernel, taken), out_shape=jax.Sha...  75.9 us
    pallas_call x2, Pallas kernels, slotted(): pl.pallas_call(slotted_kernel, out_shape=jax.ShapeDtypeStruct((rows, v, d...  28.3 us
    ppermute x6, waiting for transfers between devices, exchange(): lax.ppermute(mine[s], 'igrp', [(i, i ^ s) for i in range(groups)])  18.9 us
  transfers between devices with their start and end apart: 24, of which 11 were waited for; matrix products, arithmetic and copies ran while one was open for 2% of the time, Pallas kernels for 20%

profile of v1, /device:TPU:21, one launch (start us, length us, event | category | flops | bytes accessed | tf_op | source)
XLA Modules:
  0.0 875.0 jit_solution(17627299580325074136)
XLA Ops:
  0.0 7.8 constant_dynamic-slice_fusion.2
  7.8 3.9 collective-permute-start
  11.7 7.2 broadcast_select_fusion
  18.9 1.3 collective-permute-start.1
  20.2 0.1 copy.28
  20.3 0.1 eq.68
  20.4 0.1 fusion
  20.5 0.1 and.23
  20.6 0.1 multiply_reduce_fusion
  20.8 0.2 select_reduce_fusion.1
  21.0 0.1 constant_dynamic-slice_fusion
  21.1 0.1 copy.29
  21.2 0.1 multiply_reduce_fusion.1
  21.4 0.1 copy.30
  21.5 0.7 reshape.107.rows_ref
  22.2 7.6 pick_rows.1
  29.8 3.6 collective-permute-start.5
  33.4 121.7 %collective-permute-start.7 = (bf16[8,2,256,256]{3,2,1,0:T(8,128)(2,1)}, bf16[8,2,256,256]{3,2,1,0:T(8,128)(2,1)}, u32[]{:S(2)}, u32[]{:S(2)}) collective-permute-start(bf16[8,2,256,256]{3,2,1,0:T(8,128)(2,1)} %get-tuple-element.10), channel_id=1, source_target_pairs={{0,2},{1,3},{2,10},{3,11},{4,18},{5,19},{6,26},{7,27},{8,0},{9,1},... | collective-permute-start | bytes 6291464 | tf_op jit(solution)/shard_map/ppermute | solution.py:223
  155.2 134.0 %collective-permute-done.7.refs_2_ = bf16[8,2,256,256]{3,2,1,0:T(8,128)(2,1)} collective-permute-done((bf16[8,2,256,256]{3,2,1,0:T(8,128)(2,1)}, bf16[8,2,256,256]{3,2,1,0:T(8,128)(2,1)}, u32[]{:S(2)}, u32[]{:S(2)}) %collective-permute-start.7) | collective-permute-done | bytes 2097184 | tf_op jit(solution)/shard_map/ppermute | solution.py:223
  289.3 1.1 collective-permute-start.4
  290.4 0.1 select_reduce_fusion
  290.5 0.1 reshape.104
  290.6 0.6 reshape.106.slots_ref
  291.2 0.7 reshape.105.slots_ref
  291.9 0.8 copy.31.tall_ref.refs_6_
  292.7 18.5 %slotted.3.refs_0_.refs_1_.refs_2_.refs_3_ = bf16[16,256,2048]{2,1,0:T(8,128)(2,1)} custom-call(s32[128]{0:T(128)} %reshape.106.slots_ref, bf16[16,8,256,256]{3,2,1,0:T(8,128)(2,1)} %w_ref.1), custom_call_target="tpu_custom_call" | custom-call | bytes 33554432 | tf_op jit(solution)/shard_map/slotted/pallas_call | solution.py:89
  311.2 0.6 pad_add_fusion.where_ref.refs_1_
  311.7 0.8 slice_reduce_fusion
  312.5 0.2 collective-permute-start.6
  312.8 1.2 collective-permute-start.8
  314.0 46.2 %collective-permute-done.11.refs_6_ = bf16[8,2,256,256]{3,2,1,0:T(8,128)(2,1)} collective-permute-done((bf16[8,2,256,256]{3,2,1,0:T(8,128)(2,1)}, bf16[8,2,256,256]{3,2,1,0:T(8,128)(2,1)}, u32[]{:S(2)}, u32[]{:S(2)}) %collective-permute-start.11) | collective-permute-done | bytes 2097184 | tf_op jit(solution)/shard_map/ppermute | solution.py:223
  360.2 0.2 collective-permute-start.10
  360.4 17.1 %collective-permute-done.4.refs_7_ = bf16[8,2,256,256]{3,2,1,0:T(8,128)(2,1)} collective-permute-done((bf16[8,2,256,256]{3,2,1,0:T(8,128)(2,1)}, bf16[8,2,256,256]{3,2,1,0:T(8,128)(2,1)}, u32[]{:S(2)}, u32[]{:S(2)}) %collective-permute-start.4) | collective-permute-done | bytes 2097184 | tf_op jit(solution)/shard_map/ppermute | solution.py:220
  377.5 0.2 collective-permute-start.12
  377.7 27.9 %direct.2.c_ref = bf16[8,8,256,256]{3,2,1,0:T(8,128)(2,1)} custom-call(s32[8]{0:T(128)} %reshape.107.rows_ref, bf16[16,256,2048]{2,1,0:T(8,128)(2,1)} %slotted.3.refs_0_.refs_1_.refs_2_.refs_3_, bf16[16,256,2048]{2,1,0:T(8,128)(2,1)} %slotted.3.refs_0_.refs_1_.refs_2_.refs_3_, bf16[16,256,2048]{2,1,0:T(8,128)(2,1)} %slotted.3.refs_0_.refs_1_.refs_2_.refs_3_, ...), custom_call_target="tpu_custom_call" | custom-call | flops 17179869184 | bytes 16777216 | tf_op jit(solution)/shard_map/direct/pallas_call | solution.py:127
  405.6 7.2 broadcast_select_fusion.1.w_ref
  412.9 9.9 %slotted.2.w_ref.refs_3_ = bf16[8,256,2048]{2,1,0:T(8,128)(2,1)} custom-call(s32[64]{0:T(128)} %reshape.105.slots_ref, bf16[8,8,256,256]{3,2,1,0:T(8,128)(2,1)} %broadcast_select_fusion.1.w_ref), custom_call_target="tpu_custom_call" | custom-call | bytes 16777216 | tf_op jit(solution)/shard_map/slotted/pallas_call | solution.py:89
  422.8 27.5 %collective-permute-done.10.refs_5_ = bf16[8,2,256,256]{3,2,1,0:T(8,128)(2,1)} collective-permute-done((bf16[8,2,256,256]{3,2,1,0:T(8,128)(2,1)}, bf16[8,2,256,256]{3,2,1,0:T(8,128)(2,1)}, u32[]{:S(2)}, u32[]{:S(2)}) %collective-permute-start.10) | collective-permute-done | bytes 2097184 | tf_op jit(solution)/shard_map/ppermute | solution.py:236
  450.2 41.5 %collective-permute-done.12.refs_7_ = bf16[8,2,256,256]{3,2,1,0:T(8,128)(2,1)} collective-permute-done((bf16[8,2,256,256]{3,2,1,0:T(8,128)(2,1)}, bf16[8,2,256,256]{3,2,1,0:T(8,128)(2,1)}, u32[]{:S(2)}, u32[]{:S(2)}) %collective-permute-start.12) | collective-permute-done | bytes 2097184 | tf_op jit(solution)/shard_map/ppermute | solution.py:236
  491.7 12.4 %finish.6.refs_4_ = bf16[8,2,256,256]{3,2,1,0:T(8,128)(2,1)} custom-call(s32[2]{0:T(128)} %get-tuple-element.16.rows_ref, s32[3]{0:T(128)} %pad_add_fusion.where_ref.refs_1_, f32[64]{0:T(128)} %refs_2_.3, bf16[8,256,2048]{2,1,0:T(8,128)(2,1)} %slotted.2.w_ref.refs_3_, bf16[8,8,256,256]{3,2,1,0:T(8,128)(2,1)} %direct.2.c_ref, ...), custom_call_target="tpu_custom_call" | custom-call | flops 4294967296 | bytes 18874368 | tf_op jit(solution)/shard_map/finish/pallas_call | solution.py:190
  504.1 4.2 collective-permute-start.16
  508.3 12.5 %finish.7 = bf16[8,2,256,256]{3,2,1,0:T(8,128)(2,1)} custom-call(s32[2]{0:T(128)} %get-tuple-element.15.rows_ref, s32[3]{0:T(128)} %pad_add_fusion.where_ref.refs_1_, f32[64]{0:T(128)} %refs_2_.3, bf16[8,256,2048]{2,1,0:T(8,128)(2,1)} %slotted.2.w_ref.refs_3_, bf16[8,8,256,256]{3,2,1,0:T(8,128)(2,1)} %direct.2.c_ref, bf16[16,8,256,256]{3,2,1,0:T(8,128)(2,1)} %refs_5_.1, ...), custom_call_target="tpu_custom_call" | custom-call | flops 4294967296 | bytes 18874368 | tf_op jit(solution)/shard_map/finish/pallas_call | solution.py:190
  520.9 0.9 collective-permute-start.13
  521.8 12.4 %finish.8 = bf16[8,2,256,256]{3,2,1,0:T(8,128)(2,1)} custom-call(s32[2]{0:T(128)} %get-tuple-element.14.rows_ref, s32[3]{0:T(128)} %pad_add_fusion.where_ref.refs_1_, f32[64]{0:T(128)} %refs_2_.3, bf16[8,256,2048]{2,1,0:T(8,128)(2,1)} %slotted.2.w_ref.refs_3_, bf16[8,8,256,256]{3,2,1,0:T(8,128)(2,1)} %direct.2.c_ref, bf16[16,8,256,256]{3,2,1,0:T(8,128)(2,1)} %refs_5_.1, ...), custom_call_target="tpu_custom_call" | custom-call | flops 4294967296 | bytes 18874368 | tf_op jit(solution)/shard_map/finish/pallas_call | solution.py:190
  534.2 0.3 collective-permute-start.18
  534.5 13.7 %collective-permute-start.14 = (bf16[8,2,256,256]{3,2,1,0:T(8,128)(2,1)}, bf16[8,2,256,256]{3,2,1,0:T(8,128)(2,1)}, u32[]{:S(2)}, u32[]{:S(2)}) collective-permute-start(bf16[8,2,256,256]{3,2,1,0:T(8,128)(2,1)} %finish.8), channel_id=1, source_target_pairs={{0,16},{8,24},{16,0},{24,8},{1,17},{9,25},{17,1},{25,9},{2,18},{10... | collective-permute-start | bytes 6291464 | tf_op jit(solution)/shard_map/ppermute | solution.py:220
  548.2 12.4 %finish.9 = bf16[8,2,256,256]{3,2,1,0:T(8,128)(2,1)} custom-call(s32[2]{0:T(128)} %get-tuple-element.13.rows_ref, s32[3]{0:T(128)} %pad_add_fusion.where_ref.refs_1_, f32[64]{0:T(128)} %refs_2_.3, bf16[8,256,2048]{2,1,0:T(8,128)(2,1)} %slotted.2.w_ref.refs_3_, bf16[8,8,256,256]{3,2,1,0:T(8,128)(2,1)} %direct.2.c_ref, bf16[16,8,256,256]{3,2,1,0:T(8,128)(2,1)} %refs_5_.1, ...), custom_call_target="tpu_custom_call" | custom-call | flops 4294967296 | bytes 18874368 | tf_op jit(solution)/shard_map/finish/pallas_call | solution.py:190
  560.6 60.8 %collective-permute-done.16.refs_0_ = bf16[8,2,256,256]{3,2,1,0:T(8,128)(2,1)} collective-permute-done((bf16[8,2,256,256]{3,2,1,0:T(8,128)(2,1)}, bf16[8,2,256,256]{3,2,1,0:T(8,128)(2,1)}, u32[]{:S(2)}, u32[]{:S(2)}) %collective-permute-start.16) | collective-permute-done | bytes 2097184 | tf_op jit(solution)/shard_map/ppermute | solution.py:223
  621.4 40.5 %collective-permute-done.17.refs_1_ = bf16[8,2,256,256]{3,2,1,0:T(8,128)(2,1)} collective-permute-done((bf16[8,2,256,256]{3,2,1,0:T(8,128)(2,1)}, bf16[8,2,256,256]{3,2,1,0:T(8,128)(2,1)}, u32[]{:S(2)}, u32[]{:S(2)}) %collective-permute-start.17) | collective-permute-done | bytes 2097184 | tf_op jit(solution)/shard_map/ppermute | solution.py:223
  661.9 0.5 iota_add_fusion.1.rows_ref
  662.4 0.5 iota_add_fusion.2.refs_0_
  662.9 0.2 collective-permute-start.20
  663.1 18.8 %collective-permute-done.18.refs_2_ = bf16[8,2,256,256]{3,2,1,0:T(8,128)(2,1)S(1)} collective-permute-done((bf16[8,2,256,256]{3,2,1,0:T(8,128)(2,1)}, bf16[8,2,256,256]{3,2,1,0:T(8,128)(2,1)S(1)}, u32[]{:S(2)}, u32[]{:S(2)}) %collective-permute-start.18) | collective-permute-done | bytes 2097184 | tf_op jit(solution)/shard_map/ppermute | solution.py:223
  682.0 0.2 collective-permute-start.21
  682.2 1.1 copy-done.6
  683.3 0.2 collective-permute-start.22
  683.6 43.0 %collective-permute-done.19.refs_3_ = bf16[8,2,256,256]{3,2,1,0:T(8,128)(2,1)} collective-permute-done((bf16[8,2,256,256]{3,2,1,0:T(8,128)(2,1)}, bf16[8,2,256,256]{3,2,1,0:T(8,128)(2,1)}, u32[]{:S(2)}, u32[]{:S(2)}) %collective-permute-start.19) | collective-permute-done | bytes 2097184 | tf_op jit(solution)/shard_map/ppermute | solution.py:223
  726.6 0.2 collective-permute-start.23
  726.8 1.8 collective-permute-done.15.refs_7_
  728.5 0.5 iota.70.rows_ref
  729.1 48.0 %direct.3.c_ref.refs_4_ = bf16[16,8,256,256]{3,2,1,0:T(8,128)(2,1)} custom-call(s32[16]{0:T(128)} %iota.70.rows_ref, bf16[16,256,2048]{2,1,0:T(8,128)(2,1)} %slotted.3.refs_0_.refs_1_.refs_2_.refs_3_, bf16[16,256,2048]{2,1,0:T(8,128)(2,1)} %slotted.3.refs_0_.refs_1_.refs_2_.refs_3_, bf16[16,256,2048]{2,1,0:T(8,128)(2,1)} %slotted.3.refs_0_.refs_1_.refs_2_.refs_3_, ...), custom_call_target="tpu_custom_call" | custom-call | flops 34359738368 | bytes 33554432 | tf_op jit(solution)/shard_map/direct/pallas_call | solution.py:127
  777.1 29.9 %finish.10.refs_8_ = f32[16,8,256,256]{3,2,1,0:T(8,128)} custom-call(s32[8]{0:T(128)} %iota_add_fusion.1.rows_ref, s32[3]{0:T(128)} %pad_add_fusion.where_ref.refs_1_, f32[64]{0:T(128)} %refs_2_.3, bf16[8,256,2048]{2,1,0:T(8,128)(2,1)} %slotted.2.w_ref.refs_3_, bf16[16,8,256,256]{3,2,1,0:T(8,128)(2,1)} %direct.3.c_ref.refs_4_, ...), custom_call_target="tpu_custom_call" | custom-call | flops 17179869184 | bytes 50331648 | tf_op jit(solution)/shard_map/finish/pallas_call | solution.py:190
  807.0 38.1 %collective-permute-done.23.refs_12_ = bf16[8,2,256,256]{3,2,1,0:T(8,128)(2,1)} collective-permute-done((bf16[8,2,256,256]{3,2,1,0:T(8,128)(2,1)}, bf16[8,2,256,256]{3,2,1,0:T(8,128)(2,1)}, u32[]{:S(2)}, u32[]{:S(2)}) %collective-permute-start.23) | collective-permute-done | bytes 2097184 | tf_op jit(solution)/shard_map/ppermute | solution.py:236
  845.1 29.9 %finish.11 = f32[16,8,256,256]{3,2,1,0:T(8,128)} custom-call(s32[8]{0:T(128)} %iota_add_fusion.2.refs_0_, s32[3]{0:T(128)} %pad_add_fusion.where_ref.refs_1_, f32[64]{0:T(128)} %refs_2_.3, bf16[8,256,2048]{2,1,0:T(8,128)(2,1)} %slotted.2.w_ref.refs_3_, bf16[16,8,256,256]{3,2,1,0:T(8,128)(2,1)} %direct.3.c_ref.refs_4_, ...), custom_call_target="tpu_custom_call", output_to_operand_aliasing={{}: (8, {})} | custom-call | flops 17179869184 | bytes 50331648 | tf_op jit(solution)/shard_map/finish/pallas_call | solution.py:190
  (46 shorter events, 0.3 us)
Async XLA Ops:
  7.8 3.9 collective-permute-start
  11.7 8.5 copy-start.8
  18.9 386.7 %collective-permute-start.1 = (bf16[8,8,256,256]{3,2,1,0:T(8,128)(2,1)}, bf16[8,8,256,256]{3,2,1,0:T(8,128)(2,1)}, u32[]{:S(2)}, u32[]{:S(2)}) collective-permute-start(bf16[8,8,256,256]{3,2,1,0:T(8,128)(2,1)} %broadcast_select_fusion), channel_id=1, source_target_pairs={{0,8},{1,9},{10,2},{11,3},{20,28},{21,29},{30,22},{31,23},{16,24},... | collective-permute-start | bytes 25165832 | tf_op jit(solution)/shard_map/ppermute | solution.py:251
  22.2 269.7 %copy-start.7 = (f32[256]{0:T(256)S(1)}, f32[256]{0:T(256)}, u32[]{:S(2)}) copy-start(f32[256]{0:T(256)} %param.11) | copy-start | bytes 3076
  29.8 125.4 %collective-permute-start.5 = (bf16[8,2,256,256]{3,2,1,0:T(8,128)(2,1)}, bf16[8,2,256,256]{3,2,1,0:T(8,128)(2,1)S(1)}, u32[]{:S(2)}, u32[]{:S(2)}) collective-permute-start(bf16[8,2,256,256]{3,2,1,0:T(8,128)(2,1)} %get-tuple-element.9.refs_4_), channel_id=1, source_target_pairs={{0,0},{1,1},{2,8},{3,9},{4,16},{5,17},{6,24},{7,25},{8,2},{9,3},{1... | collective-permute-start | bytes 6291464 | tf_op jit(solution)/shard_map/ppermute | solution.py:223
  33.4 255.9 %collective-permute-start.7 = (bf16[8,2,256,256]{3,2,1,0:T(8,128)(2,1)}, bf16[8,2,256,256]{3,2,1,0:T(8,128)(2,1)}, u32[]{:S(2)}, u32[]{:S(2)}) collective-permute-start(bf16[8,2,256,256]{3,2,1,0:T(8,128)(2,1)} %get-tuple-element.10), channel_id=1, source_target_pairs={{0,2},{1,3},{2,10},{3,11},{4,18},{5,19},{6,26},{7,27},{8,0},{9,1},... | collective-permute-start | bytes 6291464 | tf_op jit(solution)/shard_map/ppermute | solution.py:223
  155.1 134.1 %collective-permute-start.2 = (bf16[8,2,256,256]{3,2,1,0:T(8,128)(2,1)}, bf16[8,2,256,256]{3,2,1,0:T(8,128)(2,1)}, u32[]{:S(2)}, u32[]{:S(2)}) collective-permute-start(bf16[8,2,256,256]{3,2,1,0:T(8,128)(2,1)} %get-tuple-element.10), channel_id=1, source_target_pairs={{0,8},{8,0},{16,24},{24,16},{1,9},{9,1},{17,25},{25,17},{2,10},{10... | collective-permute-start | bytes 6291464 | tf_op jit(solution)/shard_map/ppermute | solution.py:220
  155.1 157.4 %collective-permute-start.9 = (bf16[8,2,256,256]{3,2,1,0:T(8,128)(2,1)}, bf16[8,2,256,256]{3,2,1,0:T(8,128)(2,1)}, u32[]{:S(2)}, u32[]{:S(2)}) collective-permute-start(bf16[8,2,256,256]{3,2,1,0:T(8,128)(2,1)} %get-tuple-element.11), channel_id=1, source_target_pairs={{0,4},{1,5},{2,12},{3,13},{4,20},{5,21},{6,28},{7,29},{8,6},{9,7},... | collective-permute-start | bytes 6291464 | tf_op jit(solution)/shard_map/ppermute | solution.py:223
  155.2 157.4 %copy-start = (bf16[8,2,256,256]{3,2,1,0:T(8,128)(2,1)}, bf16[8,2,256,256]{3,2,1,0:T(8,128)(2,1)S(1)}, u32[]{:S(2)}) copy-start(bf16[8,2,256,256]{3,2,1,0:T(8,128)(2,1)S(1)} %collective-permute-done.5.refs_0_) | copy-start | bytes 6291460
  155.2 157.6 %collective-permute-start.3 = (bf16[8,2,256,256]{3,2,1,0:T(8,128)(2,1)}, bf16[8,2,256,256]{3,2,1,0:T(8,128)(2,1)}, u32[]{:S(2)}, u32[]{:S(2)}) collective-permute-start(bf16[8,2,256,256]{3,2,1,0:T(8,128)(2,1)} %get-tuple-element.11), channel_id=1, source_target_pairs={{0,16},{8,24},{16,0},{24,8},{1,17},{9,25},{17,1},{25,9},{2,18},{10... | collective-permute-start | bytes 6291464 | tf_op jit(solution)/shard_map/ppermute | solution.py:220
  289.3 70.9 %collective-permute-start.11 = (bf16[8,2,256,256]{3,2,1,0:T(8,128)(2,1)}, bf16[8,2,256,256]{3,2,1,0:T(8,128)(2,1)}, u32[]{:S(2)}, u32[]{:S(2)}) collective-permute-start(bf16[8,2,256,256]{3,2,1,0:T(8,128)(2,1)} %get-tuple-element.12), channel_id=1, source_target_pairs={{0,6},{1,7},{2,14},{3,15},{4,22},{5,23},{6,30},{7,31},{8,4},{9,5},... | collective-permute-start | bytes 6291464 | tf_op jit(solution)/shard_map/ppermute | solution.py:223
  289.3 88.2 %collective-permute-start.4 = (bf16[8,2,256,256]{3,2,1,0:T(8,128)(2,1)}, bf16[8,2,256,256]{3,2,1,0:T(8,128)(2,1)}, u32[]{:S(2)}, u32[]{:S(2)}) collective-permute-start(bf16[8,2,256,256]{3,2,1,0:T(8,128)(2,1)} %get-tuple-element.12), channel_id=1, source_target_pairs={{0,24},{8,16},{16,8},{24,0},{1,25},{9,17},{17,9},{25,1},{2,26},{10... | collective-permute-start | bytes 6291464 | tf_op jit(solution)/shard_map/ppermute | solution.py:220
  312.5 110.2 %collective-permute-start.6 = (bf16[8,2,256,256]{3,2,1,0:T(8,128)(2,1)S(1)}, bf16[8,2,256,256]{3,2,1,0:T(8,128)(2,1)S(1)}, u32[]{:S(2)}, u32[]{:S(2)}) collective-permute-start(bf16[8,2,256,256]{3,2,1,0:T(8,128)(2,1)S(1)} %collective-permute-done.5.refs_0_), channel_id=1, source_target_pairs={{0,1},{1,0},{2,3},{3,2},{4,5},{5,4},{6,7},{7,6},{8,9},{9,8},{10,11... | collective-permute-start | bytes 6291464 | tf_op jit(solution)/shard_map/ppermute | solution.py:236
  312.8 110.0 %collective-permute-start.8 = (bf16[8,2,256,256]{3,2,1,0:T(8,128)(2,1)}, bf16[8,2,256,256]{3,2,1,0:T(8,128)(2,1)S(1)}, u32[]{:S(2)}, u32[]{:S(2)}) collective-permute-start(bf16[8,2,256,256]{3,2,1,0:T(8,128)(2,1)} %collective-permute-done.7.refs_2_), channel_id=1, source_target_pairs={{0,1},{1,0},{2,3},{3,2},{4,5},{5,4},{6,7},{7,6},{8,9},{9,8},{10,11... | collective-permute-start | bytes 6291464 | tf_op jit(solution)/shard_map/ppermute | solution.py:236
  360.2 90.1 %collective-permute-start.10 = (bf16[8,2,256,256]{3,2,1,0:T(8,128)(2,1)}, bf16[8,2,256,256]{3,2,1,0:T(8,128)(2,1)}, u32[]{:S(2)}, u32[]{:S(2)}) collective-permute-start(bf16[8,2,256,256]{3,2,1,0:T(8,128)(2,1)} %collective-permute-done.9.refs_4_), channel_id=1, source_target_pairs={{0,1},{1,0},{2,3},{3,2},{4,5},{5,4},{6,7},{7,6},{8,9},{9,8},{10,11... | collective-permute-start | bytes 6291464 | tf_op jit(solution)/shard_map/ppermute | solution.py:236
  377.5 114.2 %collective-permute-start.12 = (bf16[8,2,256,256]{3,2,1,0:T(8,128)(2,1)}, bf16[8,2,256,256]{3,2,1,0:T(8,128)(2,1)}, u32[]{:S(2)}, u32[]{:S(2)}) collective-permute-start(bf16[8,2,256,256]{3,2,1,0:T(8,128)(2,1)} %collective-permute-done.11.refs_6_), channel_id=1, source_target_pairs={{0,1},{1,0},{2,3},{3,2},{4,5},{5,4},{6,7},{7,6},{8,9},{9,8},{10,11... | collective-permute-start | bytes 6291464 | tf_op jit(solution)/shard_map/ppermute | solution.py:236
  422.7 69.0 %copy-start.1 = (bf16[8,2,256,256]{3,2,1,0:T(8,128)(2,1)}, bf16[8,2,256,256]{3,2,1,0:T(8,128)(2,1)S(1)}, u32[]{:S(2)}) copy-start(bf16[8,2,256,256]{3,2,1,0:T(8,128)(2,1)S(1)} %collective-permute-done.6.refs_1_) | copy-start | bytes 6291460
  422.7 69.0 %copy-start.2 = (bf16[8,2,256,256]{3,2,1,0:T(8,128)(2,1)}, bf16[8,2,256,256]{3,2,1,0:T(8,128)(2,1)S(1)}, u32[]{:S(2)}) copy-start(bf16[8,2,256,256]{3,2,1,0:T(8,128)(2,1)S(1)} %collective-permute-done.8.refs_3_) | copy-start | bytes 6291460
  504.1 117.2 %collective-permute-start.16 = (bf16[8,2,256,256]{3,2,1,0:T(8,128)(2,1)}, bf16[8,2,256,256]{3,2,1,0:T(8,128)(2,1)}, u32[]{:S(2)}, u32[]{:S(2)}) collective-permute-start(bf16[8,2,256,256]{3,2,1,0:T(8,128)(2,1)} %finish.6.refs_4_), channel_id=1, source_target_pairs={{0,0},{1,1},{2,8},{3,9},{4,16},{5,17},{6,24},{7,25},{8,2},{9,3},{1... | collective-permute-start | bytes 6291464 | tf_op jit(solution)/shard_map/ppermute | solution.py:223
  520.8 141.1 %collective-permute-start.17 = (bf16[8,2,256,256]{3,2,1,0:T(8,128)(2,1)}, bf16[8,2,256,256]{3,2,1,0:T(8,128)(2,1)}, u32[]{:S(2)}, u32[]{:S(2)}) collective-permute-start(bf16[8,2,256,256]{3,2,1,0:T(8,128)(2,1)} %finish.7), channel_id=1, source_target_pairs={{0,2},{1,3},{2,10},{3,11},{4,18},{5,19},{6,26},{7,27},{8,0},{9,1},... | collective-permute-start | bytes 6291464 | tf_op jit(solution)/shard_map/ppermute | solution.py:223
  520.9 142.0 %collective-permute-start.13 = (bf16[8,2,256,256]{3,2,1,0:T(8,128)(2,1)}, bf16[8,2,256,256]{3,2,1,0:T(8,128)(2,1)}, u32[]{:S(2)}, u32[]{:S(2)}) collective-permute-start(bf16[8,2,256,256]{3,2,1,0:T(8,128)(2,1)} %finish.7), channel_id=1, source_target_pairs={{0,8},{8,0},{16,24},{24,16},{1,9},{9,1},{17,25},{25,17},{2,10},{10... | collective-permute-start | bytes 6291464 | tf_op jit(solution)/shard_map/ppermute | solution.py:220
  534.2 147.7 %collective-permute-start.18 = (bf16[8,2,256,256]{3,2,1,0:T(8,128)(2,1)}, bf16[8,2,256,256]{3,2,1,0:T(8,128)(2,1)S(1)}, u32[]{:S(2)}, u32[]{:S(2)}) collective-permute-start(bf16[8,2,256,256]{3,2,1,0:T(8,128)(2,1)} %finish.8), channel_id=1, source_target_pairs={{0,4},{1,5},{2,12},{3,13},{4,20},{5,21},{6,28},{7,29},{8,6},{9,7},... | collective-permute-start | bytes 6291464 | tf_op jit(solution)/shard_map/ppermute | solution.py:223
  534.5 148.8 %collective-permute-start.14 = (bf16[8,2,256,256]{3,2,1,0:T(8,128)(2,1)}, bf16[8,2,256,256]{3,2,1,0:T(8,128)(2,1)}, u32[]{:S(2)}, u32[]{:S(2)}) collective-permute-start(bf16[8,2,256,256]{3,2,1,0:T(8,128)(2,1)} %finish.8), channel_id=1, source_target_pairs={{0,16},{8,24},{16,0},{24,8},{1,17},{9,25},{17,1},{25,9},{2,18},{10... | collective-permute-start | bytes 6291464 | tf_op jit(solution)/shard_map/ppermute | solution.py:220
  621.4 105.2 %collective-permute-start.19 = (bf16[8,2,256,256]{3,2,1,0:T(8,128)(2,1)}, bf16[8,2,256,256]{3,2,1,0:T(8,128)(2,1)}, u32[]{:S(2)}, u32[]{:S(2)}) collective-permute-start(bf16[8,2,256,256]{3,2,1,0:T(8,128)(2,1)} %finish.9), channel_id=1, source_target_pairs={{0,6},{1,7},{2,14},{3,15},{4,22},{5,23},{6,30},{7,31},{8,4},{9,5},... | collective-permute-start | bytes 6291464 | tf_op jit(solution)/shard_map/ppermute | solution.py:223
  661.9 66.7 %collective-permute-start.15 = (bf16[8,2,256,256]{3,2,1,0:T(8,128)(2,1)}, bf16[8,2,256,256]{3,2,1,0:T(8,128)(2,1)}, u32[]{:S(2)}, u32[]{:S(2)}) collective-permute-start(bf16[8,2,256,256]{3,2,1,0:T(8,128)(2,1)} %finish.9), channel_id=1, source_target_pairs={{0,24},{8,16},{16,8},{24,0},{1,25},{9,17},{17,9},{25,1},{2,26},{10... | collective-permute-start | bytes 6291464 | tf_op jit(solution)/shard_map/ppermute | solution.py:220
  662.9 144.0 %collective-permute-start.20 = (bf16[8,2,256,256]{3,2,1,0:T(8,128)(2,1)}, bf16[8,2,256,256]{3,2,1,0:T(8,128)(2,1)S(1)}, u32[]{:S(2)}, u32[]{:S(2)}) collective-permute-start(bf16[8,2,256,256]{3,2,1,0:T(8,128)(2,1)} %collective-permute-done.16.refs_0_), channel_id=1, source_target_pairs={{0,1},{1,0},{2,3},{3,2},{4,5},{5,4},{6,7},{7,6},{8,9},{9,8},{10,11... | collective-permute-start | bytes 6291464 | tf_op jit(solution)/shard_map/ppermute | solution.py:236
  682.0 1.4 copy-start.6
  682.0 125.0 %collective-permute-start.21 = (bf16[8,2,256,256]{3,2,1,0:T(8,128)(2,1)}, bf16[8,2,256,256]{3,2,1,0:T(8,128)(2,1)S(1)}, u32[]{:S(2)}, u32[]{:S(2)}) collective-permute-start(bf16[8,2,256,256]{3,2,1,0:T(8,128)(2,1)} %collective-permute-done.17.refs_1_), channel_id=1, source_target_pairs={{0,1},{1,0},{2,3},{3,2},{4,5},{5,4},{6,7},{7,6},{8,9},{9,8},{10,11... | collective-permute-start | bytes 6291464 | tf_op jit(solution)/shard_map/ppermute | solution.py:236
  683.3 123.6 %collective-permute-start.22 = (bf16[8,2,256,256]{3,2,1,0:T(8,128)(2,1)}, bf16[8,2,256,256]{3,2,1,0:T(8,128)(2,1)S(1)}, u32[]{:S(2)}, u32[]{:S(2)}) collective-permute-start(bf16[8,2,256,256]{3,2,1,0:T(8,128)(2,1)} %copy-done.6), channel_id=1, source_target_pairs={{0,1},{1,0},{2,3},{3,2},{4,5},{5,4},{6,7},{7,6},{8,9},{9,8},{10,11... | collective-permute-start | bytes 6291464 | tf_op jit(solution)/shard_map/ppermute | solution.py:236
  726.6 118.5 %collective-permute-start.23 = (bf16[8,2,256,256]{3,2,1,0:T(8,128)(2,1)}, bf16[8,2,256,256]{3,2,1,0:T(8,128)(2,1)}, u32[]{:S(2)}, u32[]{:S(2)}) collective-permute-start(bf16[8,2,256,256]{3,2,1,0:T(8,128)(2,1)} %collective-permute-done.19.refs_3_), channel_id=1, source_target_pairs={{0,1},{1,0},{2,3},{3,2},{4,5},{5,4},{6,7},{7,6},{8,9},{9,8},{10,11... | collective-permute-start | bytes 6291464 | tf_op jit(solution)/shard_map/ppermute | solution.py:236
  806.9 38.1 %copy-start.3 = (bf16[8,2,256,256]{3,2,1,0:T(8,128)(2,1)}, bf16[8,2,256,256]{3,2,1,0:T(8,128)(2,1)S(1)}, u32[]{:S(2)}) copy-start(bf16[8,2,256,256]{3,2,1,0:T(8,128)(2,1)S(1)} %collective-permute-done.20.refs_9_) | copy-start | bytes 6291460
  807.0 38.1 %copy-start.4 = (bf16[8,2,256,256]{3,2,1,0:T(8,128)(2,1)}, bf16[8,2,256,256]{3,2,1,0:T(8,128)(2,1)S(1)}, u32[]{:S(2)}) copy-start(bf16[8,2,256,256]{3,2,1,0:T(8,128)(2,1)S(1)} %collective-permute-done.21.refs_10_) | copy-start | bytes 6291460
  807.0 38.1 %copy-start.5 = (bf16[8,2,256,256]{3,2,1,0:T(8,128)(2,1)}, bf16[8,2,256,256]{3,2,1,0:T(8,128)(2,1)S(1)}, u32[]{:S(2)}) copy-start(bf16[8,2,256,256]{3,2,1,0:T(8,128)(2,1)S(1)} %collective-permute-done.22.refs_11_) | copy-start | bytes 6291460

commit v2 on v1

v2 whole, which is shorter than its diff:
```python
import functools

import jax
import jax.numpy as jnp
from jax import lax
from jax.experimental import pallas as pl
from jax.experimental.pallas import tpu as pltpu
from jax.sharding import PartitionSpec as P

CAP = 2
ITERS = 2
AXES = ("igrp", "jgrp")
VMEM = 56 * 2**20
F32, BF16, I32 = jnp.float32, jnp.bfloat16, jnp.int32


def params():
    return pltpu.CompilerParams(vmem_limit_bytes=VMEM)


def cost(flops, moved):
    return pl.CostEstimate(flops=flops, bytes_accessed=moved, transcendentals=0)


def resident(shape):
    return pl.BlockSpec(shape, lambda *_: (0,) * len(shape))


def listed_offsets(neighbours, groups, rows):
    named = neighbours.reshape(groups, -1)
    every = jnp.arange(groups * rows, dtype=I32)
    flags = jnp.any(named[:, :, None] == every[None, None, :], axis=1).reshape(groups, groups, rows)
    offsets = jnp.arange(rows, dtype=I32)
    before = (offsets[:, None] < offsets[None, :]).astype(I32)
    rank = jnp.sum(flags.astype(I32)[:, :, :, None] * before[None, None], axis=2)
    hits = flags[:, :, :, None] & (rank[:, :, :, None] == jnp.arange(CAP, dtype=I32))
    return jnp.sum(hits.astype(I32) * offsets[None, None, :, None], axis=2)


def relative_slots(neighbours, lists, groups, rows):
    group = jnp.arange(groups, dtype=I32)[:, None, None]
    block = jnp.arange(groups, dtype=I32)[None, :, None]
    orbital = block * rows + lists
    slot = (group ^ block) * CAP + jnp.arange(CAP, dtype=I32)[None, None, :]
    grouped = neighbours.reshape(groups, -1)
    hits = (grouped[:, :, None, None] == orbital[:, None]).astype(I32)
    return jnp.sum(hits * slot[:, None], axis=(2, 3)).reshape(neighbours.shape)


def pick_kernel(rows_ref, *refs):
    half = len(refs) // 2
    for source, target in zip(refs[:half], refs[half:]):
        target[:, 0] = source[0]


def pick_rows(t, rows, groups, width, chunk):
    v = t.shape[-1]
    return pl.pallas_call(
        pick_kernel,
        out_shape=[jax.ShapeDtypeStruct((width, CAP, v, v), t.dtype)] * groups,
        grid_spec=pltpu.PrefetchScalarGridSpec(
            num_scalar_prefetch=1,
            grid=(CAP,),
            in_specs=[
                pl.BlockSpec((1, width, v, v), lambda c, rows, s=s: (rows[s * CAP + c], chunk, 0, 0))
                for s in range(groups)
            ],
            out_specs=[pl.BlockSpec((width, 1, v, v), lambda c, rows: (0, c, 0, 0))] * groups,
        ),
        compiler_params=params(),
        cost_estimate=cost(0, 4 * groups * CAP * width * v * v),
        name="pick_rows",
    )(rows, *[t] * groups)


def tie_kernel(*refs):
    pass


def tie(arrays, earlier):
    if not arrays:
        return arrays
    known = {id(x) for x in arrays}
    earlier = [x for x in earlier if id(x) not in known]
    return pl.pallas_call(
        tie_kernel,
        out_shape=[jax.ShapeDtypeStruct(x.shape, x.dtype) for x in arrays],
        in_specs=[pl.BlockSpec(memory_space=pl.ANY)] * (len(arrays) + len(earlier)),
        out_specs=[pl.BlockSpec(memory_space=pl.ANY)] * len(arrays),
        input_output_aliases={n: n for n in range(len(arrays))},
        name="tie",
    )(*arrays, *earlier)


def slotted_kernel(slots_ref, pick_ref, *refs):
    w_refs, o_ref = refs[:-1], refs[-1]
    listed, v = w_refs[0].shape[1], w_refs[0].shape[2]
    row = pl.program_id(0) * listed
    if o_ref.shape[2] > listed * v:
        o_ref[...] = jnp.zeros_like(o_ref)

    def place(w_ref):
        for m in range(listed):
            start = pl.multiple_of(slots_ref[row + m] * v, v)
            o_ref[0, :, pl.ds(start, v)] = w_ref[0, m]

    for n, w_ref in enumerate(w_refs):
        pl.when(pick_ref[0] == n)(functools.partial(place, w_ref))


def slotted(sources, pick, slots, groups):
    rows, listed, v, _ = sources[0].shape
    depth = groups * CAP * v
    return pl.pallas_call(
        slotted_kernel,
        out_shape=jax.ShapeDtypeStruct((rows, v, depth), sources[0].dtype),
        grid_spec=pltpu.PrefetchScalarGridSpec(
            num_scalar_prefetch=2,
            grid=(rows,),
            in_specs=[pl.BlockSpec((1, listed, v, v), lambda i, slots, pick: (i, 0, 0, 0))] * len(sources),
            out_specs=pl.BlockSpec((1, v, depth), lambda i, slots, pick: (i, 0, 0)),
        ),
        compiler_params=params(),
        cost_estimate=cost(0, 4 * rows * v * depth),
        name="slotted",
    )(slots.reshape(-1), jnp.reshape(pick, (1,)).astype(I32), *sources)


def stacked(refs, at):
    v = refs[0].shape[-1]
    return jnp.concatenate([r[at].reshape(-1, v) for r in refs], axis=0)


def direct_kernel(taken, rows_ref, *refs):
    w_refs, t_refs, o_ref = refs[:taken], refs[taken:-1], refs[-1]
    cols, v = o_ref.shape[1], o_ref.shape[2]

    def column(j, carry):
        left = jnp.concatenate([w[0] for w in w_refs], axis=0)
        product = jnp.dot(left, stacked(t_refs, j), preferred_element_type=F32).astype(BF16)
        for q in range(taken):
            o_ref[q, j] = product[q * v : (q + 1) * v]
        return carry

    lax.fori_loop(0, cols, column, 0)


def direct(wp, rows, parts, placed=False):
    cols, _, v, _ = parts[0].shape
    count, depth = rows.shape[0], wp.shape[2]
    taken = cols if placed else 4 if count % 4 == 0 else 1
    return pl.pallas_call(
        functools.partial(direct_kernel, taken),
        out_shape=jax.ShapeDtypeStruct((wp.shape[0] if placed else count, cols, v, v), BF16),
        grid_spec=pltpu.PrefetchScalarGridSpec(
            num_scalar_prefetch=1,
            grid=(count // taken,),
            in_specs=[
                pl.BlockSpec((1, v, depth), lambda n, rows, q=q: (rows[n * taken + q], 0, 0))
                for q in range(taken)
            ]
            + [resident(p.shape) for p in parts],
            out_specs=pl.BlockSpec(
                (taken, cols, v, v), lambda n, rows: (rows[n * taken] // taken if placed else n, 0, 0, 0)
            ),
        ),
        compiler_params=params(),
        cost_estimate=cost(2 * count * cols * v * v * depth, 2 * count * v * (depth + cols * v)),
        name="direct",
    )(rows, *[wp] * taken, *parts)


def finish_kernel(sets, rows_ref, crows_ref, where_ref, held_ref, use_ref, occ_ref, tall_ref, wide_ref, *refs):
    (spans, groups), choices, outs, flip = sets
    base_ref, right_ref, made_ref = refs[-3:]
    o_refs = refs[-3 - outs : -3]
    w_refs, refs = refs[:spans], refs[spans:]
    if not flip:
        c_refs, k_refs, refs = refs[:spans], refs[spans : 2 * spans], refs[2 * spans :]
    t_refs = refs[: choices * groups]
    width, v, depth = w_refs[0].shape
    step = pl.program_id(0)
    if not flip:
        base_ref[...] = tall_ref[...] + wide_ref[...] - occ_ref[where_ref[0] + rows_ref[step]]

    def load(first):
        for s in range(groups):
            piece = t_refs[first * groups + s][0].reshape(CAP * v, v)
            right_ref[s * CAP * v : (s + 1) * CAP * v] = piece

    if choices > 1:
        for n in range(choices):
            pl.when(use_ref[step] == n)(functools.partial(load, n))
    for n in range(spans):
        left = w_refs[n][...].reshape(width * v, depth)
        right = right_ref[...] if choices > 1 else stacked(t_refs, 0)
        product = jnp.dot(left, right, preferred_element_type=F32).astype(BF16)
        for j in range(width):
            value = product[j * v : (j + 1) * v].astype(F32).T
            if not flip:
                total = k_refs[n][0, j].astype(F32) + c_refs[n][0, j].astype(F32) + value
                column = where_ref[1] + where_ref[3] + n * width + j
                value = total / (base_ref[...] - occ_ref[column])
            value = value.astype(o_refs[0].dtype)
            if outs > 1:
                made_ref[j] = value
            else:
                o_refs[0][0, n * width + j] = value

    def store(o_ref):
        o_ref[:, 0] = made_ref[...]

    if outs > 1:
        for p in range(outs):
            pl.when(step // CAP == p)(functools.partial(store, o_refs[p]))


def kept_kernel(sets, *refs):
    finish_kernel(sets, *refs[:8], *refs[9:])


def finish(w, c, crows, chunks, k, tall, wide, occ, where, rows, use, far, out, into=None):
    w = [w[h] for h in chunks]
    width, v, depth = w[0].shape
    choices, groups = len(far), len(far[0])
    parts = [t for one in far for t in one]
    spans, steps = len(chunks), rows.shape[0]
    flip = c is None
    where = jnp.concatenate([where, jnp.full((1,), chunks[0] * width, I32)])
    at = rows % width
    reads = use[None] == jnp.arange(choices, dtype=I32)[:, None]
    order = jnp.arange(steps, dtype=I32)
    gap = order[None] - order[:, None]
    rank = jnp.where(gap >= 0, gap, steps - gap)
    rank = jnp.where(reads[:, None], rank[None], 4 * steps)
    nearest = (rank == jnp.min(rank, axis=2, keepdims=True)).astype(I32)
    held = jnp.where(jnp.any(reads, axis=1)[:, None], jnp.sum(nearest * at, axis=2), 0).reshape(-1)
    part = [
        pl.BlockSpec((1, CAP, v, v), lambda n, rows, crows, where, held, use, i=i: (held[i * steps + n], 0, 0, 0))
        for i in range(choices)
        for _ in range(groups)
    ]
    one_row = (1, width, v, v)
    kept = [] if into is None else [into]
    sets = ((spans, groups), choices, len(out), flip)
    if flip:
        out_specs = [pl.BlockSpec(one_row, lambda n, *_: (n, 0, 0, 0))]
    elif out[0].dtype == F32:
        place = chunks[0] if spans == 1 else 0
        out_specs = [pl.BlockSpec((1, spans * width, v, v), lambda n, rows, *_: (rows[n], place, 0, 0))]
    else:
        out_specs = [
            pl.BlockSpec((width, 1, v, v), lambda n, *_, p=p: (0, jnp.clip(n - p * CAP, 0, CAP - 1), 0, 0))
            for p in range(len(out))
        ]
    added, added_specs = [], []
    if not flip:
        added = [*c, *[k] * spans]
        added_specs = [pl.BlockSpec(one_row, lambda n, rows, crows, *_: (crows[n], 0, 0, 0))] * spans
        added_specs += [pl.BlockSpec(one_row, lambda n, rows, *_, h=h: (rows[n], h, 0, 0)) for h in chunks]
    return pl.pallas_call(
        functools.partial(finish_kernel if into is None else kept_kernel, sets),
        out_shape=out,
        grid_spec=pltpu.PrefetchScalarGridSpec(
            num_scalar_prefetch=5,
            grid=(steps,),
            in_specs=[pl.BlockSpec(memory_space=pltpu.SMEM), resident(tall.shape), resident(wide.shape)]
            + [pl.BlockSpec(memory_space=pl.ANY)] * len(kept)
            + [resident(x.shape) for x in w]
            + added_specs
            + part,
            out_specs=out_specs,
            scratch_shapes=[
                pltpu.VMEM((v, v), F32),
                pltpu.VMEM((depth, v), BF16),
                pltpu.VMEM((width, v, v), BF16),
            ],
        ),
        input_output_aliases={} if into is None else {8: 0},
        compiler_params=params(),
        cost_estimate=cost(
            2 * steps * spans * width * v * v * depth, 2 * spans * width * v * (depth + steps * v * 5)
        ),
        name="finish",
    )(rows, crows, where, held, use, occ, tall, wide, *kept, *w, *added, *parts)


def joined_kernel(groups, rows_ref, where_ref, occ_ref, tall_ref, wide_ref, into_ref, *refs):
    ct_ref, k_ref, o_ref = refs[-3:]
    taken, width, v, _ = o_ref.shape
    w_refs, t_refs = refs[:taken], refs[taken : taken + groups]
    first = pl.program_id(0) * taken

    def column(j, carry):
        left = jnp.concatenate([w[0] for w in w_refs], axis=0)
        product = jnp.dot(left, stacked(t_refs, j), preferred_element_type=F32).astype(BF16)
        for q in range(taken):
            base = tall_ref[...] + wide_ref[...] - occ_ref[where_ref[0] + rows_ref[first + q]]
            total = k_ref[q, j].astype(F32) + product[q * v : (q + 1) * v].astype(F32) + ct_ref[q, j].astype(F32)
            o_ref[q, j] = total / (base - occ_ref[where_ref[1] + where_ref[3] + j])
        return carry

    lax.fori_loop(0, width, column, 0)


def joined(wp, parts, chunk, ct, k, tall, wide, occ, where, rows, into):
    width, _, v, _ = parts[0].shape
    depth, steps = wp.shape[2], rows.shape[0] // width
    where = jnp.concatenate([where, jnp.full((1,), chunk * width, I32)])
    block = (width, width, v, v)
    by_row = pl.BlockSpec(block, lambda n, rows, where: (rows[n * width] // width, chunk, 0, 0))
    return pl.pallas_call(
        functools.partial(joined_kernel, len(parts)),
        out_shape=jax.ShapeDtypeStruct(into.shape, into.dtype),
        grid_spec=pltpu.PrefetchScalarGridSpec(
            num_scalar_prefetch=2,
            grid=(steps,),
            in_specs=[pl.BlockSpec(memory_space=pltpu.SMEM), resident(tall.shape), resident(wide.shape)]
            + [pl.BlockSpec(memory_space=pl.ANY)]
            + [
                pl.BlockSpec((1, v, depth), lambda n, rows, where, q=q: (rows[n * width + q], 0, 0))
                for q in range(width)
            ]
            + [resident(p.shape) for p in parts]
            + [pl.BlockSpec(block, lambda n, rows, where: (n, 0, 0, 0)), by_row],
            out_specs=by_row,
        ),
        input_output_aliases={5: 0},
        compiler_params=params(),
        cost_estimate=cost(2 * steps * width**2 * v * v * depth, 2 * steps * width * v * (depth + 4 * width * v)),
        name="joined",
    )(rows, where, occ, tall, wide, into, *[wp] * width, *parts, ct, k)


class Links:
    def __init__(self, groups, jgroups):
        self.groups, self.jgroups, self.ratio = groups, jgroups, jgroups // groups

    def near(self, x, s):
        return lax.ppermute(x, "igrp", [(i, i ^ s) for i in range(self.groups)])

    def route(self, x, s):
        pairs = [
            (i * self.jgroups + z * self.ratio + y, z * self.jgroups + (i ^ s) * self.ratio + y)
            for i in range(self.groups)
            for z in range(self.groups)
            for y in range(self.ratio)
        ]
        return lax.ppermute(x, AXES, pairs)

    def swap(self, x, d):
        return lax.ppermute(x, "jgrp", [(j, j ^ d) for j in range(self.jgroups)])

    def spread(self, w, bit):
        held = [h for h in range(self.groups) if h % (2 * bit) == 0]
        pairs = [
            ((z ^ h) * self.jgroups + z * self.ratio + y, (z ^ h ^ bit) * self.jgroups + z * self.ratio + y)
            for h in held
            for z in range(self.groups)
            for y in range(self.ratio)
        ]
        return lax.ppermute(w, AXES, pairs)

    def bits(self):
        bit, found = self.groups // 2, []
        while bit:
            found.append(bit)
            bit //= 2
        return found


def exchange(links, mine, near, far, window, rider=None):
    groups, chunks = links.groups, range(len(near))
    sides = [list(range(p, groups, 2)) for p in range(2)]
    steps = [(h, side) for h in chunks for side in sides]
    plan = [[] for _ in range(len(steps) + 1)]
    for h in chunks:
        for s in range(1, groups):
            at = 2 * h + s % 2 if s > 1 else h * len(steps)
            plan[min(at, len(steps))].append((h, s))
    earlier, before = [], []
    for t in range(len(steps) + 1):
        slots = []
        if t < len(steps):
            h, side = steps[t]
            slots += [(mine[h], s) for s in side]
        if t > 0:
            back, back_side = steps[t - 1]
            slots += [(far[0][back], s) for s in back_side]
        for g, s in plan[t]:
            if not any(x is mine[g] and n == s for x, n in slots):
                slots.append((mine[g], s))
        arrays = [x[n] for x, n in slots]
        riding = rider is not None and t == len(steps)
        if riding:
            arrays.append(rider[0])
        if earlier:
            arrays = tie(arrays, earlier)
        for (x, n), array in zip(slots, arrays):
            x[n] = array
        earlier = []
        if t < len(steps):
            for s in side:
                far[0][h][s] = links.route(mine[h][s], s)
                earlier.append(far[0][h][s])
        if t > 0:
            for d in range(1, links.ratio):
                for s in back_side:
                    far[d][back][s] = links.swap(far[0][back][s], d)
                    earlier.append(far[d][back][s])
        for g, s in plan[t]:
            near[g][s] = links.near(mine[g][s], s)
            earlier.append(near[g][s])
        for g in chunks:
            near[g][0] = mine[g][0]
        earlier, before = earlier + window(t, before), earlier
        if riding:
            earlier.append(rider[1](arrays[-1]))
    return earlier


def body(t_start, integrals, weights, neighbours, eps_occ, eps_vir):
    row_count, cols, v, _ = t_start.shape
    groups, jgroups = lax.axis_size("igrp"), lax.axis_size("jgrp")
    links = Links(groups, jgroups)
    ratio = links.ratio
    my_i, my_j = lax.axis_index("igrp"), lax.axis_index("jgrp")
    my_z, my_half = my_j // ratio, my_j % ratio
    width = cols // 2
    chunks = range(2)
    sides = [list(range(p, groups, 2)) for p in range(2)]

    lists = listed_offsets(neighbours, groups, row_count)
    slots = relative_slots(neighbours, lists, groups, row_count)
    asked = lax.dynamic_slice_in_dim(lists, my_i, 1, 1)[:, 0]
    order = my_i ^ jnp.arange(groups, dtype=I32)
    rows = jnp.sum(
        asked[None] * (jnp.arange(groups, dtype=I32)[None, :, None] == order[:, None, None]).astype(I32), axis=1
    ).reshape(-1)
    every_row = jnp.arange(row_count, dtype=I32)
    where = jnp.stack([my_i * row_count, my_j * cols, my_half]).astype(I32)
    tall, wide = eps_vir.reshape(v, 1), eps_vir.reshape(1, v)

    def slots_of(first, count):
        return lax.dynamic_slice_in_dim(slots, first, count, 0)

    def empty():
        return [[None] * groups for _ in chunks], [[[None] * groups for _ in chunks] for _ in range(ratio)]

    made = {}

    def opening(t, earlier):
        if t == 0:
            made["wp"] = slotted([weights], jnp.zeros((), I32), slots_of(my_i * row_count, row_count), groups)
            return [made["wp"]]
        if t in (2, 4):
            made["c", t // 2 - 1] = direct(made["wp"], rows, near[t // 2 - 1])
            return [made["c", t // 2 - 1]]
        return []

    bits = links.bits()
    apart = my_i ^ my_z

    def fresh(bit):
        return apart % (2 * bit) == bit

    def deliver(h, w, came, bit, later):
        while later:
            w = jnp.where(fresh(bit), came, w)
            bit, later = later[0], later[1:]
            came = links.spread(w, bit)
        return slotted([w, came], fresh(bit), slots_of(my_j * cols + h * width, width), groups)

    own_w = [lax.dynamic_slice_in_dim(weights, my_half * cols + h * width, width, 0) for h in chunks]
    mine = [[*pick_rows(t_start, rows, groups, width, h)] for h in chunks]
    near, far = empty()
    last = exchange(links, mine, near, far, opening, (own_w[0], lambda w: links.spread(w, bits[0])))
    came, second = tie([last.pop(), own_w[1]], last)
    second_came = links.spread(second, bits[0])
    wpj = [deliver(0, own_w[0], came, bits[0], bits[1:]), None]

    def rows_of(h, halves):
        return jnp.concatenate(
            [(my_half ^ d) * cols + h * width + jnp.arange(width, dtype=I32) for d in halves]
        )

    chosen = ((rows // cols) ^ my_half) * len(chunks) + (rows % cols) // width
    in_order = jnp.arange(groups * CAP, dtype=I32)

    def listed_rows(h, c):
        return [
            *finish(
                wpj, [c], in_order, [h], integrals, tall, wide, eps_occ, where, rows, chosen,
                [piece for half in far_now for piece in half],
                [jax.ShapeDtypeStruct((width, CAP, v, v), BF16)] * groups,
            )
        ]

    for sweep in range(ITERS - 1):
        c = [made["c", h] if sweep == 0 else direct(made["wp"], rows, near[h]) for h in chunks]
        far_now = far
        mine = [listed_rows(0, c[0]), [None] * groups]
        near, far = empty()
        final = sweep == ITERS - 2
        state = {}
        every, first_half = range(ratio), jnp.zeros((width,), I32)

        def complete(over, h, halves):
            some_rows = rows_of(h, halves)
            use = jnp.repeat(jnp.arange(len(halves), dtype=I32), width)
            [state["out"]] = finish(
                wpj, [state["c", n] for n in over], some_rows, over, integrals, tall, wide, eps_occ, where, some_rows,
                use, [far[d][h] for d in halves], [jax.ShapeDtypeStruct((row_count, cols, v, v), F32)], state.get("out"),
            )
            return state["out"]

        def middle(t, earlier):
            if t == 1:
                if wpj[1] is None:
                    [arrived] = tie([second_came], earlier)
                    wpj[1] = deliver(1, second, arrived, bits[0], bits[1:])
                mine[1][:] = listed_rows(1, c[1])
                return mine[1]
            if t == 0 or not final:
                return []
            if t == 2:
                state["c", 0] = direct(made["wp"], every_row, near[0])
                return [state["c", 0]]
            if t == 3:
                some_rows = rows_of(0, every)
                use = jnp.repeat(jnp.arange(ratio, dtype=I32), width)
                [state["ct"]] = finish(
                    wpj, None, some_rows, [1], integrals, tall, wide, eps_occ, where, some_rows, use,
                    [far[d][0] for d in every],
                    [jax.ShapeDtypeStruct((ratio * width, width, v, v), BF16)],
                )
                return [state["ct"], complete([0], 0, every)]
            return []

        exchange(links, mine, near, far, middle)
    state["c", 1] = direct(made["wp"], rows_of(1, every), near[1], placed=True)
    complete([0, 1], 1, [0])
    state["out"] = joined(
        made["wp"], near[1], 1, state["ct"], integrals, tall, wide, eps_occ, where, rows_of(0, every), state["out"]
    )
    for d in every[1:]:
        complete([0, 1], 1, [d])
    return state["out"]


def solution(mesh):
    placed = (
        P("igrp", "jgrp", None, None),
        P("igrp", "jgrp", None, None),
        P("igrp", None, None, None),
        P(),
        P(),
        P(),
    )
    return jax.shard_map(
        body, mesh=mesh, in_specs=placed, out_specs=P("igrp", "jgrp", None, None), check_vma=False
    )
```

time: 878 us -> 625 us (0.71)
  waiting for transfers between devices: 469 us -> 251 us
  starting transfers between devices: 154 us -> 70.3 us
  Pallas kernels: 221 us -> 252 us
  local copies, waits for them, and re-layouts: 13.6 us -> 33.9 us
    ppermute x24 -> x48, waiting for transfers between devices: 469 us -> 251 us  [the longest x16 158 us: route(): return lax.ppermute(x, AXES, pairs)]
    ppermute x24 -> x48, starting transfers between devices: 154 us -> 70.3 us  [the longest x16 29.3 us: route(): return lax.ppermute(x, AXES, pairs)]
    pallas_call x1 -> x13, Pallas kernels: 7.59 us -> 28.1 us  [the longest x1 18.5 us: joined(): pl.pallas_call(functools.partial(joined_kernel, len(parts)), out_shape=ja...]
    unnamed x19 -> x90, local copies, waits for them, and re-layouts: 1.25 us -> 20.1 us
    pallas_call x6, Pallas kernels: 109 us -> 118 us  [finish(): pl.pallas_call(functools.partial(finish_kernel if into is None else kept_...]
    pallas_call x2 -> x3, Pallas kernels: 28.3 us -> 31.4 us  [slotted(): pl.pallas_call(slotted_kernel, out_shape=jax.ShapeDtypeStruct((rows, v, d...]
    pallas_call x2 -> x4, Pallas kernels: 75.9 us -> 73.9 us  [direct(): pl.pallas_call(functools.partial(direct_kernel, taken), out_shape=jax.Sha...]
  transfers between devices with their start and end apart: 24 -> 48, of which waited for: 11 -> 26; matrix products, arithmetic and copies ran while one was open for 2% -> 3% of each run, Pallas kernels for 20% -> 37%
where the time goes in v2:
time: 625 us; the launch traced here: 622 us
  Pallas kernels  252 us (40%)
  waiting for transfers between devices  251 us (40%)
  starting transfers between devices  70.3 us (11%)
  local copies, waits for them, and re-layouts  33.9 us (5%)
  other arithmetic  14.5 us (2%)
    ppermute x16, waiting for transfers between devices, route(): return lax.ppermute(x, AXES, pairs)  158 us
    pallas_call x6, Pallas kernels, finish(): pl.pallas_call(functools.partial(finish_kernel if into is None else kept_...  118 us
    pallas_call x4, Pallas kernels, direct(): pl.pallas_call(functools.partial(direct_kernel, taken), out_shape=jax.Sha...  73.9 us
    ppermute x16, waiting for transfers between devices, swap(): return lax.ppermute(x, 'jgrp', [(j, j ^ d) for j in range(self.jgroups)])  45.3 us
    ppermute x12, waiting for transfers between devices, near(): return lax.ppermute(x, 'igrp', [(i, i ^ s) for i in range(self.groups)])  44.5 us
    pallas_call x3, Pallas kernels, slotted(): pl.pallas_call(slotted_kernel, out_shape=jax.ShapeDtypeStruct((rows, v, d...  31.4 us
    ppermute x16, starting transfers between devices, route(): return lax.ppermute(x, AXES, pairs)  29.3 us
    ppermute x12, starting transfers between devices, near(): return lax.ppermute(x, 'igrp', [(i, i ^ s) for i in range(self.groups)])  22.4 us
  transfers between devices with their start and end apart: 48, of which 26 were waited for; matrix products, arithmetic and copies ran while one was open for 3% of the time, Pallas kernels for 37%

profile of v2, /device:TPU:21, one launch (start us, length us, event | category | flops | bytes accessed | tf_op | source)
XLA Modules:
  0.0 622.0 jit_solution(6588475998102382573)
XLA Ops:
  2.6 4.9 pick_rows.3
  7.5 3.1 collective-permute-start
  10.6 1.5 collective-permute-start.1
  12.1 2.2 collective-permute-start.3
  15.1 18.5 %slotted.3.refs_6_.refs_0_.refs_1_.refs_2_.refs_3_ = bf16[16,256,2048]{2,1,0:T(8,128)(2,1)} custom-call(s32[128]{0:T(128)} %reshape.498.slots_ref, s32[1]{0:T(128)} %constant.139.clone.1.pick_ref, bf16[16,8,256,256]{3,2,1,0:T(8,128)(2,1)} %refs_0_.5), custom_call_target="tpu_custom_call" | custom-call | bytes 33554432 | tf_op jit(solution)/shard_map/slotted/pallas_call | solution.py:114
  33.6 24.5 %collective-permute-done.refs_2_ = bf16[4,2,256,256]{3,2,1,0:T(8,128)(2,1)S(1)} collective-permute-done((bf16[4,2,256,256]{3,2,1,0:T(8,128)(2,1)}, bf16[4,2,256,256]{3,2,1,0:T(8,128)(2,1)S(1)}, u32[]{:S(2)}, u32[]{:S(2)}) %collective-permute-start) | collective-permute-done | bytes 1048608 | tf_op jit(solution)/shard_map/ppermute | solution.py:349
  60.3 2.2 collective-permute-start.4
  62.7 1.2 collective-permute-start.7
  63.9 2.7 collective-permute-start.8
  66.6 4.7 pick_rows.2
  71.3 36.9 %collective-permute-done.4.refs_2_ = bf16[4,2,256,256]{3,2,1,0:T(8,128)(2,1)S(1)} collective-permute-done((bf16[4,2,256,256]{3,2,1,0:T(8,128)(2,1)}, bf16[4,2,256,256]{3,2,1,0:T(8,128)(2,1)S(1)}, u32[]{:S(2)}, u32[]{:S(2)}) %collective-permute-start.4) | collective-permute-done | bytes 1048608 | tf_op jit(solution)/shard_map/ppermute | solution.py:349
  108.2 1.5 collective-permute-done.5.refs_3_
  112.0 4.5 collective-permute-start.9
  117.7 1.2 collective-permute-start.12
  119.0 15.8 %direct.4.refs_7_.refs_1_ = bf16[8,4,256,256]{3,2,1,0:T(8,128)(2,1)} custom-call(s32[8]{0:T(128)} %reshape.497.rows_ref, bf16[16,256,2048]{2,1,0:T(8,128)(2,1)} %slotted.3.refs_6_.refs_0_.refs_1_.refs_2_.refs_3_, bf16[16,256,2048]{2,1,0:T(8,128)(2,1)} %slotted.3.refs_6_.refs_0_.refs_1_.refs_2_.refs_3_, ...), custom_call_target="tpu_custom_call" | custom-call | flops 8589934592 | bytes 12582912 | tf_op jit(solution)/shard_map/direct/pallas_call | solution.py:152
  134.8 27.7 %collective-permute-done.9.refs_2_ = bf16[4,2,256,256]{3,2,1,0:T(8,128)(2,1)S(1)} collective-permute-done((bf16[4,2,256,256]{3,2,1,0:T(8,128)(2,1)}, bf16[4,2,256,256]{3,2,1,0:T(8,128)(2,1)S(1)}, u32[]{:S(2)}, u32[]{:S(2)}) %collective-permute-start.9) | collective-permute-done | bytes 1048608 | tf_op jit(solution)/shard_map/ppermute | solution.py:349
  165.6 3.4 collective-permute-start.14
  169.3 1.2 collective-permute-start.17
  171.6 6.3 %constant_dynamic-slice_fusion.1 = (bf16[4,8,256,256]{3,2,1,0:T(8,128)(2,1)}, bf16[4,8,256,256]{3,2,1,0:T(8,128)(2,1)S(1)}) fusion(bf16[16,8,256,256]{3,2,1,0:T(8,128)(2,1)} %refs_0_.5, s32[]{:T(128)S(6)} %select_n.217, s32[]{:T(128)S(6)} %select_n.216), kind=kLoop, calls=%fused_computation.44 | loop fusion | bytes 16777224 | tf_op jit(solution)/shard_map/dynamic_slice | solution.py:474
  177.9 2.0 copy.81.refs_3_
  179.9 1.3 copy-done
  181.2 31.7 %collective-permute-done.14.refs_0_ = bf16[4,2,256,256]{3,2,1,0:T(8,128)(2,1)S(1)} collective-permute-done((bf16[4,2,256,256]{3,2,1,0:T(8,128)(2,1)}, bf16[4,2,256,256]{3,2,1,0:T(8,128)(2,1)S(1)}, u32[]{:S(2)}, u32[]{:S(2)}) %collective-permute-start.14) | collective-permute-done | bytes 1048608 | tf_op jit(solution)/shard_map/ppermute | solution.py:349
  212.9 3.5 collective-permute-done.15.refs_1_
  217.7 2.7 collective-permute-start.19
  220.7 1.2 collective-permute-start.21
  221.9 1.4 collective-permute-done.22.refs_5_.refs_4_
  224.3 15.9 %direct.5.refs_5_.refs_1_ = bf16[8,4,256,256]{3,2,1,0:T(8,128)(2,1)} custom-call(s32[8]{0:T(128)} %reshape.497.rows_ref, bf16[16,256,2048]{2,1,0:T(8,128)(2,1)} %slotted.3.refs_6_.refs_0_.refs_1_.refs_2_.refs_3_, bf16[16,256,2048]{2,1,0:T(8,128)(2,1)} %slotted.3.refs_6_.refs_0_.refs_1_.refs_2_.refs_3_, ...), custom_call_target="tpu_custom_call" | custom-call | flops 8589934592 | bytes 12582912 | tf_op jit(solution)/shard_map/direct/pallas_call | solution.py:152
  240.2 4.8 collective-permute-done.20.refs_2_.refs_16_
  245.0 22.5 %collective-permute-done.21.refs_3_.refs_18_ = bf16[4,2,256,256]{3,2,1,0:T(8,128)(2,1)S(1)} collective-permute-done((bf16[4,2,256,256]{3,2,1,0:T(8,128)(2,1)}, bf16[4,2,256,256]{3,2,1,0:T(8,128)(2,1)S(1)}, u32[]{:S(2)}, u32[]{:S(2)}) %collective-permute-start.21) | collective-permute-done | bytes 1048608 | tf_op jit(solution)/shard_map/ppermute | solution.py:352
  268.5 4.6 broadcast_select_fusion.1.refs_0_
  273.0 1.3 collective-permute-start.23
  274.3 2.7 collective-permute-start.29
  281.0 1.6 collective-permute-done.23.refs_1_
  282.6 6.5 %slotted.4.refs_0_.refs_9_ = bf16[4,256,2048]{2,1,0:T(8,128)(2,1)} custom-call(s32[32]{0:T(128)} %reshape.496.slots_ref, s32[1]{0:T(128)} %bitcast.5.pick_ref, bf16[4,8,256,256]{3,2,1,0:T(8,128)(2,1)} %broadcast_select_fusion.1.refs_0_, bf16[4,8,256,256]{3,2,1,0:T(8,128)(2,1)} %collective-permute-done.23.refs_1_), custom_call_target="tpu_custom_call" | custom-call | bytes 8388608 | tf_op jit(solution)/shard_map/slotted/pallas_call | solution.py:114
  289.6 22.9 %finish.6 = (bf16[4,2,256,256]{3,2,1,0:T(8,128)(2,1)}, bf16[4,2,256,256]{3,2,1,0:T(8,128)(2,1)}, bf16[4,2,256,256]{3,2,1,0:T(8,128)(2,1)}, bf16[4,2,256,256]{3,2,1,0:T(8,128)(2,1)}) custom-call(s32[8]{0:T(128)} %reshape.497.rows_ref, s32[8]{0:T(128)} %iota.159.crows_ref, s32[4]{0:T(128)} %pad_add_fusion.where_ref.refs_2_, s32[32]{0:T(128)} %select_n.225.held_ref, ...), custom_call_target="tpu_custom_call" | custom-call | flops 8589934592 | bytes 25165824 | tf_op jit(solution)/shard_map/finish/pallas_call | solution.py:261
  312.8 5.7 collective-permute-start.25
  318.5 2.7 collective-permute-start.26
  322.0 38.2 %collective-permute-done.25.refs_5_.refs_6_.refs_4_ = bf16[4,2,256,256]{3,2,1,0:T(8,128)(2,1)S(1)} collective-permute-done((bf16[4,2,256,256]{3,2,1,0:T(8,128)(2,1)}, bf16[4,2,256,256]{3,2,1,0:T(8,128)(2,1)S(1)}, u32[]{:S(2)}, u32[]{:S(2)}) %collective-permute-start.25) | collective-permute-done | bytes 1048608 | tf_op jit(solution)/shard_map/ppermute | solution.py:340
  360.2 9.1 %collective-permute-done.26.refs_2_.refs_1_ = bf16[4,2,256,256]{3,2,1,0:T(8,128)(2,1)S(1)} collective-permute-done((bf16[4,2,256,256]{3,2,1,0:T(8,128)(2,1)}, bf16[4,2,256,256]{3,2,1,0:T(8,128)(2,1)S(1)}, u32[]{:S(2)}, u32[]{:S(2)}) %collective-permute-start.26) | collective-permute-done | bytes 1048608 | tf_op jit(solution)/shard_map/ppermute | solution.py:349
  370.3 4.6 broadcast_select_fusion.refs_0_
  375.0 1.3 collective-permute-start.30
  377.2 6.8 %collective-permute-start.28 = (bf16[4,2,256,256]{3,2,1,0:T(8,128)(2,1)}, bf16[4,2,256,256]{3,2,1,0:T(8,128)(2,1)S(1)}, u32[]{:S(2)}, u32[]{:S(2)}) collective-permute-start(bf16[4,2,256,256]{3,2,1,0:T(8,128)(2,1)} %get-tuple-element.83), channel_id=1, source_target_pairs={{0,24},{8,16},{16,8},{24,0},{1,25},{9,17},{17,9},{25,1},{2,26},{10... | collective-permute-start | bytes 3145736 | tf_op jit(solution)/shard_map/ppermute | solution.py:340
  384.0 2.9 collective-permute-start.31
  387.2 1.5 collective-permute-done.30.refs_1_
  390.4 6.5 %slotted.5.refs_0_.refs_10_ = bf16[4,256,2048]{2,1,0:T(8,128)(2,1)} custom-call(s32[32]{0:T(128)} %reshape.499.slots_ref, s32[1]{0:T(128)} %bitcast.5.pick_ref, bf16[4,8,256,256]{3,2,1,0:T(8,128)(2,1)} %broadcast_select_fusion.refs_0_, bf16[4,8,256,256]{3,2,1,0:T(8,128)(2,1)} %collective-permute-done.30.refs_1_), custom_call_target="tpu_custom_call" | custom-call | bytes 8388608 | tf_op jit(solution)/shard_map/slotted/pallas_call | solution.py:114
  397.3 22.8 %finish.7 = (bf16[4,2,256,256]{3,2,1,0:T(8,128)(2,1)}, bf16[4,2,256,256]{3,2,1,0:T(8,128)(2,1)}, bf16[4,2,256,256]{3,2,1,0:T(8,128)(2,1)}, bf16[4,2,256,256]{3,2,1,0:T(8,128)(2,1)}) custom-call(s32[8]{0:T(128)} %reshape.497.rows_ref, s32[8]{0:T(128)} %iota.160.crows_ref, s32[4]{0:T(128)} %get-tuple-element.107.where_ref, s32[32]{0:T(128)} %select_n.225.held_ref, ...), custom_call_target="tpu_custom_call" | custom-call | flops 8589934592 | bytes 25165824 | tf_op jit(solution)/shard_map/finish/pallas_call | solution.py:261
  420.2 4.5 collective-permute-done.28.refs_7_.refs_6_
  424.7 8.0 %collective-permute-done.31.refs_2_ = bf16[4,2,256,256]{3,2,1,0:T(8,128)(2,1)} collective-permute-done((bf16[4,2,256,256]{3,2,1,0:T(8,128)(2,1)}, bf16[4,2,256,256]{3,2,1,0:T(8,128)(2,1)}, u32[]{:S(2)}, u32[]{:S(2)}) %collective-permute-start.31) | collective-permute-done | bytes 1048608 | tf_op jit(solution)/shard_map/ppermute | solution.py:349
  432.7 1.8 collective-permute-done.34.refs_5_.refs_9_.refs_7_
  435.5 1.8 collective-permute-start.38
  439.0 3.6 collective-permute-start.37
  443.2 26.2 %direct.6.refs_1_.refs_7_.refs_11_ = bf16[16,4,256,256]{3,2,1,0:T(8,128)(2,1)} custom-call(s32[16]{0:T(128)} %iota.158.rows_ref, bf16[16,256,2048]{2,1,0:T(8,128)(2,1)} %slotted.3.refs_6_.refs_0_.refs_1_.refs_2_.refs_3_, bf16[16,256,2048]{2,1,0:T(8,128)(2,1)} %slotted.3.refs_6_.refs_0_.refs_1_.refs_2_.refs_3_, ...), custom_call_target="tpu_custom_call" | custom-call | flops 17179869184 | bytes 25165824 | tf_op jit(solution)/shard_map/direct/pallas_call | solution.py:152
  469.5 14.0 %collective-permute-done.36.refs_10_.refs_5_.refs_8_ = bf16[4,2,256,256]{3,2,1,0:T(8,128)(2,1)S(1)} collective-permute-done((bf16[4,2,256,256]{3,2,1,0:T(8,128)(2,1)}, bf16[4,2,256,256]{3,2,1,0:T(8,128)(2,1)S(1)}, u32[]{:S(2)}, u32[]{:S(2)}) %collective-permute-start.36) | collective-permute-done | bytes 1048608 | tf_op jit(solution)/shard_map/ppermute | solution.py:352
  483.5 5.3 collective-permute-done.37.refs_2_
  490.9 2.0 collective-permute-start.44
  492.9 1.7 collective-permute-start.40
  496.1 19.1 %finish.8.refs_7_.refs_8_ = f32[16,8,256,256]{3,2,1,0:T(8,128)} custom-call(s32[8]{0:T(128)} %get-tuple-element.106.rows_ref.crows_ref, s32[8]{0:T(128)} %get-tuple-element.106.rows_ref.crows_ref, s32[4]{0:T(128)} %pad_add_fusion.where_ref.refs_2_, s32[16]{0:T(128)} %select_n.208.held_ref, s32[8]{0:T(128)} %copy-done.43, f32[64]{0:T(128)} %refs_5_.3, ...), custom_call_target="tpu_custom_call" | custom-call | flops 8589934592 | bytes 25165824 | tf_op jit(solution)/shard_map/finish/pallas_call | solution.py:261
  515.2 17.0 %finish.9.refs_6_.refs_8_ = bf16[8,4,256,256]{3,2,1,0:T(8,128)(2,1)} custom-call(s32[8]{0:T(128)} %get-tuple-element.106.rows_ref.crows_ref, s32[8]{0:T(128)} %get-tuple-element.106.rows_ref.crows_ref, s32[4]{0:T(128)} %get-tuple-element.107.where_ref, s32[16]{0:T(128)} %select_n.208.held_ref, s32[8]{0:T(128)} %copy-done.43, f32[64]{0:T(128)} %refs_5_.3, ...), custom_call_target="tpu_custom_call" | custom-call | flops 8589934592 | bytes 25165824 | tf_op jit(solution)/shard_map/finish/pallas_call | solution.py:261
  532.1 8.1 %collective-permute-done.40.refs_0_ = bf16[4,2,256,256]{3,2,1,0:T(8,128)(2,1)S(1)} collective-permute-done((bf16[4,2,256,256]{3,2,1,0:T(8,128)(2,1)}, bf16[4,2,256,256]{3,2,1,0:T(8,128)(2,1)S(1)}, u32[]{:S(2)}, u32[]{:S(2)}) %collective-permute-start.40) | collective-permute-done | bytes 1048608 | tf_op jit(solution)/shard_map/ppermute | solution.py:349
  543.5 1.3 collective-permute-start.45
  548.9 16.0 %direct.7.refs_12_ = bf16[16,4,256,256]{3,2,1,0:T(8,128)(2,1)} custom-call(s32[8]{0:T(128)} %pad_add_fusion.4.rows_ref, bf16[16,256,2048]{2,1,0:T(8,128)(2,1)} %slotted.3.refs_6_.refs_0_.refs_1_.refs_2_.refs_3_, bf16[16,256,2048]{2,1,0:T(8,128)(2,1)} %slotted.3.refs_6_.refs_0_.refs_1_.refs_2_.refs_3_, ...), custom_call_target="tpu_custom_call" | custom-call | flops 8589934592 | bytes 12582912 | tf_op jit(solution)/shard_map/direct/pallas_call | solution.py:152
  565.5 18.3 %finish.10.into_ref = f32[16,8,256,256]{3,2,1,0:T(8,128)} custom-call(s32[4]{0:T(128)} %copy-done.42, s32[4]{0:T(128)} %copy-done.42, s32[4]{0:T(128)} %pad_add_fusion.where_ref.refs_2_, s32[4]{0:T(128)} %get-tuple-element.103.refs_3_, s32[4]{0:T(128)} %broadcast.535.refs_4_, f32[64]{0:T(128)} %refs_5_.3, ...), custom_call_target="tpu_custom_call", output_to_operand_aliasing={{}: (8, {})} | custom-call | flops 8589934592 | bytes 29360128 | tf_op jit(solution)/shard_map/finish/pallas_call | solution.py:261
  583.8 18.5 %joined.1.refs_8_ = f32[16,8,256,256]{3,2,1,0:T(8,128)} custom-call(s32[8]{0:T(128)} %get-tuple-element.106.rows_ref.crows_ref, s32[4]{0:T(128)} %get-tuple-element.107.where_ref, f32[64]{0:T(128)} %refs_5_.3, f32[256,1]{1,0:T(8,128)} %copy.65.tall_ref.refs_6_, f32[1,256]{1,0:T(1,128)} %bitcast.12, ...), custom_call_target="tpu_custom_call", output_to_operand_aliasing={{}: (5, {})} | custom-call | flops 8589934592 | bytes 25165824 | tf_op jit(solution)/shard_map/joined/pallas_call | solution.py:312
  603.6 18.3 %finish.11 = f32[16,8,256,256]{3,2,1,0:T(8,128)} custom-call(s32[4]{0:T(128)} %copy-done.41, s32[4]{0:T(128)} %copy-done.41, s32[4]{0:T(128)} %pad_add_fusion.where_ref.refs_2_, s32[4]{0:T(128)} %get-tuple-element.104.refs_3_, s32[4]{0:T(128)} %broadcast.535.refs_4_, f32[64]{0:T(128)} %refs_5_.3, ...), custom_call_target="tpu_custom_call", output_to_operand_aliasing={{}: (8, {})} | custom-call | flops 8589934592 | bytes 29360128 | tf_op jit(solution)/shard_map/finish/pallas_call | solution.py:261
  (204 shorter events, 43.3 us)
Async XLA Ops:
  7.5 50.6 %collective-permute-start = (bf16[4,2,256,256]{3,2,1,0:T(8,128)(2,1)}, bf16[4,2,256,256]{3,2,1,0:T(8,128)(2,1)S(1)}, u32[]{:S(2)}, u32[]{:S(2)}) collective-permute-start(bf16[4,2,256,256]{3,2,1,0:T(8,128)(2,1)} %get-tuple-element.60.refs_4_), channel_id=1, source_target_pairs={{0,0},{1,1},{2,8},{3,9},{4,16},{5,17},{6,24},{7,25},{8,2},{9,3},{1... | collective-permute-start | bytes 3145736 | tf_op jit(solution)/shard_map/ppermute | solution.py:349
  10.6 48.4 %collective-permute-start.1 = (bf16[4,2,256,256]{3,2,1,0:T(8,128)(2,1)}, bf16[4,2,256,256]{3,2,1,0:T(8,128)(2,1)S(1)}, u32[]{:S(2)}, u32[]{:S(2)}) collective-permute-start(bf16[4,2,256,256]{3,2,1,0:T(8,128)(2,1)} %get-tuple-element.61), channel_id=1, source_target_pairs={{0,4},{1,5},{2,12},{3,13},{4,20},{5,21},{6,28},{7,29},{8,6},{9,7},... | collective-permute-start | bytes 3145736 | tf_op jit(solution)/shard_map/ppermute | solution.py:349
  12.1 46.9 %collective-permute-start.2 = (bf16[4,2,256,256]{3,2,1,0:T(8,128)(2,1)}, bf16[4,2,256,256]{3,2,1,0:T(8,128)(2,1)S(1)}, u32[]{:S(2)}, u32[]{:S(2)}) collective-permute-start(bf16[4,2,256,256]{3,2,1,0:T(8,128)(2,1)} %get-tuple-element.58.refs_0_), channel_id=1, source_target_pairs={{0,8},{8,0},{16,24},{24,16},{1,9},{9,1},{17,25},{25,17},{2,10},{10... | collective-permute-start | bytes 3145736 | tf_op jit(solution)/shard_map/ppermute | solution.py:340
  12.1 47.2 %collective-permute-start.3 = (bf16[4,2,256,256]{3,2,1,0:T(8,128)(2,1)}, bf16[4,2,256,256]{3,2,1,0:T(8,128)(2,1)}, u32[]{:S(2)}, u32[]{:S(2)}) collective-permute-start(bf16[4,2,256,256]{3,2,1,0:T(8,128)(2,1)} %get-tuple-element.61), channel_id=1, source_target_pairs={{0,16},{8,24},{16,0},{24,8},{1,17},{9,25},{17,1},{25,9},{2,18},{10... | collective-permute-start | bytes 3145736 | tf_op jit(solution)/shard_map/ppermute | solution.py:340
  60.3 47.9 %collective-permute-start.4 = (bf16[4,2,256,256]{3,2,1,0:T(8,128)(2,1)}, bf16[4,2,256,256]{3,2,1,0:T(8,128)(2,1)S(1)}, u32[]{:S(2)}, u32[]{:S(2)}) collective-permute-start(bf16[4,2,256,256]{3,2,1,0:T(8,128)(2,1)} %get-tuple-element.62), channel_id=1, source_target_pairs={{0,2},{1,3},{2,10},{3,11},{4,18},{5,19},{6,26},{7,27},{8,0},{9,1},... | collective-permute-start | bytes 3145736 | tf_op jit(solution)/shard_map/ppermute | solution.py:349
  62.5 47.2 %collective-permute-start.5 = (bf16[4,2,256,256]{3,2,1,0:T(8,128)(2,1)}, bf16[4,2,256,256]{3,2,1,0:T(8,128)(2,1)S(1)}, u32[]{:S(2)}, u32[]{:S(2)}) collective-permute-start(bf16[4,2,256,256]{3,2,1,0:T(8,128)(2,1)} %get-tuple-element.63), channel_id=1, source_target_pairs={{0,6},{1,7},{2,14},{3,15},{4,22},{5,23},{6,30},{7,31},{8,4},{9,5},... | collective-permute-start | bytes 3145736 | tf_op jit(solution)/shard_map/ppermute | solution.py:349
  62.5 47.2 %collective-permute-start.6 = (bf16[4,2,256,256]{3,2,1,0:T(8,128)(2,1)}, bf16[4,2,256,256]{3,2,1,0:T(8,128)(2,1)S(1)}, u32[]{:S(2)}, u32[]{:S(2)}) collective-permute-start(bf16[4,2,256,256]{3,2,1,0:T(8,128)(2,1)} %get-tuple-element.64.refs_3_), channel_id=1, source_target_pairs={{0,1},{1,0},{2,3},{3,2},{4,5},{5,4},{6,7},{7,6},{8,9},{9,8},{10,11... | collective-permute-start | bytes 3145736 | tf_op jit(solution)/shard_map/ppermute | solution.py:352
  62.7 47.0 %collective-permute-start.7 = (bf16[4,2,256,256]{3,2,1,0:T(8,128)(2,1)}, bf16[4,2,256,256]{3,2,1,0:T(8,128)(2,1)S(1)}, u32[]{:S(2)}, u32[]{:S(2)}) collective-permute-start(bf16[4,2,256,256]{3,2,1,0:T(8,128)(2,1)} %get-tuple-element.65.refs_5_), channel_id=1, source_target_pairs={{0,1},{1,0},{2,3},{3,2},{4,5},{5,4},{6,7},{7,6},{8,9},{9,8},{10,11... | collective-permute-start | bytes 3145736 | tf_op jit(solution)/shard_map/ppermute | solution.py:352
  63.9 46.7 %collective-permute-start.8 = (bf16[4,2,256,256]{3,2,1,0:T(8,128)(2,1)}, bf16[4,2,256,256]{3,2,1,0:T(8,128)(2,1)S(1)}, u32[]{:S(2)}, u32[]{:S(2)}) collective-permute-start(bf16[4,2,256,256]{3,2,1,0:T(8,128)(2,1)} %get-tuple-element.63), channel_id=1, source_target_pairs={{0,24},{8,16},{16,8},{24,0},{1,25},{9,17},{17,9},{25,1},{2,26},{10... | collective-permute-start | bytes 3145736 | tf_op jit(solution)/shard_map/ppermute | solution.py:340
  108.2 3.5 copy-start.13
  112.0 50.5 %collective-permute-start.9 = (bf16[4,2,256,256]{3,2,1,0:T(8,128)(2,1)}, bf16[4,2,256,256]{3,2,1,0:T(8,128)(2,1)S(1)}, u32[]{:S(2)}, u32[]{:S(2)}) collective-permute-start(bf16[4,2,256,256]{3,2,1,0:T(8,128)(2,1)} %get-tuple-element.66.refs_4_), channel_id=1, source_target_pairs={{0,0},{1,1},{2,8},{3,9},{4,16},{5,17},{6,24},{7,25},{8,2},{9,3},{1... | collective-permute-start | bytes 3145736 | tf_op jit(solution)/shard_map/ppermute | solution.py:349
  116.5 46.8 %collective-permute-start.10 = (bf16[4,2,256,256]{3,2,1,0:T(8,128)(2,1)}, bf16[4,2,256,256]{3,2,1,0:T(8,128)(2,1)S(1)}, u32[]{:S(2)}, u32[]{:S(2)}) collective-permute-start(bf16[4,2,256,256]{3,2,1,0:T(8,128)(2,1)} %get-tuple-element.67), channel_id=1, source_target_pairs={{0,4},{1,5},{2,12},{3,13},{4,20},{5,21},{6,28},{7,29},{8,6},{9,7},... | collective-permute-start | bytes 3145736 | tf_op jit(solution)/shard_map/ppermute | solution.py:349
  117.5 45.8 %collective-permute-start.11 = (bf16[4,2,256,256]{3,2,1,0:T(8,128)(2,1)}, bf16[4,2,256,256]{3,2,1,0:T(8,128)(2,1)S(1)}, u32[]{:S(2)}, u32[]{:S(2)}) collective-permute-start(bf16[4,2,256,256]{3,2,1,0:T(8,128)(2,1)} %get-tuple-element.68.refs_4_), channel_id=1, source_target_pairs={{0,1},{1,0},{2,3},{3,2},{4,5},{5,4},{6,7},{7,6},{8,9},{9,8},{10,11... | collective-permute-start | bytes 3145736 | tf_op jit(solution)/shard_map/ppermute | solution.py:352
  117.7 46.4 %collective-permute-start.12 = (bf16[4,2,256,256]{3,2,1,0:T(8,128)(2,1)}, bf16[4,2,256,256]{3,2,1,0:T(8,128)(2,1)S(1)}, u32[]{:S(2)}, u32[]{:S(2)}) collective-permute-start(bf16[4,2,256,256]{3,2,1,0:T(8,128)(2,1)} %get-tuple-element.69.refs_6_), channel_id=1, source_target_pairs={{0,1},{1,0},{2,3},{3,2},{4,5},{5,4},{6,7},{7,6},{8,9},{9,8},{10,11... | collective-permute-start | bytes 3145736 | tf_op jit(solution)/shard_map/ppermute | solution.py:352
  119.0 45.3 %collective-permute-start.13 = (bf16[4,2,256,256]{3,2,1,0:T(8,128)(2,1)}, bf16[4,2,256,256]{3,2,1,0:T(8,128)(2,1)S(1)}, u32[]{:S(2)}, u32[]{:S(2)}) collective-permute-start(bf16[4,2,256,256]{3,2,1,0:T(8,128)(2,1)} %get-tuple-element.67), channel_id=1, source_target_pairs={{0,16},{8,24},{16,0},{24,8},{1,17},{9,25},{17,1},{25,9},{2,18},{10... | collective-permute-start | bytes 3145736 | tf_op jit(solution)/shard_map/ppermute | solution.py:340
  162.5 2.8 copy-start.17
  165.6 47.3 %collective-permute-start.14 = (bf16[4,2,256,256]{3,2,1,0:T(8,128)(2,1)}, bf16[4,2,256,256]{3,2,1,0:T(8,128)(2,1)S(1)}, u32[]{:S(2)}, u32[]{:S(2)}) collective-permute-start(bf16[4,2,256,256]{3,2,1,0:T(8,128)(2,1)} %get-tuple-element.70.refs_2_), channel_id=1, source_target_pairs={{0,2},{1,3},{2,10},{3,11},{4,18},{5,19},{6,26},{7,27},{8,0},{9,1},... | collective-permute-start | bytes 3145736 | tf_op jit(solution)/shard_map/ppermute | solution.py:349
  169.0 47.4 %collective-permute-start.15 = (bf16[4,2,256,256]{3,2,1,0:T(8,128)(2,1)}, bf16[4,2,256,256]{3,2,1,0:T(8,128)(2,1)}, u32[]{:S(2)}, u32[]{:S(2)}) collective-permute-start(bf16[4,2,256,256]{3,2,1,0:T(8,128)(2,1)} %get-tuple-element.71), channel_id=1, source_target_pairs={{0,6},{1,7},{2,14},{3,15},{4,22},{5,23},{6,30},{7,31},{8,4},{9,5},... | collective-permute-start | bytes 3145736 | tf_op jit(solution)/shard_map/ppermute | solution.py:349
  169.1 47.4 %collective-permute-start.16 = (bf16[4,2,256,256]{3,2,1,0:T(8,128)(2,1)}, bf16[4,2,256,256]{3,2,1,0:T(8,128)(2,1)S(1)}, u32[]{:S(2)}, u32[]{:S(2)}) collective-permute-start(bf16[4,2,256,256]{3,2,1,0:T(8,128)(2,1)} %get-tuple-element.72.refs_7_), channel_id=1, source_target_pairs={{0,1},{1,0},{2,3},{3,2},{4,5},{5,4},{6,7},{7,6},{8,9},{9,8},{10,11... | collective-permute-start | bytes 3145736 | tf_op jit(solution)/shard_map/ppermute | solution.py:352
  169.3 47.4 %collective-permute-start.17 = (bf16[4,2,256,256]{3,2,1,0:T(8,128)(2,1)}, bf16[4,2,256,256]{3,2,1,0:T(8,128)(2,1)S(1)}, u32[]{:S(2)}, u32[]{:S(2)}) collective-permute-start(bf16[4,2,256,256]{3,2,1,0:T(8,128)(2,1)} %get-tuple-element.73.refs_9_), channel_id=1, source_target_pairs={{0,1},{1,0},{2,3},{3,2},{4,5},{5,4},{6,7},{7,6},{8,9},{9,8},{10,11... | collective-permute-start | bytes 3145736 | tf_op jit(solution)/shard_map/ppermute | solution.py:352
  170.5 46.2 %collective-permute-start.18 = (bf16[4,2,256,256]{3,2,1,0:T(8,128)(2,1)}, bf16[4,2,256,256]{3,2,1,0:T(8,128)(2,1)}, u32[]{:S(2)}, u32[]{:S(2)}) collective-permute-start(bf16[4,2,256,256]{3,2,1,0:T(8,128)(2,1)} %get-tuple-element.71), channel_id=1, source_target_pairs={{0,24},{8,16},{16,8},{24,0},{1,25},{9,17},{17,9},{25,1},{2,26},{10... | collective-permute-start | bytes 3145736 | tf_op jit(solution)/shard_map/ppermute | solution.py:340
  177.9 3.3 copy-start
  212.9 3.8 copy-start.10
  217.7 49.7 %collective-permute-start.19 = (bf16[4,8,256,256]{3,2,1,0:T(8,128)(2,1)}, bf16[4,8,256,256]{3,2,1,0:T(8,128)(2,1)}, u32[]{:S(2)}, u32[]{:S(2)}) collective-permute-start(bf16[4,8,256,256]{3,2,1,0:T(8,128)(2,1)} %get-tuple-element.74), channel_id=1, source_target_pairs={{0,16},{1,17},{10,26},{11,27},{20,4},{21,5},{30,14},{31,15}} | collective-permute-start | bytes 12582920 | tf_op jit(solution)/shard_map/ppermute | solution.py:362
  220.5 2.9 collective-permute-start.22
  220.5 24.5 %collective-permute-start.20 = (bf16[4,2,256,256]{3,2,1,0:T(8,128)(2,1)}, bf16[4,2,256,256]{3,2,1,0:T(8,128)(2,1)S(1)}, u32[]{:S(2)}, u32[]{:S(2)}) collective-permute-start(bf16[4,2,256,256]{3,2,1,0:T(8,128)(2,1)} %get-tuple-element.75.refs_8_), channel_id=1, source_target_pairs={{0,1},{1,0},{2,3},{3,2},{4,5},{5,4},{6,7},{7,6},{8,9},{9,8},{10,11... | collective-permute-start | bytes 3145736 | tf_op jit(solution)/shard_map/ppermute | solution.py:352
  220.7 46.8 %collective-permute-start.21 = (bf16[4,2,256,256]{3,2,1,0:T(8,128)(2,1)}, bf16[4,2,256,256]{3,2,1,0:T(8,128)(2,1)S(1)}, u32[]{:S(2)}, u32[]{:S(2)}) collective-permute-start(bf16[4,2,256,256]{3,2,1,0:T(8,128)(2,1)} %get-tuple-element.76.refs_10_), channel_id=1, source_target_pairs={{0,1},{1,0},{2,3},{3,2},{4,5},{5,4},{6,7},{7,6},{8,9},{9,8},{10,11... | collective-permute-start | bytes 3145736 | tf_op jit(solution)/shard_map/ppermute | solution.py:352
  245.0 22.5 %copy-start.19 = (bf16[4,2,256,256]{3,2,1,0:T(8,128)(2,1)}, bf16[4,2,256,256]{3,2,1,0:T(8,128)(2,1)S(1)}, u32[]{:S(2)}) copy-start(bf16[4,2,256,256]{3,2,1,0:T(8,128)(2,1)S(1)} %collective-permute-done.20.refs_2_.refs_16_) | copy-start | bytes 3145732
  268.5 8.6 %copy-start.38 = (f32[256]{0:T(256)S(1)}, f32[256]{0:T(256)}, u32[]{:S(2)}) copy-start(f32[256]{0:T(256)} %param.11) | copy-start | bytes 3076
  268.5 10.1 %copy-start.39 = (s32[8]{0:T(128)S(1)}, s32[8]{0:T(128)}, u32[]{:S(2)}) copy-start(s32[8]{0:T(128)} %reshape.497.rows_ref) | copy-start | bytes 100
  273.0 9.5 %collective-permute-start.23 = (bf16[4,8,256,256]{3,2,1,0:T(8,128)(2,1)}, bf16[4,8,256,256]{3,2,1,0:T(8,128)(2,1)}, u32[]{:S(2)}, u32[]{:S(2)}) collective-permute-start(bf16[4,8,256,256]{3,2,1,0:T(8,128)(2,1)} %broadcast_select_fusion.1.refs_0_), channel_id=1, source_target_pairs={{0,8},{1,9},{10,2},{11,3},{20,28},{21,29},{30,22},{31,23},{16,24},... | collective-permute-start | bytes 12582920 | tf_op jit(solution)/shard_map/ppermute | solution.py:362
  274.3 47.6 %collective-permute-start.29 = (bf16[4,8,256,256]{3,2,1,0:T(8,128)(2,1)}, bf16[4,8,256,256]{3,2,1,0:T(8,128)(2,1)}, u32[]{:S(2)}, u32[]{:S(2)}) collective-permute-start(bf16[4,8,256,256]{3,2,1,0:T(8,128)(2,1)} %get-tuple-element.85), channel_id=1, source_target_pairs={{0,16},{1,17},{10,26},{11,27},{20,4},{21,5},{30,14},{31,15}} | collective-permute-start | bytes 12582920 | tf_op jit(solution)/shard_map/ppermute | solution.py:362
  278.5 10.5 %copy-start.40 = (s32[8]{0:T(128)}, s32[8]{0:T(128)S(1)}, u32[]{:S(2)}) copy-start(s32[8]{0:T(128)S(1)} %get-tuple-element.115.use_ref) | copy-start | bytes 100
  312.5 9.5 %collective-permute-start.24 = (bf16[4,2,256,256]{3,2,1,0:T(8,128)(2,1)}, bf16[4,2,256,256]{3,2,1,0:T(8,128)(2,1)S(1)}, u32[]{:S(2)}, u32[]{:S(2)}) collective-permute-start(bf16[4,2,256,256]{3,2,1,0:T(8,128)(2,1)} %get-tuple-element.80.refs_0_), channel_id=1, source_target_pairs={{0,8},{8,0},{16,24},{24,16},{1,9},{9,1},{17,25},{25,17},{2,10},{10... | collective-permute-start | bytes 3145736 | tf_op jit(solution)/shard_map/ppermute | solution.py:340
  312.8 47.4 %collective-permute-start.25 = (bf16[4,2,256,256]{3,2,1,0:T(8,128)(2,1)}, bf16[4,2,256,256]{3,2,1,0:T(8,128)(2,1)S(1)}, u32[]{:S(2)}, u32[]{:S(2)}) collective-permute-start(bf16[4,2,256,256]{3,2,1,0:T(8,128)(2,1)} %get-tuple-element.81), channel_id=1, source_target_pairs={{0,16},{8,24},{16,0},{24,8},{1,17},{9,25},{17,1},{25,9},{2,18},{10... | collective-permute-start | bytes 3145736 | tf_op jit(solution)/shard_map/ppermute | solution.py:340
  318.5 50.8 %collective-permute-start.26 = (bf16[4,2,256,256]{3,2,1,0:T(8,128)(2,1)}, bf16[4,2,256,256]{3,2,1,0:T(8,128)(2,1)S(1)}, u32[]{:S(2)}, u32[]{:S(2)}) collective-permute-start(bf16[4,2,256,256]{3,2,1,0:T(8,128)(2,1)} %get-tuple-element.79.refs_4_), channel_id=1, source_target_pairs={{0,0},{1,1},{2,8},{3,9},{4,16},{5,17},{6,24},{7,25},{8,2},{9,3},{1... | collective-permute-start | bytes 3145736 | tf_op jit(solution)/shard_map/ppermute | solution.py:349
  321.3 48.2 %collective-permute-start.27 = (bf16[4,2,256,256]{3,2,1,0:T(8,128)(2,1)}, bf16[4,2,256,256]{3,2,1,0:T(8,128)(2,1)}, u32[]{:S(2)}, u32[]{:S(2)}) collective-permute-start(bf16[4,2,256,256]{3,2,1,0:T(8,128)(2,1)} %get-tuple-element.81), channel_id=1, source_target_pairs={{0,4},{1,5},{2,12},{3,13},{4,20},{5,21},{6,28},{7,29},{8,6},{9,7},... | collective-permute-start | bytes 3145736 | tf_op jit(solution)/shard_map/ppermute | solution.py:349
  322.0 47.5 %copy-start.3 = (bf16[4,2,256,256]{3,2,1,0:T(8,128)(2,1)}, bf16[4,2,256,256]{3,2,1,0:T(8,128)(2,1)S(1)}, u32[]{:S(2)}) copy-start(bf16[4,2,256,256]{3,2,1,0:T(8,128)(2,1)S(1)} %collective-permute-done.24.refs_4_.refs_5_.refs_3_) | copy-start | bytes 3145732
  360.2 9.3 %copy-start.4 = (bf16[4,2,256,256]{3,2,1,0:T(8,128)(2,1)}, bf16[4,2,256,256]{3,2,1,0:T(8,128)(2,1)S(1)}, u32[]{:S(2)}) copy-start(bf16[4,2,256,256]{3,2,1,0:T(8,128)(2,1)S(1)} %collective-permute-done.25.refs_5_.refs_6_.refs_4_) | copy-start | bytes 3145732
  375.0 13.7 %collective-permute-start.30 = (bf16[4,8,256,256]{3,2,1,0:T(8,128)(2,1)}, bf16[4,8,256,256]{3,2,1,0:T(8,128)(2,1)}, u32[]{:S(2)}, u32[]{:S(2)}) collective-permute-start(bf16[4,8,256,256]{3,2,1,0:T(8,128)(2,1)} %broadcast_select_fusion.refs_0_), channel_id=1, source_target_pairs={{0,8},{1,9},{10,2},{11,3},{20,28},{21,29},{30,22},{31,23},{16,24},... | collective-permute-start | bytes 12582920 | tf_op jit(solution)/shard_map/ppermute | solution.py:362
  376.4 20.5 %copy-start.43 = (s32[8]{0:T(128)}, s32[8]{0:T(128)S(1)}, u32[]{:S(2)}) copy-start(s32[8]{0:T(128)S(1)} %eq.200.use_ref) | copy-start | bytes 100
  377.2 47.5 %collective-permute-start.28 = (bf16[4,2,256,256]{3,2,1,0:T(8,128)(2,1)}, bf16[4,2,256,256]{3,2,1,0:T(8,128)(2,1)S(1)}, u32[]{:S(2)}, u32[]{:S(2)}) collective-permute-start(bf16[4,2,256,256]{3,2,1,0:T(8,128)(2,1)} %get-tuple-element.83), channel_id=1, source_target_pairs={{0,24},{8,16},{16,8},{24,0},{1,25},{9,17},{17,9},{25,1},{2,26},{10... | collective-permute-start | bytes 3145736 | tf_op jit(solution)/shard_map/ppermute | solution.py:340
  384.0 48.7 %collective-permute-start.32 = (bf16[4,2,256,256]{3,2,1,0:T(8,128)(2,1)}, bf16[4,2,256,256]{3,2,1,0:T(8,128)(2,1)}, u32[]{:S(2)}, u32[]{:S(2)}) collective-permute-start(bf16[4,2,256,256]{3,2,1,0:T(8,128)(2,1)} %get-tuple-element.83), channel_id=1, source_target_pairs={{0,6},{1,7},{2,14},{3,15},{4,22},{5,23},{6,30},{7,31},{8,4},{9,5},... | collective-permute-start | bytes 3145736 | tf_op jit(solution)/shard_map/ppermute | solution.py:349
  384.0 48.7 %collective-permute-start.31 = (bf16[4,2,256,256]{3,2,1,0:T(8,128)(2,1)}, bf16[4,2,256,256]{3,2,1,0:T(8,128)(2,1)}, u32[]{:S(2)}, u32[]{:S(2)}) collective-permute-start(bf16[4,2,256,256]{3,2,1,0:T(8,128)(2,1)} %get-tuple-element.88), channel_id=1, source_target_pairs={{0,2},{1,3},{2,10},{3,11},{4,18},{5,19},{6,26},{7,27},{8,0},{9,1},... | collective-permute-start | bytes 3145736 | tf_op jit(solution)/shard_map/ppermute | solution.py:349
  387.0 45.7 %collective-permute-start.33 = (bf16[4,2,256,256]{3,2,1,0:T(8,128)(2,1)}, bf16[4,2,256,256]{3,2,1,0:T(8,128)(2,1)S(1)}, u32[]{:S(2)}, u32[]{:S(2)}) collective-permute-start(bf16[4,2,256,256]{3,2,1,0:T(8,128)(2,1)} %get-tuple-element.84.refs_3_.refs_1_), channel_id=1, source_target_pairs={{0,1},{1,0},{2,3},{3,2},{4,5},{5,4},{6,7},{7,6},{8,9},{9,8},{10,11... | collective-permute-start | bytes 3145736 | tf_op jit(solution)/shard_map/ppermute | solution.py:352
  388.6 45.9 %collective-permute-start.34 = (bf16[4,2,256,256]{3,2,1,0:T(8,128)(2,1)}, bf16[4,2,256,256]{3,2,1,0:T(8,128)(2,1)S(1)}, u32[]{:S(2)}, u32[]{:S(2)}) collective-permute-start(bf16[4,2,256,256]{3,2,1,0:T(8,128)(2,1)} %get-tuple-element.89.refs_5_.refs_3_), channel_id=1, source_target_pairs={{0,1},{1,0},{2,3},{3,2},{4,5},{5,4},{6,7},{7,6},{8,9},{9,8},{10,11... | collective-permute-start | bytes 3145736 | tf_op jit(solution)/shard_map/ppermute | solution.py:352
  424.7 9.8 %copy-start.25 = (bf16[4,2,256,256]{3,2,1,0:T(8,128)(2,1)}, bf16[4,2,256,256]{3,2,1,0:T(8,128)(2,1)S(1)}, u32[]{:S(2)}) copy-start(bf16[4,2,256,256]{3,2,1,0:T(8,128)(2,1)S(1)} %collective-permute-done.28.refs_7_.refs_6_) | copy-start | bytes 3145732
  435.5 54.3 %collective-permute-start.38 = (bf16[4,2,256,256]{3,2,1,0:T(8,128)(2,1)}, bf16[4,2,256,256]{3,2,1,0:T(8,128)(2,1)}, u32[]{:S(2)}, u32[]{:S(2)}) collective-permute-start(bf16[4,2,256,256]{3,2,1,0:T(8,128)(2,1)} %get-tuple-element.95), channel_id=1, source_target_pairs={{0,4},{1,5},{2,12},{3,13},{4,20},{5,21},{6,28},{7,29},{8,6},{9,7},... | collective-permute-start | bytes 3145736 | tf_op jit(solution)/shard_map/ppermute | solution.py:349
  437.3 52.6 %collective-permute-start.39 = (bf16[4,2,256,256]{3,2,1,0:T(8,128)(2,1)}, bf16[4,2,256,256]{3,2,1,0:T(8,128)(2,1)S(1)}, u32[]{:S(2)}, u32[]{:S(2)}) collective-permute-start(bf16[4,2,256,256]{3,2,1,0:T(8,128)(2,1)} %get-tuple-element.95), channel_id=1, source_target_pairs={{0,16},{8,24},{16,0},{24,8},{1,17},{9,25},{17,1},{25,9},{2,18},{10... | collective-permute-start | bytes 3145736 | tf_op jit(solution)/shard_map/ppermute | solution.py:340
  437.5 31.9 %collective-permute-start.35 = (bf16[4,2,256,256]{3,2,1,0:T(8,128)(2,1)}, bf16[4,2,256,256]{3,2,1,0:T(8,128)(2,1)S(1)}, u32[]{:S(2)}, u32[]{:S(2)}) collective-permute-start(bf16[4,2,256,256]{3,2,1,0:T(8,128)(2,1)} %get-tuple-element.92.refs_4_.refs_2_), channel_id=1, source_target_pairs={{0,1},{1,0},{2,3},{3,2},{4,5},{5,4},{6,7},{7,6},{8,9},{9,8},{10,11... | collective-permute-start | bytes 3145736 | tf_op jit(solution)/shard_map/ppermute | solution.py:352
  437.7 45.7 %collective-permute-start.36 = (bf16[4,2,256,256]{3,2,1,0:T(8,128)(2,1)}, bf16[4,2,256,256]{3,2,1,0:T(8,128)(2,1)S(1)}, u32[]{:S(2)}, u32[]{:S(2)}) collective-permute-start(bf16[4,2,256,256]{3,2,1,0:T(8,128)(2,1)} %get-tuple-element.93.refs_6_.refs_4_), channel_id=1, source_target_pairs={{0,1},{1,0},{2,3},{3,2},{4,5},{5,4},{6,7},{7,6},{8,9},{9,8},{10,11... | collective-permute-start | bytes 3145736 | tf_op jit(solution)/shard_map/ppermute | solution.py:352
  439.0 49.8 %collective-permute-start.37 = (bf16[4,2,256,256]{3,2,1,0:T(8,128)(2,1)}, bf16[4,2,256,256]{3,2,1,0:T(8,128)(2,1)S(1)}, u32[]{:S(2)}, u32[]{:S(2)}) collective-permute-start(bf16[4,2,256,256]{3,2,1,0:T(8,128)(2,1)} %get-tuple-element.94.refs_4_), channel_id=1, source_target_pairs={{0,0},{1,1},{2,8},{3,9},{4,16},{5,17},{6,24},{7,25},{8,2},{9,3},{1... | collective-permute-start | bytes 3145736 | tf_op jit(solution)/shard_map/ppermute | solution.py:349
  469.4 20.4 %copy-start.33 = (bf16[4,2,256,256]{3,2,1,0:T(8,128)(2,1)}, bf16[4,2,256,256]{3,2,1,0:T(8,128)(2,1)S(1)}, u32[]{:S(2)}) copy-start(bf16[4,2,256,256]{3,2,1,0:T(8,128)(2,1)S(1)} %collective-permute-done.35.refs_8_.refs_4_.refs_6_) | copy-start | bytes 3145732
  483.5 6.3 %copy-start.34 = (bf16[4,2,256,256]{3,2,1,0:T(8,128)(2,1)}, bf16[4,2,256,256]{3,2,1,0:T(8,128)(2,1)S(1)}, u32[]{:S(2)}) copy-start(bf16[4,2,256,256]{3,2,1,0:T(8,128)(2,1)S(1)} %collective-permute-done.36.refs_10_.refs_5_.refs_8_) | copy-start | bytes 3145732
  490.8 49.4 %collective-permute-start.41 = (bf16[4,2,256,256]{3,2,1,0:T(8,128)(2,1)}, bf16[4,2,256,256]{3,2,1,0:T(8,128)(2,1)S(1)}, u32[]{:S(2)}, u32[]{:S(2)}) collective-permute-start(bf16[4,2,256,256]{3,2,1,0:T(8,128)(2,1)} %get-tuple-element.97), channel_id=1, source_target_pairs={{0,6},{1,7},{2,14},{3,15},{4,22},{5,23},{6,30},{7,31},{8,4},{9,5},... | collective-permute-start | bytes 3145736 | tf_op jit(solution)/shard_map/ppermute | solution.py:349
  490.9 50.7 %collective-permute-start.44 = (bf16[4,2,256,256]{3,2,1,0:T(8,128)(2,1)}, bf16[4,2,256,256]{3,2,1,0:T(8,128)(2,1)S(1)}, u32[]{:S(2)}, u32[]{:S(2)}) collective-permute-start(bf16[4,2,256,256]{3,2,1,0:T(8,128)(2,1)} %get-tuple-element.97), channel_id=1, source_target_pairs={{0,24},{8,16},{16,8},{24,0},{1,25},{9,17},{17,9},{25,1},{2,26},{10... | collective-permute-start | bytes 3145736 | tf_op jit(solution)/shard_map/ppermute | solution.py:340
  492.9 47.3 %collective-permute-start.40 = (bf16[4,2,256,256]{3,2,1,0:T(8,128)(2,1)}, bf16[4,2,256,256]{3,2,1,0:T(8,128)(2,1)S(1)}, u32[]{:S(2)}, u32[]{:S(2)}) collective-permute-start(bf16[4,2,256,256]{3,2,1,0:T(8,128)(2,1)} %get-tuple-element.96.refs_2_), channel_id=1, source_target_pairs={{0,2},{1,3},{2,10},{3,11},{4,18},{5,19},{6,26},{7,27},{8,0},{9,1},... | collective-permute-start | bytes 3145736 | tf_op jit(solution)/shard_map/ppermute | solution.py:349
  494.6 45.6 %collective-permute-start.42 = (bf16[4,2,256,256]{3,2,1,0:T(8,128)(2,1)}, bf16[4,2,256,256]{3,2,1,0:T(8,128)(2,1)S(1)}, u32[]{:S(2)}, u32[]{:S(2)}) collective-permute-start(bf16[4,2,256,256]{3,2,1,0:T(8,128)(2,1)} %get-tuple-element.98.refs_15_), channel_id=1, source_target_pairs={{0,1},{1,0},{2,3},{3,2},{4,5},{5,4},{6,7},{7,6},{8,9},{9,8},{10,11... | collective-permute-start | bytes 3145736 | tf_op jit(solution)/shard_map/ppermute | solution.py:352
  494.9 46.5 %collective-permute-start.43 = (bf16[4,2,256,256]{3,2,1,0:T(8,128)(2,1)}, bf16[4,2,256,256]{3,2,1,0:T(8,128)(2,1)S(1)}, u32[]{:S(2)}, u32[]{:S(2)}) collective-permute-start(bf16[4,2,256,256]{3,2,1,0:T(8,128)(2,1)} %get-tuple-element.99.refs_17_), channel_id=1, source_target_pairs={{0,1},{1,0},{2,3},{3,2},{4,5},{5,4},{6,7},{7,6},{8,9},{9,8},{10,11... | collective-permute-start | bytes 3145736 | tf_op jit(solution)/shard_map/ppermute | solution.py:352
  543.5 4.4 collective-permute-start.45
  545.0 19.9 %copy-start.42 = (s32[4]{0:T(128)}, s32[4]{0:T(128)S(1)}, u32[]{:S(2)}) copy-start(s32[4]{0:T(128)S(1)} %iota_add_fusion.1.refs_0_.refs_1_) | copy-start | bytes 52
  545.0 19.9 %copy-start.41 = (s32[4]{0:T(128)}, s32[4]{0:T(128)S(1)}, u32[]{:S(2)}) copy-start(s32[4]{0:T(128)S(1)} %iota_add_fusion.4.refs_0_.refs_1_) | copy-start | bytes 52
  546.4 55.9 %collective-permute-start.46 = (bf16[4,2,256,256]{3,2,1,0:T(8,128)(2,1)}, bf16[4,2,256,256]{3,2,1,0:T(8,128)(2,1)S(1)}, u32[]{:S(2)}, u32[]{:S(2)}) collective-permute-start(bf16[4,2,256,256]{3,2,1,0:T(8,128)(2,1)} %get-tuple-element.101.refs_16_), channel_id=1, source_target_pairs={{0,1},{1,0},{2,3},{3,2},{4,5},{5,4},{6,7},{7,6},{8,9},{9,8},{10,11... | collective-permute-start | bytes 3145736 | tf_op jit(solution)/shard_map/ppermute | solution.py:352
  546.7 55.7 %collective-permute-start.47 = (bf16[4,2,256,256]{3,2,1,0:T(8,128)(2,1)}, bf16[4,2,256,256]{3,2,1,0:T(8,128)(2,1)S(1)}, u32[]{:S(2)}, u32[]{:S(2)}) collective-permute-start(bf16[4,2,256,256]{3,2,1,0:T(8,128)(2,1)} %get-tuple-element.102.refs_18_), channel_id=1, source_target_pairs={{0,1},{1,0},{2,3},{3,2},{4,5},{5,4},{6,7},{7,6},{8,9},{9,8},{10,11... | collective-permute-start | bytes 3145736 | tf_op jit(solution)/shard_map/ppermute | solution.py:352
  (28 other events, 33.3 us)

commit v3 on v2

--- a/solution.py
+++ b/solution.py
@@ -10,7 +10,7 @@
 CAP = 2
 ITERS = 2
 AXES = ("igrp", "jgrp")
-VMEM = 56 * 2**20
+VMEM = 38 * 2**20
 F32, BF16, I32 = jnp.float32, jnp.bfloat16, jnp.int32
 
 
@@ -23,7 +23,7 @@
 
 
 def resident(shape):
-    return pl.BlockSpec(shape, lambda *_: (0,) * len(shape))
+    return pl.BlockSpec(shape, lambda *_: (0,) * len(shape), pipeline_mode=pl.Buffered(1))
 
 
 def listed_offsets(neighbours, groups, rows):
@@ -117,7 +117,10 @@
         grid_spec=pltpu.PrefetchScalarGridSpec(
             num_scalar_prefetch=2,
             grid=(rows,),
-            in_specs=[pl.BlockSpec((1, listed, v, v), lambda i, slots, pick: (i, 0, 0, 0))] * len(sources),
+            in_specs=[
+                pl.BlockSpec((1, listed, v, v), lambda i, slots, pick, n=n: (jnp.where(pick[0] == n, i, 0), 0, 0, 0))
+                for n in range(len(sources))
+            ],
             out_specs=pl.BlockSpec((1, v, depth), lambda i, slots, pick: (i, 0, 0)),
         ),
         compiler_params=params(),
@@ -351,11 +354,9 @@
     def swap(self, x, d):
         return lax.ppermute(x, "jgrp", [(j, j ^ d) for j in range(self.jgroups)])
 
-    def spread(self, w, bit):
-        held = [h for h in range(self.groups) if h % (2 * bit) == 0]
+    def spread(self, w, held, bit):
         pairs = [
-            ((z ^ h) * self.jgroups + z * self.ratio + y, (z ^ h ^ bit) * self.jgroups + z * self.ratio + y)
-            for h in held
+            ((z ^ held) * self.jgroups + z * self.ratio + y, (z ^ held ^ bit) * self.jgroups + z * self.ratio + y)
             for z in range(self.groups)
             for y in range(self.ratio)
         ]
@@ -459,25 +460,22 @@
         return []
 
     bits = links.bits()
-    apart = my_i ^ my_z
-
-    def fresh(bit):
-        return apart % (2 * bit) == bit
-
-    def deliver(h, w, came, bit, later):
-        while later:
-            w = jnp.where(fresh(bit), came, w)
-            bit, later = later[0], later[1:]
-            came = links.spread(w, bit)
-        return slotted([w, came], fresh(bit), slots_of(my_j * cols + h * width, width), groups)
+
+    def deliver(h, w, far_side):
+        there = {0: w, bits[0]: far_side}
+        for bit in bits[1:]:
+            for held in list(there):
+                there[held ^ bit] = links.spread(there[held], held, bit)
+        sources = [there[n] for n in range(groups)]
+        return slotted(sources, my_i ^ my_z, slots_of(my_j * cols + h * width, width), groups)
 
     own_w = [lax.dynamic_slice_in_dim(weights, my_half * cols + h * width, width, 0) for h in chunks]
     mine = [[*pick_rows(t_start, rows, groups, width, h)] for h in chunks]
     near, far = empty()
-    last = exchange(links, mine, near, far, opening, (own_w[0], lambda w: links.spread(w, bits[0])))
+    last = exchange(links, mine, near, far, opening, (own_w[0], lambda w: links.spread(w, 0, bits[0])))
     came, second = tie([last.pop(), own_w[1]], last)
-    second_came = links.spread(second, bits[0])
-    wpj = [deliver(0, own_w[0], came, bits[0], bits[1:]), None]
+    second_came = links.spread(second, 0, bits[0])
+    wpj = [deliver(0, own_w[0], came), None]
 
     def rows_of(h, halves):
         return jnp.concatenate(
@@ -518,7 +516,7 @@
             if t == 1:
                 if wpj[1] is None:
                     [arrived] = tie([second_came], earlier)
-                    wpj[1] = deliver(1, second, arrived, bits[0], bits[1:])
+                    wpj[1] = deliver(1, second, arrived)
                 mine[1][:] = listed_rows(1, c[1])
                 return mine[1]
             if t == 0 or not final:

time: 625 us -> 606 us (0.970)
  local copies, waits for them, and re-layouts: 33.9 us -> 72.9 us
  Pallas kernels: 252 us -> 216 us
  waiting for transfers between devices: 251 us -> 237 us
  other arithmetic: 14.5 us -> 2.6 us
    unnamed x90 -> x210, local copies, waits for them, and re-layouts: 20.1 us -> 65.3 us
    pallas_call x6, Pallas kernels: 118 us -> 98.8 us  [finish(): pl.pallas_call(functools.partial(finish_kernel if into is None else kept_...]
    pallas_call x4, Pallas kernels: 73.9 us -> 64.2 us  [direct(): pl.pallas_call(functools.partial(direct_kernel, taken), out_shape=jax.Sha...]
    select_n x2 -> x0, other arithmetic: 9.21 us -> none  [deliver(): w = jnp.where(fresh(bit), came, w)]
    ppermute x12, waiting for transfers between devices: 44.5 us -> 37.7 us  [near(): return lax.ppermute(x, 'igrp', [(i, i ^ s) for i in range(self.groups)])]
    ppermute x16, waiting for transfers between devices: 45.3 us -> 39 us  [swap(): return lax.ppermute(x, 'jgrp', [(j, j ^ d) for j in range(self.jgroups)])]
  transfers between devices with their start and end apart: 48 -> 50, of which waited for: 26 -> 24; matrix products, arithmetic and copies ran while one was open for 3% -> 2% of each run, Pallas kernels for 37% -> 33%
where the time goes in v3:
time: 606 us; the launch traced here: 603 us
  waiting for transfers between devices  237 us (39%)
  Pallas kernels  216 us (36%)
  starting transfers between devices  73.1 us (12%)
  local copies, waits for them, and re-layouts  72.9 us (12%)
    ppermute x16, waiting for transfers between devices, route(): return lax.ppermute(x, AXES, pairs)  155 us
    pallas_call x6, Pallas kernels, finish(): pl.pallas_call(functools.partial(finish_kernel if into is None else kept_...  98.8 us
    unnamed x210, local copies, waits for them, and re-layouts  65.3 us
    pallas_call x4, Pallas kernels, direct(): pl.pallas_call(functools.partial(direct_kernel, taken), out_shape=jax.Sha...  64.2 us
    ppermute x16, waiting for transfers between devices, swap(): return lax.ppermute(x, 'jgrp', [(j, j ^ d) for j in range(self.jgroups)])  39 us
    ppermute x12, waiting for transfers between devices, near(): return lax.ppermute(x, 'igrp', [(i, i ^ s) for i in range(self.groups)])  37.7 us
    ppermute x16, starting transfers between devices, route(): return lax.ppermute(x, AXES, pairs)  30.9 us
    pallas_call x3, Pallas kernels, slotted(): pl.pallas_call(slotted_kernel, out_shape=jax.ShapeDtypeStruct((rows, v, d...  29.5 us
  transfers between devices with their start and end apart: 50, of which 24 were waited for; matrix products, arithmetic and copies ran while one was open for 2% of the time, Pallas kernels for 33%

profile of v3, /device:TPU:21, one launch (start us, length us, event | category | flops | bytes accessed | tf_op | source)
XLA Modules:
  0.0 602.8 jit_solution(4565076913312195169)
XLA Ops:
  2.1 4.0 pick_rows.3
  7.1 4.5 collective-permute-start.1
  12.8 1.4 collective-permute-start.4
  14.5 18.4 %slotted.3.refs_6_.refs_0_.refs_1_.refs_2_.refs_3_ = bf16[16,256,2048]{2,1,0:T(8,128)(2,1)} custom-call(s32[128]{0:T(128)S(1)} %reshape.499.slots_ref, s32[1]{0:T(128)} %constant.127.clone.1.pick_ref, bf16[16,8,256,256]{3,2,1,0:T(8,128)(2,1)} %refs_0_.5), custom_call_target="tpu_custom_call" | custom-call | bytes 33554432 | tf_op jit(solution)/shard_map/slotted/pallas_call | solution.py:114
  32.9 24.7 %collective-permute-done.1.refs_2_ = bf16[4,2,256,256]{3,2,1,0:T(8,128)(2,1)S(1)} collective-permute-done((bf16[4,2,256,256]{3,2,1,0:T(8,128)(2,1)}, bf16[4,2,256,256]{3,2,1,0:T(8,128)(2,1)S(1)}, u32[]{:S(2)}, u32[]{:S(2)}) %collective-permute-start.1) | collective-permute-done | bytes 1048608 | tf_op jit(solution)/shard_map/ppermute | solution.py:352
  60.4 2.9 collective-permute-start.5
  64.7 1.6 collective-permute-start.9
  66.3 3.1 pick_rows.2
  73.3 35.3 %collective-permute-done.5.refs_2_ = bf16[4,2,256,256]{3,2,1,0:T(8,128)(2,1)S(1)} collective-permute-done((bf16[4,2,256,256]{3,2,1,0:T(8,128)(2,1)}, bf16[4,2,256,256]{3,2,1,0:T(8,128)(2,1)S(1)}, u32[]{:S(2)}, u32[]{:S(2)}) %collective-permute-start.5) | collective-permute-done | bytes 1048608 | tf_op jit(solution)/shard_map/ppermute | solution.py:352
  108.6 1.9 collective-permute-done.6.refs_3_
  112.8 3.4 collective-permute-start.10
  121.6 13.8 %direct.4.refs_7_.refs_1_ = bf16[8,4,256,256]{3,2,1,0:T(8,128)(2,1)S(1)} custom-call(s32[8]{0:T(128)S(1)} %reshape.498.rows_ref, bf16[16,256,2048]{2,1,0:T(8,128)(2,1)} %slotted.3.refs_6_.refs_0_.refs_1_.refs_2_.refs_3_, bf16[16,256,2048]{2,1,0:T(8,128)(2,1)} %slotted.3.refs_6_.refs_0_.refs_1_.refs_2_.refs_3_, ...), custom_call_target="tpu_custom_call" | custom-call | flops 8589934592 | bytes 12582912 | tf_op jit(solution)/shard_map/direct/pallas_call | solution.py:155
  135.5 2.0 copy-done.10
  137.5 26.0 %collective-permute-done.10.refs_2_ = bf16[4,2,256,256]{3,2,1,0:T(8,128)(2,1)S(1)} collective-permute-done((bf16[4,2,256,256]{3,2,1,0:T(8,128)(2,1)}, bf16[4,2,256,256]{3,2,1,0:T(8,128)(2,1)S(1)}, u32[]{:S(2)}, u32[]{:S(2)}) %collective-permute-start.10) | collective-permute-done | bytes 1048608 | tf_op jit(solution)/shard_map/ppermute | solution.py:352
  165.2 2.9 collective-permute-start.15
  169.5 1.8 collective-permute-start.19
  171.3 6.2 %constant_dynamic-slice_fusion.1 = (bf16[4,8,256,256]{3,2,1,0:T(8,128)(2,1)}, bf16[4,8,256,256]{3,2,1,0:T(8,128)(2,1)S(1)}) fusion(bf16[16,8,256,256]{3,2,1,0:T(8,128)(2,1)} %refs_0_.5, s32[]{:T(128)S(6)} %select_n.190, s32[]{:T(128)S(6)} %select_n.187), kind=kLoop, calls=%fused_computation.42 | loop fusion | bytes 16777224 | tf_op jit(solution)/shard_map/dynamic_slice | solution.py:472
  177.6 2.0 copy.81.refs_3_
  179.5 1.3 copy-done.7
  180.9 31.3 %collective-permute-done.15.refs_0_ = bf16[4,2,256,256]{3,2,1,0:T(8,128)(2,1)S(1)} collective-permute-done((bf16[4,2,256,256]{3,2,1,0:T(8,128)(2,1)}, bf16[4,2,256,256]{3,2,1,0:T(8,128)(2,1)S(1)}, u32[]{:S(2)}, u32[]{:S(2)}) %collective-permute-start.15) | collective-permute-done | bytes 1048608 | tf_op jit(solution)/shard_map/ppermute | solution.py:352
  212.2 3.5 collective-permute-done.16.refs_1_
  220.2 2.6 collective-permute-start
  225.3 13.5 %direct.5.refs_5_.refs_1_ = bf16[8,4,256,256]{3,2,1,0:T(8,128)(2,1)S(1)} custom-call(s32[8]{0:T(128)S(1)} %reshape.498.rows_ref, bf16[16,256,2048]{2,1,0:T(8,128)(2,1)} %slotted.3.refs_6_.refs_0_.refs_1_.refs_2_.refs_3_, bf16[16,256,2048]{2,1,0:T(8,128)(2,1)} %slotted.3.refs_6_.refs_0_.refs_1_.refs_2_.refs_3_, ...), custom_call_target="tpu_custom_call" | custom-call | flops 8589934592 | bytes 12582912 | tf_op jit(solution)/shard_map/direct/pallas_call | solution.py:155
  238.9 2.0 copy-done.9
  240.9 2.4 collective-permute-done.21.refs_2_.refs_16_
  243.3 22.5 %collective-permute-done.22.refs_3_.refs_18_ = bf16[4,2,256,256]{3,2,1,0:T(8,128)(2,1)S(1)} collective-permute-done((bf16[4,2,256,256]{3,2,1,0:T(8,128)(2,1)}, bf16[4,2,256,256]{3,2,1,0:T(8,128)(2,1)S(1)}, u32[]{:S(2)}, u32[]{:S(2)}) %collective-permute-start.22) | collective-permute-done | bytes 1048608 | tf_op jit(solution)/shard_map/ppermute | solution.py:355
  265.8 2.1 copy-done.101
  268.2 1.4 collective-permute-start.24
  269.7 2.7 collective-permute-start.31
  273.4 5.0 collective-permute-done.24.refs_3_
  278.4 2.2 copy-done.8
  280.7 5.4 slotted.4.refs_0_.refs_9_
  286.1 1.9 copy-done.1
  288.1 18.9 %finish.6 = (bf16[4,2,256,256]{3,2,1,0:T(8,128)(2,1)S(1)}, bf16[4,2,256,256]{3,2,1,0:T(8,128)(2,1)S(1)}, bf16[4,2,256,256]{3,2,1,0:T(8,128)(2,1)S(1)}, bf16[4,2,256,256]{3,2,1,0:T(8,128)(2,1)S(1)}) custom-call(s32[8]{0:T(128)S(1)} %reshape.498.rows_ref, s32[8]{0:T(128)S(1)} %iota.159.crows_ref, s32[4]{0:T(128)S(1)} %pad_add_fusion.where_ref.refs_2_, ...), custom_call_target="tpu_custom_call" | custom-call | flops 8589934592 | bytes 25165824 | tf_op jit(solution)/shard_map/finish/pallas_call | solution.py:264
  309.0 3.8 collective-permute-start.27
  314.5 2.7 collective-permute-start.30
  317.1 35.2 %collective-permute-done.26.refs_5_.refs_6_.refs_4_ = bf16[4,2,256,256]{3,2,1,0:T(8,128)(2,1)S(1)} collective-permute-done((bf16[4,2,256,256]{3,2,1,0:T(8,128)(2,1)S(1)}, bf16[4,2,256,256]{3,2,1,0:T(8,128)(2,1)S(1)}, u32[]{:S(2)}, u32[]{:S(2)}) %collective-permute-start.26) | collective-permute-done | bytes 1048608 | tf_op jit(solution)/shard_map/ppermute | solution.py:343
  352.3 7.0 %collective-permute-done.27.refs_2_.refs_1_ = bf16[4,2,256,256]{3,2,1,0:T(8,128)(2,1)S(1)} collective-permute-done((bf16[4,2,256,256]{3,2,1,0:T(8,128)(2,1)S(1)}, bf16[4,2,256,256]{3,2,1,0:T(8,128)(2,1)S(1)}, u32[]{:S(2)}, u32[]{:S(2)}) %collective-permute-start.27) | collective-permute-done | bytes 1048608 | tf_op jit(solution)/shard_map/ppermute | solution.py:352
  359.4 2.3 collective-permute-done.28.refs_3_.refs_2_
  363.4 9.2 %collective-permute-start.29 = (bf16[4,2,256,256]{3,2,1,0:T(8,128)(2,1)}, bf16[4,2,256,256]{3,2,1,0:T(8,128)(2,1)}, u32[]{:S(2)}, u32[]{:S(2)}) collective-permute-start(bf16[4,2,256,256]{3,2,1,0:T(8,128)(2,1)} %get-tuple-element.83), channel_id=1, source_target_pairs={{0,24},{8,16},{16,8},{24,0},{1,25},{9,17},{17,9},{25,1},{2,26},{10... | collective-permute-start | bytes 3145736 | tf_op jit(solution)/shard_map/ppermute | solution.py:343
  372.7 4.7 collective-permute-start.33
  379.4 5.7 slotted.5.refs_0_.refs_10_
  385.2 2.0 copy-done.5
  387.2 18.9 %finish.7 = (bf16[4,2,256,256]{3,2,1,0:T(8,128)(2,1)S(1)}, bf16[4,2,256,256]{3,2,1,0:T(8,128)(2,1)S(1)}, bf16[4,2,256,256]{3,2,1,0:T(8,128)(2,1)S(1)}, bf16[4,2,256,256]{3,2,1,0:T(8,128)(2,1)S(1)}) custom-call(s32[8]{0:T(128)S(1)} %reshape.498.rows_ref, s32[8]{0:T(128)S(1)} %iota.160.crows_ref, s32[4]{0:T(128)S(1)} %get-tuple-element.107.where_ref, ...), custom_call_target="tpu_custom_call" | custom-call | flops 8589934592 | bytes 25165824 | tf_op jit(solution)/shard_map/finish/pallas_call | solution.py:264
  411.4 12.2 %collective-permute-done.33.refs_2_ = bf16[4,2,256,256]{3,2,1,0:T(8,128)(2,1)} collective-permute-done((bf16[4,2,256,256]{3,2,1,0:T(8,128)(2,1)}, bf16[4,2,256,256]{3,2,1,0:T(8,128)(2,1)}, u32[]{:S(2)}, u32[]{:S(2)}) %collective-permute-start.33) | collective-permute-done | bytes 1048608 | tf_op jit(solution)/shard_map/ppermute | solution.py:352
  426.2 1.7 collective-permute-start.41
  429.3 3.2 collective-permute-start.39
  433.8 23.7 %direct.6.refs_1_.refs_7_.refs_11_ = bf16[16,4,256,256]{3,2,1,0:T(8,128)(2,1)S(1)} custom-call(s32[16]{0:T(128)S(1)} %iota.158.rows_ref, bf16[16,256,2048]{2,1,0:T(8,128)(2,1)} %slotted.3.refs_6_.refs_0_.refs_1_.refs_2_.refs_3_, bf16[16,256,2048]{2,1,0:T(8,128)(2,1)} %slotted.3.refs_6_.refs_0_.refs_1_.refs_2_.refs_3_, ...), custom_call_target="tpu_custom_call" | custom-call | flops 17179869184 | bytes 25165824 | tf_op jit(solution)/shard_map/direct/pallas_call | solution.py:155
  457.5 3.3 copy-done
  460.8 13.3 %collective-permute-done.38.refs_10_.refs_5_.refs_8_ = bf16[4,2,256,256]{3,2,1,0:T(8,128)(2,1)S(1)} collective-permute-done((bf16[4,2,256,256]{3,2,1,0:T(8,128)(2,1)}, bf16[4,2,256,256]{3,2,1,0:T(8,128)(2,1)S(1)}, u32[]{:S(2)}, u32[]{:S(2)}) %collective-permute-start.38) | collective-permute-done | bytes 1048608 | tf_op jit(solution)/shard_map/ppermute | solution.py:355
  474.1 4.9 collective-permute-done.39.refs_2_
  481.9 1.7 collective-permute-start.46
  483.7 1.8 collective-permute-start.42
  486.9 2.2 copy-done.2
  494.0 16.4 %finish.8.refs_7_.refs_8_ = f32[16,8,256,256]{3,2,1,0:T(8,128)} custom-call(s32[8]{0:T(128)S(1)} %get-tuple-element.106.rows_ref.crows_ref, s32[8]{0:T(128)S(1)} %get-tuple-element.106.rows_ref.crows_ref, s32[4]{0:T(128)S(1)} %pad_add_fusion.where_ref.refs_2_, s32[16]{0:T(128)S(1)} %select_n.184.held_ref, s32[8]{0:T(128)S(1)} %eq.188.use_ref, ...), custom_call_target="tpu_custom_call" | custom-call | flops 8589934592 | bytes 25165824 | tf_op jit(solution)/shard_map/finish/pallas_call | solution.py:264
  510.3 14.8 %finish.9.refs_6_.refs_8_ = bf16[8,4,256,256]{3,2,1,0:T(8,128)(2,1)S(1)} custom-call(s32[8]{0:T(128)S(1)} %get-tuple-element.106.rows_ref.crows_ref, s32[8]{0:T(128)S(1)} %get-tuple-element.106.rows_ref.crows_ref, s32[4]{0:T(128)S(1)} %get-tuple-element.107.where_ref, s32[16]{0:T(128)S(1)} %select_n.184.held_ref, s32[8]{0:T(128)S(1)} %eq.188.use_ref, ...), custom_call_target="tpu_custom_call" | custom-call | flops 8589934592 | bytes 25165824 | tf_op jit(solution)/shard_map/finish/pallas_call | solution.py:264
  525.1 2.1 copy-done.11
  527.2 4.0 collective-permute-done.42.refs_0_
  538.2 1.9 copy-done.14
  540.1 13.2 %direct.7.refs_12_ = bf16[16,4,256,256]{3,2,1,0:T(8,128)(2,1)S(1)} custom-call(s32[8]{0:T(128)S(1)} %pad_add_fusion.4.rows_ref, bf16[16,256,2048]{2,1,0:T(8,128)(2,1)} %slotted.3.refs_6_.refs_0_.refs_1_.refs_2_.refs_3_, bf16[16,256,2048]{2,1,0:T(8,128)(2,1)} %slotted.3.refs_6_.refs_0_.refs_1_.refs_2_.refs_3_, ...), custom_call_target="tpu_custom_call" | custom-call | flops 8589934592 | bytes 12582912 | tf_op jit(solution)/shard_map/direct/pallas_call | solution.py:155
  553.3 3.2 copy-done.4
  556.6 15.0 %finish.10.into_ref = f32[16,8,256,256]{3,2,1,0:T(8,128)} custom-call(s32[4]{0:T(128)S(1)} %iota_add_fusion.1.refs_0_.refs_1_, s32[4]{0:T(128)S(1)} %iota_add_fusion.1.refs_0_.refs_1_, s32[4]{0:T(128)S(1)} %pad_add_fusion.where_ref.refs_2_, s32[4]{0:T(128)S(1)} %get-tuple-element.103.refs_3_, ...), custom_call_target="tpu_custom_call", output_to_operand_aliasing={{}: (8, {})} | custom-call | flops 8589934592 | bytes 29360128 | tf_op jit(solution)/shard_map/finish/pallas_call | solution.py:264
  571.5 16.5 %joined.1.refs_8_ = f32[16,8,256,256]{3,2,1,0:T(8,128)} custom-call(s32[8]{0:T(128)S(1)} %get-tuple-element.106.rows_ref.crows_ref, s32[4]{0:T(128)S(1)} %get-tuple-element.107.where_ref, f32[64]{0:T(128)S(1)} %copy-done.100, f32[256,1]{1,0:T(8,128)S(1)} %copy.65.tall_ref.refs_6_, f32[1,256]{1,0:T(1,128)S(1)} %bitcast.13, ...), custom_call_target="tpu_custom_call", output_to_operand_aliasing={{}: (5, {})} | custom-call | flops 8589934592 | bytes 25165824 | tf_op jit(solution)/shard_map/joined/pallas_call | solution.py:315
  588.1 14.8 %finish.11 = f32[16,8,256,256]{3,2,1,0:T(8,128)} custom-call(s32[4]{0:T(128)S(1)} %iota_add_fusion.4.refs_0_.refs_1_, s32[4]{0:T(128)S(1)} %iota_add_fusion.4.refs_0_.refs_1_, s32[4]{0:T(128)S(1)} %pad_add_fusion.where_ref.refs_2_, s32[4]{0:T(128)S(1)} %get-tuple-element.104.refs_3_, s32[4]{0:T(128)S(1)} %broadcast.533.refs_4_, ...), custom_call_target="tpu_custom_call", output_to_operand_aliasing={{}: (8, {})} | custom-call | flops 8589934592 | bytes 29360128 | tf_op jit(solution)/shard_map/finish/pallas_call | solution.py:264
  (327 shorter events, 65.8 us)
Async XLA Ops:
  7.1 50.6 %collective-permute-start.1 = (bf16[4,2,256,256]{3,2,1,0:T(8,128)(2,1)}, bf16[4,2,256,256]{3,2,1,0:T(8,128)(2,1)S(1)}, u32[]{:S(2)}, u32[]{:S(2)}) collective-permute-start(bf16[4,2,256,256]{3,2,1,0:T(8,128)(2,1)} %get-tuple-element.60.refs_4_), channel_id=1, source_target_pairs={{0,0},{1,1},{2,8},{3,9},{4,16},{5,17},{6,24},{7,25},{8,2},{9,3},{1... | collective-permute-start | bytes 3145736 | tf_op jit(solution)/shard_map/ppermute | solution.py:352
  11.6 47.4 %collective-permute-start.2 = (bf16[4,2,256,256]{3,2,1,0:T(8,128)(2,1)}, bf16[4,2,256,256]{3,2,1,0:T(8,128)(2,1)S(1)}, u32[]{:S(2)}, u32[]{:S(2)}) collective-permute-start(bf16[4,2,256,256]{3,2,1,0:T(8,128)(2,1)} %get-tuple-element.61), channel_id=1, source_target_pairs={{0,4},{1,5},{2,12},{3,13},{4,20},{5,21},{6,28},{7,29},{8,6},{9,7},... | collective-permute-start | bytes 3145736 | tf_op jit(solution)/shard_map/ppermute | solution.py:352
  12.8 46.2 %collective-permute-start.3 = (bf16[4,2,256,256]{3,2,1,0:T(8,128)(2,1)}, bf16[4,2,256,256]{3,2,1,0:T(8,128)(2,1)S(1)}, u32[]{:S(2)}, u32[]{:S(2)}) collective-permute-start(bf16[4,2,256,256]{3,2,1,0:T(8,128)(2,1)} %get-tuple-element.58.refs_0_), channel_id=1, source_target_pairs={{0,8},{8,0},{16,24},{24,16},{1,9},{9,1},{17,25},{25,17},{2,10},{10... | collective-permute-start | bytes 3145736 | tf_op jit(solution)/shard_map/ppermute | solution.py:343
  12.8 46.2 %collective-permute-start.4 = (bf16[4,2,256,256]{3,2,1,0:T(8,128)(2,1)}, bf16[4,2,256,256]{3,2,1,0:T(8,128)(2,1)}, u32[]{:S(2)}, u32[]{:S(2)}) collective-permute-start(bf16[4,2,256,256]{3,2,1,0:T(8,128)(2,1)} %get-tuple-element.61), channel_id=1, source_target_pairs={{0,16},{8,24},{16,0},{24,8},{1,17},{9,25},{17,1},{25,9},{2,18},{10... | collective-permute-start | bytes 3145736 | tf_op jit(solution)/shard_map/ppermute | solution.py:343
  60.4 48.2 %collective-permute-start.5 = (bf16[4,2,256,256]{3,2,1,0:T(8,128)(2,1)}, bf16[4,2,256,256]{3,2,1,0:T(8,128)(2,1)S(1)}, u32[]{:S(2)}, u32[]{:S(2)}) collective-permute-start(bf16[4,2,256,256]{3,2,1,0:T(8,128)(2,1)} %get-tuple-element.62), channel_id=1, source_target_pairs={{0,2},{1,3},{2,10},{3,11},{4,18},{5,19},{6,26},{7,27},{8,0},{9,1},... | collective-permute-start | bytes 3145736 | tf_op jit(solution)/shard_map/ppermute | solution.py:352
  63.2 47.2 %collective-permute-start.6 = (bf16[4,2,256,256]{3,2,1,0:T(8,128)(2,1)}, bf16[4,2,256,256]{3,2,1,0:T(8,128)(2,1)S(1)}, u32[]{:S(2)}, u32[]{:S(2)}) collective-permute-start(bf16[4,2,256,256]{3,2,1,0:T(8,128)(2,1)} %get-tuple-element.63), channel_id=1, source_target_pairs={{0,6},{1,7},{2,14},{3,15},{4,22},{5,23},{6,30},{7,31},{8,4},{9,5},... | collective-permute-start | bytes 3145736 | tf_op jit(solution)/shard_map/ppermute | solution.py:352
  63.2 47.2 %collective-permute-start.7 = (bf16[4,2,256,256]{3,2,1,0:T(8,128)(2,1)}, bf16[4,2,256,256]{3,2,1,0:T(8,128)(2,1)S(1)}, u32[]{:S(2)}, u32[]{:S(2)}) collective-permute-start(bf16[4,2,256,256]{3,2,1,0:T(8,128)(2,1)} %get-tuple-element.64.refs_3_), channel_id=1, source_target_pairs={{0,1},{1,0},{2,3},{3,2},{4,5},{5,4},{6,7},{7,6},{8,9},{9,8},{10,11... | collective-permute-start | bytes 3145736 | tf_op jit(solution)/shard_map/ppermute | solution.py:355
  63.4 47.0 %collective-permute-start.8 = (bf16[4,2,256,256]{3,2,1,0:T(8,128)(2,1)}, bf16[4,2,256,256]{3,2,1,0:T(8,128)(2,1)S(1)}, u32[]{:S(2)}, u32[]{:S(2)}) collective-permute-start(bf16[4,2,256,256]{3,2,1,0:T(8,128)(2,1)} %get-tuple-element.65.refs_5_), channel_id=1, source_target_pairs={{0,1},{1,0},{2,3},{3,2},{4,5},{5,4},{6,7},{7,6},{8,9},{9,8},{10,11... | collective-permute-start | bytes 3145736 | tf_op jit(solution)/shard_map/ppermute | solution.py:355
  64.7 46.8 %collective-permute-start.9 = (bf16[4,2,256,256]{3,2,1,0:T(8,128)(2,1)}, bf16[4,2,256,256]{3,2,1,0:T(8,128)(2,1)S(1)}, u32[]{:S(2)}, u32[]{:S(2)}) collective-permute-start(bf16[4,2,256,256]{3,2,1,0:T(8,128)(2,1)} %get-tuple-element.63), channel_id=1, source_target_pairs={{0,24},{8,16},{16,8},{24,0},{1,25},{9,17},{17,9},{25,1},{2,26},{10... | collective-permute-start | bytes 3145736 | tf_op jit(solution)/shard_map/ppermute | solution.py:343
  112.8 50.7 %collective-permute-start.10 = (bf16[4,2,256,256]{3,2,1,0:T(8,128)(2,1)}, bf16[4,2,256,256]{3,2,1,0:T(8,128)(2,1)S(1)}, u32[]{:S(2)}, u32[]{:S(2)}) collective-permute-start(bf16[4,2,256,256]{3,2,1,0:T(8,128)(2,1)} %get-tuple-element.66.refs_4_), channel_id=1, source_target_pairs={{0,0},{1,1},{2,8},{3,9},{4,16},{5,17},{6,24},{7,25},{8,2},{9,3},{1... | collective-permute-start | bytes 3145736 | tf_op jit(solution)/shard_map/ppermute | solution.py:352
  116.2 47.4 %collective-permute-start.11 = (bf16[4,2,256,256]{3,2,1,0:T(8,128)(2,1)}, bf16[4,2,256,256]{3,2,1,0:T(8,128)(2,1)S(1)}, u32[]{:S(2)}, u32[]{:S(2)}) collective-permute-start(bf16[4,2,256,256]{3,2,1,0:T(8,128)(2,1)} %get-tuple-element.67), channel_id=1, source_target_pairs={{0,4},{1,5},{2,12},{3,13},{4,20},{5,21},{6,28},{7,29},{8,6},{9,7},... | collective-permute-start | bytes 3145736 | tf_op jit(solution)/shard_map/ppermute | solution.py:352
  117.1 46.5 %collective-permute-start.12 = (bf16[4,2,256,256]{3,2,1,0:T(8,128)(2,1)}, bf16[4,2,256,256]{3,2,1,0:T(8,128)(2,1)S(1)}, u32[]{:S(2)}, u32[]{:S(2)}) collective-permute-start(bf16[4,2,256,256]{3,2,1,0:T(8,128)(2,1)} %get-tuple-element.68.refs_4_), channel_id=1, source_target_pairs={{0,1},{1,0},{2,3},{3,2},{4,5},{5,4},{6,7},{7,6},{8,9},{9,8},{10,11... | collective-permute-start | bytes 3145736 | tf_op jit(solution)/shard_map/ppermute | solution.py:355
  117.4 46.3 %collective-permute-start.13 = (bf16[4,2,256,256]{3,2,1,0:T(8,128)(2,1)}, bf16[4,2,256,256]{3,2,1,0:T(8,128)(2,1)}, u32[]{:S(2)}, u32[]{:S(2)}) collective-permute-start(bf16[4,2,256,256]{3,2,1,0:T(8,128)(2,1)} %get-tuple-element.69.refs_6_), channel_id=1, source_target_pairs={{0,1},{1,0},{2,3},{3,2},{4,5},{5,4},{6,7},{7,6},{8,9},{9,8},{10,11... | collective-permute-start | bytes 3145736 | tf_op jit(solution)/shard_map/ppermute | solution.py:355
  118.6 45.8 %collective-permute-start.14 = (bf16[4,2,256,256]{3,2,1,0:T(8,128)(2,1)}, bf16[4,2,256,256]{3,2,1,0:T(8,128)(2,1)}, u32[]{:S(2)}, u32[]{:S(2)}) collective-permute-start(bf16[4,2,256,256]{3,2,1,0:T(8,128)(2,1)} %get-tuple-element.67), channel_id=1, source_target_pairs={{0,16},{8,24},{16,0},{24,8},{1,17},{9,25},{17,1},{25,9},{2,18},{10... | collective-permute-start | bytes 3145736 | tf_op jit(solution)/shard_map/ppermute | solution.py:343
  165.2 47.0 %collective-permute-start.15 = (bf16[4,2,256,256]{3,2,1,0:T(8,128)(2,1)}, bf16[4,2,256,256]{3,2,1,0:T(8,128)(2,1)S(1)}, u32[]{:S(2)}, u32[]{:S(2)}) collective-permute-start(bf16[4,2,256,256]{3,2,1,0:T(8,128)(2,1)} %get-tuple-element.70.refs_2_), channel_id=1, source_target_pairs={{0,2},{1,3},{2,10},{3,11},{4,18},{5,19},{6,26},{7,27},{8,0},{9,1},... | collective-permute-start | bytes 3145736 | tf_op jit(solution)/shard_map/ppermute | solution.py:352
  168.1 47.6 %collective-permute-start.16 = (bf16[4,2,256,256]{3,2,1,0:T(8,128)(2,1)}, bf16[4,2,256,256]{3,2,1,0:T(8,128)(2,1)S(1)}, u32[]{:S(2)}, u32[]{:S(2)}) collective-permute-start(bf16[4,2,256,256]{3,2,1,0:T(8,128)(2,1)} %get-tuple-element.71), channel_id=1, source_target_pairs={{0,6},{1,7},{2,14},{3,15},{4,22},{5,23},{6,30},{7,31},{8,4},{9,5},... | collective-permute-start | bytes 3145736 | tf_op jit(solution)/shard_map/ppermute | solution.py:352
  168.1 47.6 %collective-permute-start.17 = (bf16[4,2,256,256]{3,2,1,0:T(8,128)(2,1)}, bf16[4,2,256,256]{3,2,1,0:T(8,128)(2,1)}, u32[]{:S(2)}, u32[]{:S(2)}) collective-permute-start(bf16[4,2,256,256]{3,2,1,0:T(8,128)(2,1)} %get-tuple-element.72.refs_7_), channel_id=1, source_target_pairs={{0,1},{1,0},{2,3},{3,2},{4,5},{5,4},{6,7},{7,6},{8,9},{9,8},{10,11... | collective-permute-start | bytes 3145736 | tf_op jit(solution)/shard_map/ppermute | solution.py:355
  168.3 47.5 %collective-permute-start.18 = (bf16[4,2,256,256]{3,2,1,0:T(8,128)(2,1)}, bf16[4,2,256,256]{3,2,1,0:T(8,128)(2,1)}, u32[]{:S(2)}, u32[]{:S(2)}) collective-permute-start(bf16[4,2,256,256]{3,2,1,0:T(8,128)(2,1)} %get-tuple-element.73.refs_9_), channel_id=1, source_target_pairs={{0,1},{1,0},{2,3},{3,2},{4,5},{5,4},{6,7},{7,6},{8,9},{9,8},{10,11... | collective-permute-start | bytes 3145736 | tf_op jit(solution)/shard_map/ppermute | solution.py:355
  169.5 46.2 %collective-permute-start.19 = (bf16[4,2,256,256]{3,2,1,0:T(8,128)(2,1)}, bf16[4,2,256,256]{3,2,1,0:T(8,128)(2,1)S(1)}, u32[]{:S(2)}, u32[]{:S(2)}) collective-permute-start(bf16[4,2,256,256]{3,2,1,0:T(8,128)(2,1)} %get-tuple-element.71), channel_id=1, source_target_pairs={{0,24},{8,16},{16,8},{24,0},{1,25},{9,17},{17,9},{25,1},{2,26},{10... | collective-permute-start | bytes 3145736 | tf_op jit(solution)/shard_map/ppermute | solution.py:343
  217.7 48.2 %collective-permute-start.20 = (bf16[4,8,256,256]{3,2,1,0:T(8,128)(2,1)}, bf16[4,8,256,256]{3,2,1,0:T(8,128)(2,1)S(1)}, u32[]{:S(2)}, u32[]{:S(2)}) collective-permute-start(bf16[4,8,256,256]{3,2,1,0:T(8,128)(2,1)} %get-tuple-element.74), channel_id=1, source_target_pairs={{0,16},{1,17},{10,26},{11,27},{20,4},{21,5},{30,14},{31,15}} | collective-permute-start | bytes 12582920 | tf_op jit(solution)/shard_map/ppermute | solution.py:363
  218.6 4.3 collective-permute-start.23
  218.8 24.6 %collective-permute-start.21 = (bf16[4,2,256,256]{3,2,1,0:T(8,128)(2,1)}, bf16[4,2,256,256]{3,2,1,0:T(8,128)(2,1)S(1)}, u32[]{:S(2)}, u32[]{:S(2)}) collective-permute-start(bf16[4,2,256,256]{3,2,1,0:T(8,128)(2,1)} %get-tuple-element.75.refs_8_), channel_id=1, source_target_pairs={{0,1},{1,0},{2,3},{3,2},{4,5},{5,4},{6,7},{7,6},{8,9},{9,8},{10,11... | collective-permute-start | bytes 3145736 | tf_op jit(solution)/shard_map/ppermute | solution.py:355
  219.0 46.8 %collective-permute-start.22 = (bf16[4,2,256,256]{3,2,1,0:T(8,128)(2,1)}, bf16[4,2,256,256]{3,2,1,0:T(8,128)(2,1)S(1)}, u32[]{:S(2)}, u32[]{:S(2)}) collective-permute-start(bf16[4,2,256,256]{3,2,1,0:T(8,128)(2,1)} %get-tuple-element.76.refs_10_), channel_id=1, source_target_pairs={{0,1},{1,0},{2,3},{3,2},{4,5},{5,4},{6,7},{7,6},{8,9},{9,8},{10,11... | collective-permute-start | bytes 3145736 | tf_op jit(solution)/shard_map/ppermute | solution.py:355
  220.2 53.2 %collective-permute-start = (bf16[4,8,256,256]{3,2,1,0:T(8,128)(2,1)}, bf16[4,8,256,256]{3,2,1,0:T(8,128)(2,1)}, u32[]{:S(2)}, u32[]{:S(2)}) collective-permute-start(bf16[4,8,256,256]{3,2,1,0:T(8,128)(2,1)} %copy-done.7), channel_id=1, source_target_pairs={{0,8},{1,9},{10,2},{11,3},{20,28},{21,29},{30,22},{31,23}} | collective-permute-start | bytes 12582920 | tf_op jit(solution)/shard_map/ppermute | solution.py:363
  243.3 24.6 %copy-start.102 = (bf16[4,2,256,256]{3,2,1,0:T(8,128)(2,1)}, bf16[4,2,256,256]{3,2,1,0:T(8,128)(2,1)S(1)}, u32[]{:S(2)}) copy-start(bf16[4,2,256,256]{3,2,1,0:T(8,128)(2,1)S(1)} %collective-permute-done.21.refs_2_.refs_16_) | copy-start | bytes 3145732
  268.2 10.2 %collective-permute-start.24 = (bf16[4,8,256,256]{3,2,1,0:T(8,128)(2,1)}, bf16[4,8,256,256]{3,2,1,0:T(8,128)(2,1)}, u32[]{:S(2)}, u32[]{:S(2)}) collective-permute-start(bf16[4,8,256,256]{3,2,1,0:T(8,128)(2,1)} %get-tuple-element.78.refs_2_), channel_id=1, source_target_pairs={{16,24},{17,25},{26,18},{27,19},{4,12},{5,13},{14,6},{15,7}} | collective-permute-start | bytes 12582920 | tf_op jit(solution)/shard_map/ppermute | solution.py:363
  269.7 44.8 %collective-permute-start.31 = (bf16[4,8,256,256]{3,2,1,0:T(8,128)(2,1)}, bf16[4,8,256,256]{3,2,1,0:T(8,128)(2,1)}, u32[]{:S(2)}, u32[]{:S(2)}) collective-permute-start(bf16[4,8,256,256]{3,2,1,0:T(8,128)(2,1)} %get-tuple-element.85.refs_0_), channel_id=1, source_target_pairs={{0,16},{1,17},{10,26},{11,27},{20,4},{21,5},{30,14},{31,15}} | collective-permute-start | bytes 12582920 | tf_op jit(solution)/shard_map/ppermute | solution.py:363
  308.1 51.3 %copy-start.96 = (bf16[4,2,256,256]{3,2,1,0:T(8,128)(2,1)}, bf16[4,2,256,256]{3,2,1,0:T(8,128)(2,1)S(1)}, u32[]{:S(2)}) copy-start(bf16[4,2,256,256]{3,2,1,0:T(8,128)(2,1)S(1)} %get-tuple-element.80.refs_0_) | copy-start | bytes 3145732
  308.1 9.1 %collective-permute-start.25 = (bf16[4,2,256,256]{3,2,1,0:T(8,128)(2,1)S(1)}, bf16[4,2,256,256]{3,2,1,0:T(8,128)(2,1)S(1)}, u32[]{:S(2)}, u32[]{:S(2)}) collective-permute-start(bf16[4,2,256,256]{3,2,1,0:T(8,128)(2,1)S(1)} %get-tuple-element.80.refs_0_), channel_id=1, source_target_pairs={{0,8},{8,0},{16,24},{24,16},{1,9},{9,1},{17,25},{25,17},{2,10},{10... | collective-permute-start | bytes 3145736 | tf_op jit(solution)/shard_map/ppermute | solution.py:343
  308.2 44.1 %collective-permute-start.26 = (bf16[4,2,256,256]{3,2,1,0:T(8,128)(2,1)S(1)}, bf16[4,2,256,256]{3,2,1,0:T(8,128)(2,1)S(1)}, u32[]{:S(2)}, u32[]{:S(2)}) collective-permute-start(bf16[4,2,256,256]{3,2,1,0:T(8,128)(2,1)S(1)} %get-tuple-element.81), channel_id=1, source_target_pairs={{0,16},{8,24},{16,0},{24,8},{1,17},{9,25},{17,1},{25,9},{2,18},{10... | collective-permute-start | bytes 3145736 | tf_op jit(solution)/shard_map/ppermute | solution.py:343
  309.0 50.4 %collective-permute-start.27 = (bf16[4,2,256,256]{3,2,1,0:T(8,128)(2,1)S(1)}, bf16[4,2,256,256]{3,2,1,0:T(8,128)(2,1)S(1)}, u32[]{:S(2)}, u32[]{:S(2)}) collective-permute-start(bf16[4,2,256,256]{3,2,1,0:T(8,128)(2,1)S(1)} %get-tuple-element.79.refs_4_), channel_id=1, source_target_pairs={{0,0},{1,1},{2,8},{3,9},{4,16},{5,17},{6,24},{7,25},{8,2},{9,3},{1... | collective-permute-start | bytes 3145736 | tf_op jit(solution)/shard_map/ppermute | solution.py:352
  313.8 47.9 %collective-permute-start.28 = (bf16[4,2,256,256]{3,2,1,0:T(8,128)(2,1)S(1)}, bf16[4,2,256,256]{3,2,1,0:T(8,128)(2,1)}, u32[]{:S(2)}, u32[]{:S(2)}) collective-permute-start(bf16[4,2,256,256]{3,2,1,0:T(8,128)(2,1)S(1)} %get-tuple-element.81), channel_id=1, source_target_pairs={{0,4},{1,5},{2,12},{3,13},{4,20},{5,21},{6,28},{7,29},{8,6},{9,7},... | collective-permute-start | bytes 3145736 | tf_op jit(solution)/shard_map/ppermute | solution.py:352
  314.5 62.9 %collective-permute-start.30 = (bf16[4,8,256,256]{3,2,1,0:T(8,128)(2,1)}, bf16[4,8,256,256]{3,2,1,0:T(8,128)(2,1)}, u32[]{:S(2)}, u32[]{:S(2)}) collective-permute-start(bf16[4,8,256,256]{3,2,1,0:T(8,128)(2,1)} %get-tuple-element.85.refs_0_), channel_id=1, source_target_pairs={{0,8},{1,9},{10,2},{11,3},{20,28},{21,29},{30,22},{31,23}} | collective-permute-start | bytes 12582920 | tf_op jit(solution)/shard_map/ppermute | solution.py:363
  317.1 44.5 %copy-start.20 = (bf16[4,2,256,256]{3,2,1,0:T(8,128)(2,1)}, bf16[4,2,256,256]{3,2,1,0:T(8,128)(2,1)S(1)}, u32[]{:S(2)}) copy-start(bf16[4,2,256,256]{3,2,1,0:T(8,128)(2,1)S(1)} %collective-permute-done.25.refs_4_.refs_5_.refs_3_) | copy-start | bytes 3145732
  361.7 16.8 %collective-permute-start.32 = (bf16[4,8,256,256]{3,2,1,0:T(8,128)(2,1)}, bf16[4,8,256,256]{3,2,1,0:T(8,128)(2,1)}, u32[]{:S(2)}, u32[]{:S(2)}) collective-permute-start(bf16[4,8,256,256]{3,2,1,0:T(8,128)(2,1)} %tie.16.refs_2_), channel_id=1, source_target_pairs={{16,24},{17,25},{26,18},{27,19},{4,12},{5,13},{14,6},{15,7}} | collective-permute-start | bytes 12582920 | tf_op jit(solution)/shard_map/ppermute | solution.py:363
  363.4 48.0 %collective-permute-start.29 = (bf16[4,2,256,256]{3,2,1,0:T(8,128)(2,1)}, bf16[4,2,256,256]{3,2,1,0:T(8,128)(2,1)}, u32[]{:S(2)}, u32[]{:S(2)}) collective-permute-start(bf16[4,2,256,256]{3,2,1,0:T(8,128)(2,1)} %get-tuple-element.83), channel_id=1, source_target_pairs={{0,24},{8,16},{16,8},{24,0},{1,25},{9,17},{17,9},{25,1},{2,26},{10... | collective-permute-start | bytes 3145736 | tf_op jit(solution)/shard_map/ppermute | solution.py:343
  372.6 51.0 %collective-permute-start.34 = (bf16[4,2,256,256]{3,2,1,0:T(8,128)(2,1)}, bf16[4,2,256,256]{3,2,1,0:T(8,128)(2,1)}, u32[]{:S(2)}, u32[]{:S(2)}) collective-permute-start(bf16[4,2,256,256]{3,2,1,0:T(8,128)(2,1)} %get-tuple-element.83), channel_id=1, source_target_pairs={{0,6},{1,7},{2,14},{3,15},{4,22},{5,23},{6,30},{7,31},{8,4},{9,5},... | collective-permute-start | bytes 3145736 | tf_op jit(solution)/shard_map/ppermute | solution.py:352
  372.7 50.9 %collective-permute-start.33 = (bf16[4,2,256,256]{3,2,1,0:T(8,128)(2,1)}, bf16[4,2,256,256]{3,2,1,0:T(8,128)(2,1)}, u32[]{:S(2)}, u32[]{:S(2)}) collective-permute-start(bf16[4,2,256,256]{3,2,1,0:T(8,128)(2,1)} %get-tuple-element.88), channel_id=1, source_target_pairs={{0,2},{1,3},{2,10},{3,11},{4,18},{5,19},{6,26},{7,27},{8,0},{9,1},... | collective-permute-start | bytes 3145736 | tf_op jit(solution)/shard_map/ppermute | solution.py:352
  377.4 46.2 %collective-permute-start.35 = (bf16[4,2,256,256]{3,2,1,0:T(8,128)(2,1)}, bf16[4,2,256,256]{3,2,1,0:T(8,128)(2,1)S(1)}, u32[]{:S(2)}, u32[]{:S(2)}) collective-permute-start(bf16[4,2,256,256]{3,2,1,0:T(8,128)(2,1)} %get-tuple-element.84.refs_3_.refs_1_), channel_id=1, source_target_pairs={{0,1},{1,0},{2,3},{3,2},{4,5},{5,4},{6,7},{7,6},{8,9},{9,8},{10,11... | collective-permute-start | bytes 3145736 | tf_op jit(solution)/shard_map/ppermute | solution.py:355
  378.5 45.8 %collective-permute-start.36 = (bf16[4,2,256,256]{3,2,1,0:T(8,128)(2,1)}, bf16[4,2,256,256]{3,2,1,0:T(8,128)(2,1)S(1)}, u32[]{:S(2)}, u32[]{:S(2)}) collective-permute-start(bf16[4,2,256,256]{3,2,1,0:T(8,128)(2,1)} %get-tuple-element.89.refs_5_.refs_3_), channel_id=1, source_target_pairs={{0,1},{1,0},{2,3},{3,2},{4,5},{5,4},{6,7},{7,6},{8,9},{9,8},{10,11... | collective-permute-start | bytes 3145736 | tf_op jit(solution)/shard_map/ppermute | solution.py:355
  425.4 53.7 %collective-permute-start.40 = (bf16[4,2,256,256]{3,2,1,0:T(8,128)(2,1)}, bf16[4,2,256,256]{3,2,1,0:T(8,128)(2,1)S(1)}, u32[]{:S(2)}, u32[]{:S(2)}) collective-permute-start(bf16[4,2,256,256]{3,2,1,0:T(8,128)(2,1)} %get-tuple-element.95), channel_id=1, source_target_pairs={{0,4},{1,5},{2,12},{3,13},{4,20},{5,21},{6,28},{7,29},{8,6},{9,7},... | collective-permute-start | bytes 3145736 | tf_op jit(solution)/shard_map/ppermute | solution.py:352
  426.2 54.8 %collective-permute-start.41 = (bf16[4,2,256,256]{3,2,1,0:T(8,128)(2,1)}, bf16[4,2,256,256]{3,2,1,0:T(8,128)(2,1)S(1)}, u32[]{:S(2)}, u32[]{:S(2)}) collective-permute-start(bf16[4,2,256,256]{3,2,1,0:T(8,128)(2,1)} %get-tuple-element.95), channel_id=1, source_target_pairs={{0,16},{8,24},{16,0},{24,8},{1,17},{9,25},{17,1},{25,9},{2,18},{10... | collective-permute-start | bytes 3145736 | tf_op jit(solution)/shard_map/ppermute | solution.py:343
  427.9 33.0 %collective-permute-start.37 = (bf16[4,2,256,256]{3,2,1,0:T(8,128)(2,1)}, bf16[4,2,256,256]{3,2,1,0:T(8,128)(2,1)S(1)}, u32[]{:S(2)}, u32[]{:S(2)}) collective-permute-start(bf16[4,2,256,256]{3,2,1,0:T(8,128)(2,1)} %get-tuple-element.92.refs_4_.refs_2_), channel_id=1, source_target_pairs={{0,1},{1,0},{2,3},{3,2},{4,5},{5,4},{6,7},{7,6},{8,9},{9,8},{10,11... | collective-permute-start | bytes 3145736 | tf_op jit(solution)/shard_map/ppermute | solution.py:355
  428.1 46.1 %collective-permute-start.38 = (bf16[4,2,256,256]{3,2,1,0:T(8,128)(2,1)}, bf16[4,2,256,256]{3,2,1,0:T(8,128)(2,1)S(1)}, u32[]{:S(2)}, u32[]{:S(2)}) collective-permute-start(bf16[4,2,256,256]{3,2,1,0:T(8,128)(2,1)} %get-tuple-element.93.refs_6_.refs_4_), channel_id=1, source_target_pairs={{0,1},{1,0},{2,3},{3,2},{4,5},{5,4},{6,7},{7,6},{8,9},{9,8},{10,11... | collective-permute-start | bytes 3145736 | tf_op jit(solution)/shard_map/ppermute | solution.py:355
  429.3 49.7 %collective-permute-start.39 = (bf16[4,2,256,256]{3,2,1,0:T(8,128)(2,1)}, bf16[4,2,256,256]{3,2,1,0:T(8,128)(2,1)S(1)}, u32[]{:S(2)}, u32[]{:S(2)}) collective-permute-start(bf16[4,2,256,256]{3,2,1,0:T(8,128)(2,1)} %get-tuple-element.94.refs_4_), channel_id=1, source_target_pairs={{0,0},{1,1},{2,8},{3,9},{4,16},{5,17},{6,24},{7,25},{8,2},{9,3},{1... | collective-permute-start | bytes 3145736 | tf_op jit(solution)/shard_map/ppermute | solution.py:352
  460.8 26.1 %copy-start.25 = (bf16[4,2,256,256]{3,2,1,0:T(8,128)(2,1)S(1)}, bf16[4,2,256,256]{3,2,1,0:T(8,128)(2,1)}, u32[]{:S(2)}) copy-start(bf16[4,2,256,256]{3,2,1,0:T(8,128)(2,1)} %get-tuple-element.84.refs_3_.refs_1_) | copy-start | bytes 3145732
  460.8 18.2 %copy-start.80 = (bf16[4,2,256,256]{3,2,1,0:T(8,128)(2,1)}, bf16[4,2,256,256]{3,2,1,0:T(8,128)(2,1)S(1)}, u32[]{:S(2)}) copy-start(bf16[4,2,256,256]{3,2,1,0:T(8,128)(2,1)S(1)} %collective-permute-done.37.refs_8_.refs_4_.refs_6_) | copy-start | bytes 3145732
  481.9 49.3 %collective-permute-start.43 = (bf16[4,2,256,256]{3,2,1,0:T(8,128)(2,1)}, bf16[4,2,256,256]{3,2,1,0:T(8,128)(2,1)S(1)}, u32[]{:S(2)}, u32[]{:S(2)}) collective-permute-start(bf16[4,2,256,256]{3,2,1,0:T(8,128)(2,1)} %get-tuple-element.97), channel_id=1, source_target_pairs={{0,6},{1,7},{2,14},{3,15},{4,22},{5,23},{6,30},{7,31},{8,4},{9,5},... | collective-permute-start | bytes 3145736 | tf_op jit(solution)/shard_map/ppermute | solution.py:352
  481.9 52.0 %collective-permute-start.46 = (bf16[4,2,256,256]{3,2,1,0:T(8,128)(2,1)}, bf16[4,2,256,256]{3,2,1,0:T(8,128)(2,1)S(1)}, u32[]{:S(2)}, u32[]{:S(2)}) collective-permute-start(bf16[4,2,256,256]{3,2,1,0:T(8,128)(2,1)} %get-tuple-element.97), channel_id=1, source_target_pairs={{0,24},{8,16},{16,8},{24,0},{1,25},{9,17},{17,9},{25,1},{2,26},{10... | collective-permute-start | bytes 3145736 | tf_op jit(solution)/shard_map/ppermute | solution.py:343
  483.7 47.6 %collective-permute-start.42 = (bf16[4,2,256,256]{3,2,1,0:T(8,128)(2,1)}, bf16[4,2,256,256]{3,2,1,0:T(8,128)(2,1)S(1)}, u32[]{:S(2)}, u32[]{:S(2)}) collective-permute-start(bf16[4,2,256,256]{3,2,1,0:T(8,128)(2,1)} %get-tuple-element.96.refs_2_), channel_id=1, source_target_pairs={{0,2},{1,3},{2,10},{3,11},{4,18},{5,19},{6,26},{7,27},{8,0},{9,1},... | collective-permute-start | bytes 3145736 | tf_op jit(solution)/shard_map/ppermute | solution.py:352
  485.4 45.8 %collective-permute-start.44 = (bf16[4,2,256,256]{3,2,1,0:T(8,128)(2,1)}, bf16[4,2,256,256]{3,2,1,0:T(8,128)(2,1)S(1)}, u32[]{:S(2)}, u32[]{:S(2)}) collective-permute-start(bf16[4,2,256,256]{3,2,1,0:T(8,128)(2,1)} %get-tuple-element.98.refs_15_), channel_id=1, source_target_pairs={{0,1},{1,0},{2,3},{3,2},{4,5},{5,4},{6,7},{7,6},{8,9},{9,8},{10,11... | collective-permute-start | bytes 3145736 | tf_op jit(solution)/shard_map/ppermute | solution.py:355
  485.6 46.6 %collective-permute-start.45 = (bf16[4,2,256,256]{3,2,1,0:T(8,128)(2,1)}, bf16[4,2,256,256]{3,2,1,0:T(8,128)(2,1)S(1)}, u32[]{:S(2)}, u32[]{:S(2)}) collective-permute-start(bf16[4,2,256,256]{3,2,1,0:T(8,128)(2,1)} %get-tuple-element.99.refs_17_), channel_id=1, source_target_pairs={{0,1},{1,0},{2,3},{3,2},{4,5},{5,4},{6,7},{7,6},{8,9},{9,8},{10,11... | collective-permute-start | bytes 3145736 | tf_op jit(solution)/shard_map/ppermute | solution.py:355
  534.9 3.3 collective-permute-start.47
  536.1 51.9 %collective-permute-start.48 = (bf16[4,2,256,256]{3,2,1,0:T(8,128)(2,1)}, bf16[4,2,256,256]{3,2,1,0:T(8,128)(2,1)S(1)}, u32[]{:S(2)}, u32[]{:S(2)}) collective-permute-start(bf16[4,2,256,256]{3,2,1,0:T(8,128)(2,1)} %get-tuple-element.101.refs_16_), channel_id=1, source_target_pairs={{0,1},{1,0},{2,3},{3,2},{4,5},{5,4},{6,7},{7,6},{8,9},{9,8},{10,11... | collective-permute-start | bytes 3145736 | tf_op jit(solution)/shard_map/ppermute | solution.py:355
  536.4 20.1 %copy-start.3 = (bf16[4,256,2048]{2,1,0:T(8,128)(2,1)S(1)}, bf16[4,256,2048]{2,1,0:T(8,128)(2,1)}, u32[]{:S(2)}) copy-start(bf16[4,256,2048]{2,1,0:T(8,128)(2,1)} %copy-done.1) | copy-start | bytes 12582916
  536.4 20.1 %copy-start.6 = (bf16[4,256,2048]{2,1,0:T(8,128)(2,1)S(1)}, bf16[4,256,2048]{2,1,0:T(8,128)(2,1)}, u32[]{:S(2)}) copy-start(bf16[4,256,2048]{2,1,0:T(8,128)(2,1)} %copy-done.5) | copy-start | bytes 12582916
  536.4 51.7 %collective-permute-start.49 = (bf16[4,2,256,256]{3,2,1,0:T(8,128)(2,1)}, bf16[4,2,256,256]{3,2,1,0:T(8,128)(2,1)}, u32[]{:S(2)}, u32[]{:S(2)}) collective-permute-start(bf16[4,2,256,256]{3,2,1,0:T(8,128)(2,1)} %get-tuple-element.102.refs_18_), channel_id=1, source_target_pairs={{0,1},{1,0},{2,3},{3,2},{4,5},{5,4},{6,7},{7,6},{8,9},{9,8},{10,11... | collective-permute-start | bytes 3145736 | tf_op jit(solution)/shard_map/ppermute | solution.py:355
  540.1 16.4 %copy-start.75 = (bf16[4,2,256,256]{3,2,1,0:T(8,128)(2,1)S(1)}, bf16[4,2,256,256]{3,2,1,0:T(8,128)(2,1)}, u32[]{:S(2)}) copy-start(bf16[4,2,256,256]{3,2,1,0:T(8,128)(2,1)} %get-tuple-element.102.refs_18_) | copy-start | bytes 3145732
  540.1 16.4 %copy-start.77 = (bf16[4,2,256,256]{3,2,1,0:T(8,128)(2,1)S(1)}, bf16[4,2,256,256]{3,2,1,0:T(8,128)(2,1)}, u32[]{:S(2)}) copy-start(bf16[4,2,256,256]{3,2,1,0:T(8,128)(2,1)} %get-tuple-element.101.refs_16_) | copy-start | bytes 3145732
  540.1 16.4 %copy-start.85 = (bf16[4,2,256,256]{3,2,1,0:T(8,128)(2,1)S(1)}, bf16[4,2,256,256]{3,2,1,0:T(8,128)(2,1)}, u32[]{:S(2)}) copy-start(bf16[4,2,256,256]{3,2,1,0:T(8,128)(2,1)} %get-tuple-element.99.refs_17_) | copy-start | bytes 3145732
  540.1 16.4 %copy-start.88 = (bf16[4,2,256,256]{3,2,1,0:T(8,128)(2,1)S(1)}, bf16[4,2,256,256]{3,2,1,0:T(8,128)(2,1)}, u32[]{:S(2)}) copy-start(bf16[4,2,256,256]{3,2,1,0:T(8,128)(2,1)} %get-tuple-element.98.refs_15_) | copy-start | bytes 3145732
  556.5 15.0 %copy-start.12 = (bf16[8,4,256,256]{3,2,1,0:T(8,128)(2,1)S(1)}, bf16[8,4,256,256]{3,2,1,0:T(8,128)(2,1)}, u32[]{:S(2)}) copy-start(bf16[8,4,256,256]{3,2,1,0:T(8,128)(2,1)} %copy-done.11) | copy-start | bytes 12582916
  571.5 16.5 %copy-start.67 = (bf16[4,2,256,256]{3,2,1,0:T(8,128)(2,1)S(1)}, bf16[4,2,256,256]{3,2,1,0:T(8,128)(2,1)}, u32[]{:S(2)}) copy-start(bf16[4,2,256,256]{3,2,1,0:T(8,128)(2,1)} %copy-done.66) | copy-start | bytes 3145732
  571.5 16.5 %copy-start.69 = (bf16[4,2,256,256]{3,2,1,0:T(8,128)(2,1)S(1)}, bf16[4,2,256,256]{3,2,1,0:T(8,128)(2,1)}, u32[]{:S(2)}) copy-start(bf16[4,2,256,256]{3,2,1,0:T(8,128)(2,1)} %copy-done.68) | copy-start | bytes 3145732
  (90 other events, 347.6 us)

commit v4 on v3

--- a/solution.py
+++ b/solution.py
@@ -377,7 +377,7 @@
     plan = [[] for _ in range(len(steps) + 1)]
     for h in chunks:
         for s in range(1, groups):
-            at = 2 * h + s % 2 if s > 1 else h * len(steps)
+            at = 2 * h + s % 2 if s > 1 else h * len(steps) if rider is not None or h else 1
             plan[min(at, len(steps))].append((h, s))
     earlier, before = [], []
     for t in range(len(steps) + 1):
@@ -483,16 +483,21 @@
         )
 
     chosen = ((rows // cols) ^ my_half) * len(chunks) + (rows % cols) // width
-    in_order = jnp.arange(groups * CAP, dtype=I32)
 
     def listed_rows(h, c):
-        return [
-            *finish(
-                wpj, [c], in_order, [h], integrals, tall, wide, eps_occ, where, rows, chosen,
+        ready = [None] * groups
+        for side in [[*range(p, groups, 2)] for p in range(2)] if h == 0 else [[*range(groups)]]:
+            which = jnp.asarray([s * CAP + n for s in side for n in range(CAP)], I32)
+            some = finish(
+                wpj, [c], which, [h], integrals, tall, wide, eps_occ, where,
+                jnp.concatenate([rows[s * CAP : (s + 1) * CAP] for s in side]),
+                jnp.concatenate([chosen[s * CAP : (s + 1) * CAP] for s in side]),
                 [piece for half in far_now for piece in half],
-                [jax.ShapeDtypeStruct((width, CAP, v, v), BF16)] * groups,
+                [jax.ShapeDtypeStruct((width, CAP, v, v), BF16)] * len(side),
             )
-        ]
+            for s, x in zip(side, some):
+                ready[s] = x
+        return ready
 
     for sweep in range(ITERS - 1):
         c = [made["c", h] if sweep == 0 else direct(made["wp"], rows, near[h]) for h in chunks]
@@ -515,8 +520,8 @@
         def middle(t, earlier):
             if t == 1:
                 if wpj[1] is None:
-                    [arrived] = tie([second_came], earlier)
-                    wpj[1] = deliver(1, second, arrived)
+                    arrived, held_rows = tie([second_came, second], earlier + mine[0][1::2])
+                    wpj[1] = deliver(1, held_rows, arrived)
                 mine[1][:] = listed_rows(1, c[1])
                 return mine[1]
             if t == 0 or not final:

time: 606 us -> 613 us (1.012)
  waiting for transfers between devices: 237 us -> 214 us
  local copies, waits for them, and re-layouts: 72.9 us -> 91.6 us
    ppermute x12, waiting for transfers between devices: 37.7 us -> 10.8 us  [near(): return lax.ppermute(x, 'igrp', [(i, i ^ s) for i in range(self.groups)])]
    unnamed x210 -> x224, local copies, waits for them, and re-layouts: 65.3 us -> 83.6 us
    ppermute x16, waiting for transfers between devices: 155 us -> 163 us  [route(): return lax.ppermute(x, AXES, pairs)]
    pallas_call x6 -> x7, Pallas kernels: 98.8 us -> 103 us  [finish(): pl.pallas_call(functools.partial(finish_kernel if into is None else kept_...]
  transfers between devices with their start and end apart: 50 -> 50, of which waited for: 24 -> 22; matrix products, arithmetic and copies ran while one was open for 2% -> 3% of each run, Pallas kernels for 33% -> 33%
where the time goes in v4:
time: 613 us; the launch traced here: 609 us
  Pallas kernels  220 us (36%)
  waiting for transfers between devices  214 us (35%)
  local copies, waits for them, and re-layouts  91.6 us (15%)
  starting transfers between devices  78.3 us (13%)
    ppermute x16, waiting for transfers between devices, route(): return lax.ppermute(x, AXES, pairs)  163 us
    pallas_call x7, Pallas kernels, finish(): pl.pallas_call(functools.partial(finish_kernel if into is None else kept_...  103 us
    unnamed x224, local copies, waits for them, and re-layouts  83.6 us
    pallas_call x4, Pallas kernels, direct(): pl.pallas_call(functools.partial(direct_kernel, taken), out_shape=jax.Sha...  64.9 us
    ppermute x16, waiting for transfers between devices, swap(): return lax.ppermute(x, 'jgrp', [(j, j ^ d) for j in range(self.jgroups)])  36.2 us
    ppermute x16, starting transfers between devices, route(): return lax.ppermute(x, AXES, pairs)  29.3 us
    pallas_call x3, Pallas kernels, slotted(): pl.pallas_call(slotted_kernel, out_shape=jax.ShapeDtypeStruct((rows, v, d...  29.2 us
    ppermute x12, starting transfers between devices, near(): return lax.ppermute(x, 'igrp', [(i, i ^ s) for i in range(self.groups)])  25.4 us
  transfers between devices with their start and end apart: 50, of which 22 were waited for; matrix products, arithmetic and copies ran while one was open for 3% of the time, Pallas kernels for 33%

profile of v4, /device:TPU:21, one launch (start us, length us, event | category | flops | bytes accessed | tf_op | source)
XLA Modules:
  0.0 608.9 jit_solution(3593512093193516104)
XLA Ops:
  2.1 4.1 pick_rows.3
  7.1 3.7 collective-permute-start.1
  12.1 1.8 collective-permute-start.4
  14.2 18.4 %slotted.3.refs_6_.refs_0_.refs_1_.refs_2_.refs_3_ = bf16[16,256,2048]{2,1,0:T(8,128)(2,1)} custom-call(s32[128]{0:T(128)S(1)} %reshape.662.slots_ref, s32[1]{0:T(128)} %constant.140.clone.1.pick_ref, bf16[16,8,256,256]{3,2,1,0:T(8,128)(2,1)} %refs_0_.5), custom_call_target="tpu_custom_call" | custom-call | bytes 33554432 | tf_op jit(solution)/shard_map/slotted/pallas_call | solution.py:114
  32.6 25.1 %collective-permute-done.1.refs_2_ = bf16[4,2,256,256]{3,2,1,0:T(8,128)(2,1)S(1)} collective-permute-done((bf16[4,2,256,256]{3,2,1,0:T(8,128)(2,1)}, bf16[4,2,256,256]{3,2,1,0:T(8,128)(2,1)S(1)}, u32[]{:S(2)}, u32[]{:S(2)}) %collective-permute-start.1) | collective-permute-done | bytes 1048608 | tf_op jit(solution)/shard_map/ppermute | solution.py:352
  60.3 2.1 collective-permute-start.5
  63.9 2.4 collective-permute-start.9
  66.3 3.1 pick_rows.2
  73.3 35.4 %collective-permute-done.5.refs_2_ = bf16[4,2,256,256]{3,2,1,0:T(8,128)(2,1)S(1)} collective-permute-done((bf16[4,2,256,256]{3,2,1,0:T(8,128)(2,1)}, bf16[4,2,256,256]{3,2,1,0:T(8,128)(2,1)S(1)}, u32[]{:S(2)}, u32[]{:S(2)}) %collective-permute-start.5) | collective-permute-done | bytes 1048608 | tf_op jit(solution)/shard_map/ppermute | solution.py:352
  112.1 4.1 collective-permute-start.10
  121.0 13.8 %direct.4.refs_7_.refs_1_ = bf16[8,4,256,256]{3,2,1,0:T(8,128)(2,1)S(1)} custom-call(s32[8]{0:T(128)S(1)} %reshape.661.rows_ref, bf16[16,256,2048]{2,1,0:T(8,128)(2,1)} %slotted.3.refs_6_.refs_0_.refs_1_.refs_2_.refs_3_, bf16[16,256,2048]{2,1,0:T(8,128)(2,1)} %slotted.3.refs_6_.refs_0_.refs_1_.refs_2_.refs_3_, ...), custom_call_target="tpu_custom_call" | custom-call | flops 8589934592 | bytes 12582912 | tf_op jit(solution)/shard_map/direct/pallas_call | solution.py:155
  134.9 2.0 copy-done.8
  136.9 25.9 %collective-permute-done.10.refs_2_ = bf16[4,2,256,256]{3,2,1,0:T(8,128)(2,1)S(1)} collective-permute-done((bf16[4,2,256,256]{3,2,1,0:T(8,128)(2,1)}, bf16[4,2,256,256]{3,2,1,0:T(8,128)(2,1)S(1)}, u32[]{:S(2)}, u32[]{:S(2)}) %collective-permute-start.10) | collective-permute-done | bytes 1048608 | tf_op jit(solution)/shard_map/ppermute | solution.py:352
  165.8 2.9 collective-permute-start.15
  171.6 6.2 %constant_dynamic-slice_fusion.1 = (bf16[4,8,256,256]{3,2,1,0:T(8,128)(2,1)}, bf16[4,8,256,256]{3,2,1,0:T(8,128)(2,1)S(1)}) fusion(bf16[16,8,256,256]{3,2,1,0:T(8,128)(2,1)} %refs_0_.5, s32[]{:T(128)S(6)} %select_n.219, s32[]{:T(128)S(6)} %select_n.216), kind=kLoop, calls=%fused_computation.59 | loop fusion | bytes 16777224 | tf_op jit(solution)/shard_map/dynamic_slice | solution.py:472
  177.9 2.0 copy.98.refs_3_
  181.2 31.9 %collective-permute-done.15.refs_0_ = bf16[4,2,256,256]{3,2,1,0:T(8,128)(2,1)S(1)} collective-permute-done((bf16[4,2,256,256]{3,2,1,0:T(8,128)(2,1)}, bf16[4,2,256,256]{3,2,1,0:T(8,128)(2,1)S(1)}, u32[]{:S(2)}, u32[]{:S(2)}) %collective-permute-start.15) | collective-permute-done | bytes 1048608 | tf_op jit(solution)/shard_map/ppermute | solution.py:352
  213.1 3.3 collective-permute-done.16.refs_1_
  220.3 2.6 collective-permute-start
  225.4 13.5 %direct.5.refs_5_.refs_1_ = bf16[8,4,256,256]{3,2,1,0:T(8,128)(2,1)S(1)} custom-call(s32[8]{0:T(128)S(1)} %reshape.661.rows_ref, bf16[16,256,2048]{2,1,0:T(8,128)(2,1)} %slotted.3.refs_6_.refs_0_.refs_1_.refs_2_.refs_3_, bf16[16,256,2048]{2,1,0:T(8,128)(2,1)} %slotted.3.refs_6_.refs_0_.refs_1_.refs_2_.refs_3_, ...), custom_call_target="tpu_custom_call" | custom-call | flops 8589934592 | bytes 12582912 | tf_op jit(solution)/shard_map/direct/pallas_call | solution.py:155
  238.9 2.0 copy-done.11
  240.9 2.4 collective-permute-done.21.refs_2_.refs_16_
  243.4 22.5 %collective-permute-done.22.refs_3_.refs_18_ = bf16[4,2,256,256]{3,2,1,0:T(8,128)(2,1)S(1)} collective-permute-done((bf16[4,2,256,256]{3,2,1,0:T(8,128)(2,1)}, bf16[4,2,256,256]{3,2,1,0:T(8,128)(2,1)S(1)}, u32[]{:S(2)}, u32[]{:S(2)}) %collective-permute-start.22) | collective-permute-done | bytes 1048608 | tf_op jit(solution)/shard_map/ppermute | solution.py:355
  265.9 2.1 copy-done.107
  269.7 2.6 collective-permute-start.30
  274.1 4.0 collective-permute-done.24.refs_3_
  278.1 2.2 copy-done.10
  280.4 5.4 slotted.4.refs_0_.refs_9_
  285.8 1.9 copy-done.1
  287.9 11.7 %finish.7 = (bf16[4,2,256,256]{3,2,1,0:T(8,128)(2,1)}, bf16[4,2,256,256]{3,2,1,0:T(8,128)(2,1)}) custom-call(s32[4]{0:T(128)S(1)} %get-tuple-element.144.rows_ref, s32[4]{0:T(128)S(1)} %copy-done.106, s32[4]{0:T(128)S(1)} %pad_add_fusion.where_ref.refs_2_, s32[16]{0:T(128)S(1)} %select_n.227.held_ref, s32[4]{0:T(128)S(1)} %get-tuple-element.145.use_ref, ...), custom_call_target="tpu_custom_call" | custom-call | flops 4294967296 | bytes 14680064 | tf_op jit(solution)/shard_map/finish/pallas_call | solution.py:264
  299.6 3.8 collective-permute-start.25
  317.1 10.7 %finish.8 = (bf16[4,2,256,256]{3,2,1,0:T(8,128)(2,1)S(1)}, bf16[4,2,256,256]{3,2,1,0:T(8,128)(2,1)S(1)}) custom-call(s32[4]{0:T(128)S(1)} %get-tuple-element.122.rows_ref, s32[4]{0:T(128)S(1)} %copy-done.105, s32[4]{0:T(128)S(1)} %pad_add_fusion.where_ref.refs_2_, s32[16]{0:T(128)S(1)} %select_n.231.held_ref, s32[4]{0:T(128)S(1)} %get-tuple-element.146.use_ref, ...), custom_call_target="tpu_custom_call" | custom-call | flops 4294967296 | bytes 14680064 | tf_op jit(solution)/shard_map/finish/pallas_call | solution.py:264
  329.8 20.0 %collective-permute-done.25.refs_2_ = bf16[4,2,256,256]{3,2,1,0:T(8,128)(2,1)} collective-permute-done((bf16[4,2,256,256]{3,2,1,0:T(8,128)(2,1)}, bf16[4,2,256,256]{3,2,1,0:T(8,128)(2,1)}, u32[]{:S(2)}, u32[]{:S(2)}) %collective-permute-start.25) | collective-permute-done | bytes 1048608 | tf_op jit(solution)/shard_map/ppermute | solution.py:352
  349.8 2.3 copy.103.refs_2_
  352.0 2.3 copy.104.refs_3_
  354.3 2.8 collective-permute-start.31
  358.5 16.5 %collective-permute-start.28 = (bf16[4,2,256,256]{3,2,1,0:T(8,128)(2,1)}, bf16[4,2,256,256]{3,2,1,0:T(8,128)(2,1)}, u32[]{:S(2)}, u32[]{:S(2)}) collective-permute-start(bf16[4,2,256,256]{3,2,1,0:T(8,128)(2,1)} %get-tuple-element.85.refs_5_), channel_id=1, source_target_pairs={{0,8},{8,0},{16,24},{24,16},{1,9},{9,1},{17,25},{25,17},{2,10},{10... | collective-permute-start | bytes 3145736 | tf_op jit(solution)/shard_map/ppermute | solution.py:343
  376.0 2.9 collective-permute-start.33
  379.0 2.3 collective-permute-done.28.refs_5_.refs_6_
  383.4 2.2 copy-done.7
  385.7 5.4 slotted.5.refs_0_.refs_10_
  391.0 2.0 copy-done.5
  393.1 19.0 %finish.9 = (bf16[4,2,256,256]{3,2,1,0:T(8,128)(2,1)S(1)}, bf16[4,2,256,256]{3,2,1,0:T(8,128)(2,1)S(1)}, bf16[4,2,256,256]{3,2,1,0:T(8,128)(2,1)S(1)}, bf16[4,2,256,256]{3,2,1,0:T(8,128)(2,1)S(1)}) custom-call(s32[8]{0:T(128)S(1)} %get-tuple-element.118.rows_ref, s32[8]{0:T(128)S(1)} %call_exported.0.crows_ref, s32[4]{0:T(128)S(1)} %get-tuple-element.125.where_ref, ...), custom_call_target="tpu_custom_call" | custom-call | flops 8589934592 | bytes 25165824 | tf_op jit(solution)/shard_map/finish/pallas_call | solution.py:264
  415.9 7.6 %collective-permute-done.29.refs_7_ = bf16[4,2,256,256]{3,2,1,0:T(8,128)(2,1)} collective-permute-done((bf16[4,2,256,256]{3,2,1,0:T(8,128)(2,1)}, bf16[4,2,256,256]{3,2,1,0:T(8,128)(2,1)}, u32[]{:S(2)}, u32[]{:S(2)}) %collective-permute-start.29) | collective-permute-done | bytes 1048608 | tf_op jit(solution)/shard_map/ppermute | solution.py:343
  424.0 4.5 collective-permute-done.34.refs_3_
  428.6 1.6 collective-permute-start.40
  432.1 4.1 collective-permute-start.39
  436.2 24.6 %direct.6.refs_1_.refs_7_.refs_11_ = bf16[16,4,256,256]{3,2,1,0:T(8,128)(2,1)S(1)} custom-call(s32[16]{0:T(128)S(1)} %iota.174.rows_ref, bf16[16,256,2048]{2,1,0:T(8,128)(2,1)} %slotted.3.refs_6_.refs_0_.refs_1_.refs_2_.refs_3_, bf16[16,256,2048]{2,1,0:T(8,128)(2,1)} %slotted.3.refs_6_.refs_0_.refs_1_.refs_2_.refs_3_, ...), custom_call_target="tpu_custom_call" | custom-call | flops 17179869184 | bytes 25165824 | tf_op jit(solution)/shard_map/direct/pallas_call | solution.py:155
  460.9 3.3 copy-done
  464.2 11.1 %collective-permute-done.38.refs_10_.refs_5_.refs_8_ = bf16[4,2,256,256]{3,2,1,0:T(8,128)(2,1)S(1)} collective-permute-done((bf16[4,2,256,256]{3,2,1,0:T(8,128)(2,1)}, bf16[4,2,256,256]{3,2,1,0:T(8,128)(2,1)S(1)}, u32[]{:S(2)}, u32[]{:S(2)}) %collective-permute-start.38) | collective-permute-done | bytes 1048608 | tf_op jit(solution)/shard_map/ppermute | solution.py:355
  475.3 7.7 %collective-permute-done.39.refs_2_ = bf16[4,2,256,256]{3,2,1,0:T(8,128)(2,1)S(1)} collective-permute-done((bf16[4,2,256,256]{3,2,1,0:T(8,128)(2,1)}, bf16[4,2,256,256]{3,2,1,0:T(8,128)(2,1)S(1)}, u32[]{:S(2)}, u32[]{:S(2)}) %collective-permute-start.39) | collective-permute-done | bytes 1048608 | tf_op jit(solution)/shard_map/ppermute | solution.py:352
  485.9 1.6 collective-permute-start.46
  487.5 1.7 collective-permute-start.42
  490.7 2.2 copy-done.2
  496.5 16.5 %finish.10.refs_7_.refs_8_ = f32[16,8,256,256]{3,2,1,0:T(8,128)} custom-call(s32[8]{0:T(128)S(1)} %get-tuple-element.124.rows_ref.crows_ref, s32[8]{0:T(128)S(1)} %get-tuple-element.124.rows_ref.crows_ref, s32[4]{0:T(128)S(1)} %pad_add_fusion.where_ref.refs_2_, s32[16]{0:T(128)S(1)} %select_n.213.held_ref, s32[8]{0:T(128)S(1)} %eq.224.use_ref, ...), custom_call_target="tpu_custom_call" | custom-call | flops 8589934592 | bytes 25165824 | tf_op jit(solution)/shard_map/finish/pallas_call | solution.py:264
  513.1 15.0 %finish.11.refs_6_.refs_8_ = bf16[8,4,256,256]{3,2,1,0:T(8,128)(2,1)S(1)} custom-call(s32[8]{0:T(128)S(1)} %get-tuple-element.124.rows_ref.crows_ref, s32[8]{0:T(128)S(1)} %get-tuple-element.124.rows_ref.crows_ref, s32[4]{0:T(128)S(1)} %get-tuple-element.125.where_ref, s32[16]{0:T(128)S(1)} %select_n.213.held_ref, s32[8]{0:T(128)S(1)} %eq.224.use_ref, ...), custom_call_target="tpu_custom_call" | custom-call | flops 8589934592 | bytes 25165824 | tf_op jit(solution)/shard_map/finish/pallas_call | solution.py:264
  528.0 2.1 copy-done.57
  530.1 5.7 collective-permute-done.42.refs_0_
  542.3 1.6 copy-done.60
  543.9 12.9 %direct.7.refs_12_ = bf16[16,4,256,256]{3,2,1,0:T(8,128)(2,1)S(1)} custom-call(s32[8]{0:T(128)S(1)} %pad_add_fusion.9.rows_ref, bf16[16,256,2048]{2,1,0:T(8,128)(2,1)} %slotted.3.refs_6_.refs_0_.refs_1_.refs_2_.refs_3_, bf16[16,256,2048]{2,1,0:T(8,128)(2,1)} %slotted.3.refs_6_.refs_0_.refs_1_.refs_2_.refs_3_, ...), custom_call_target="tpu_custom_call" | custom-call | flops 8589934592 | bytes 12582912 | tf_op jit(solution)/shard_map/direct/pallas_call | solution.py:155
  556.8 3.2 copy-done.4
  562.5 14.9 %finish.12.into_ref = f32[16,8,256,256]{3,2,1,0:T(8,128)} custom-call(s32[4]{0:T(128)S(1)} %iota_add_fusion.1.refs_0_.refs_1_, s32[4]{0:T(128)S(1)} %iota_add_fusion.1.refs_0_.refs_1_, s32[4]{0:T(128)S(1)} %pad_add_fusion.where_ref.refs_2_, s32[4]{0:T(128)S(1)} %get-tuple-element.115.refs_3_, ...), custom_call_target="tpu_custom_call", output_to_operand_aliasing={{}: (8, {})} | custom-call | flops 8589934592 | bytes 29360128 | tf_op jit(solution)/shard_map/finish/pallas_call | solution.py:264
  577.5 16.5 %joined.1.refs_8_ = f32[16,8,256,256]{3,2,1,0:T(8,128)} custom-call(s32[8]{0:T(128)S(1)} %get-tuple-element.124.rows_ref.crows_ref, s32[4]{0:T(128)S(1)} %get-tuple-element.125.where_ref, f32[64]{0:T(128)S(1)} %copy-done.104, f32[256,1]{1,0:T(8,128)S(1)} %copy.82.tall_ref.refs_6_, f32[1,256]{1,0:T(1,128)S(1)} %bitcast.14, ...), custom_call_target="tpu_custom_call", output_to_operand_aliasing={{}: (5, {})} | custom-call | flops 8589934592 | bytes 25165824 | tf_op jit(solution)/shard_map/joined/pallas_call | solution.py:315
  594.0 14.9 %finish.13 = f32[16,8,256,256]{3,2,1,0:T(8,128)} custom-call(s32[4]{0:T(128)S(1)} %iota_add_fusion.4.refs_0_.refs_1_, s32[4]{0:T(128)S(1)} %iota_add_fusion.4.refs_0_.refs_1_, s32[4]{0:T(128)S(1)} %pad_add_fusion.where_ref.refs_2_, s32[4]{0:T(128)S(1)} %get-tuple-element.116.refs_3_, s32[4]{0:T(128)S(1)} %broadcast.544.refs_4_, ...), custom_call_target="tpu_custom_call", output_to_operand_aliasing={{}: (8, {})} | custom-call | flops 8589934592 | bytes 29360128 | tf_op jit(solution)/shard_map/finish/pallas_call | solution.py:264
  (355 shorter events, 81.5 us)
Async XLA Ops:
  7.1 50.6 %collective-permute-start.1 = (bf16[4,2,256,256]{3,2,1,0:T(8,128)(2,1)}, bf16[4,2,256,256]{3,2,1,0:T(8,128)(2,1)S(1)}, u32[]{:S(2)}, u32[]{:S(2)}) collective-permute-start(bf16[4,2,256,256]{3,2,1,0:T(8,128)(2,1)} %get-tuple-element.62.refs_4_), channel_id=1, source_target_pairs={{0,0},{1,1},{2,8},{3,9},{4,16},{5,17},{6,24},{7,25},{8,2},{9,3},{1... | collective-permute-start | bytes 3145736 | tf_op jit(solution)/shard_map/ppermute | solution.py:352
  10.9 48.1 %collective-permute-start.2 = (bf16[4,2,256,256]{3,2,1,0:T(8,128)(2,1)}, bf16[4,2,256,256]{3,2,1,0:T(8,128)(2,1)S(1)}, u32[]{:S(2)}, u32[]{:S(2)}) collective-permute-start(bf16[4,2,256,256]{3,2,1,0:T(8,128)(2,1)} %get-tuple-element.63), channel_id=1, source_target_pairs={{0,4},{1,5},{2,12},{3,13},{4,20},{5,21},{6,28},{7,29},{8,6},{9,7},... | collective-permute-start | bytes 3145736 | tf_op jit(solution)/shard_map/ppermute | solution.py:352
  12.1 46.9 %collective-permute-start.3 = (bf16[4,2,256,256]{3,2,1,0:T(8,128)(2,1)}, bf16[4,2,256,256]{3,2,1,0:T(8,128)(2,1)S(1)}, u32[]{:S(2)}, u32[]{:S(2)}) collective-permute-start(bf16[4,2,256,256]{3,2,1,0:T(8,128)(2,1)} %get-tuple-element.60.refs_0_), channel_id=1, source_target_pairs={{0,8},{8,0},{16,24},{24,16},{1,9},{9,1},{17,25},{25,17},{2,10},{10... | collective-permute-start | bytes 3145736 | tf_op jit(solution)/shard_map/ppermute | solution.py:343
  12.1 46.9 %collective-permute-start.4 = (bf16[4,2,256,256]{3,2,1,0:T(8,128)(2,1)}, bf16[4,2,256,256]{3,2,1,0:T(8,128)(2,1)}, u32[]{:S(2)}, u32[]{:S(2)}) collective-permute-start(bf16[4,2,256,256]{3,2,1,0:T(8,128)(2,1)} %get-tuple-element.63), channel_id=1, source_target_pairs={{0,16},{8,24},{16,0},{24,8},{1,17},{9,25},{17,1},{25,9},{2,18},{10... | collective-permute-start | bytes 3145736 | tf_op jit(solution)/shard_map/ppermute | solution.py:343
  60.3 48.3 %collective-permute-start.5 = (bf16[4,2,256,256]{3,2,1,0:T(8,128)(2,1)}, bf16[4,2,256,256]{3,2,1,0:T(8,128)(2,1)S(1)}, u32[]{:S(2)}, u32[]{:S(2)}) collective-permute-start(bf16[4,2,256,256]{3,2,1,0:T(8,128)(2,1)} %get-tuple-element.64), channel_id=1, source_target_pairs={{0,2},{1,3},{2,10},{3,11},{4,18},{5,19},{6,26},{7,27},{8,0},{9,1},... | collective-permute-start | bytes 3145736 | tf_op jit(solution)/shard_map/ppermute | solution.py:352
  62.4 47.4 %collective-permute-start.6 = (bf16[4,2,256,256]{3,2,1,0:T(8,128)(2,1)}, bf16[4,2,256,256]{3,2,1,0:T(8,128)(2,1)S(1)}, u32[]{:S(2)}, u32[]{:S(2)}) collective-permute-start(bf16[4,2,256,256]{3,2,1,0:T(8,128)(2,1)} %get-tuple-element.65), channel_id=1, source_target_pairs={{0,6},{1,7},{2,14},{3,15},{4,22},{5,23},{6,30},{7,31},{8,4},{9,5},... | collective-permute-start | bytes 3145736 | tf_op jit(solution)/shard_map/ppermute | solution.py:352
  62.5 47.4 %collective-permute-start.7 = (bf16[4,2,256,256]{3,2,1,0:T(8,128)(2,1)}, bf16[4,2,256,256]{3,2,1,0:T(8,128)(2,1)S(1)}, u32[]{:S(2)}, u32[]{:S(2)}) collective-permute-start(bf16[4,2,256,256]{3,2,1,0:T(8,128)(2,1)} %get-tuple-element.66.refs_3_), channel_id=1, source_target_pairs={{0,1},{1,0},{2,3},{3,2},{4,5},{5,4},{6,7},{7,6},{8,9},{9,8},{10,11... | collective-permute-start | bytes 3145736 | tf_op jit(solution)/shard_map/ppermute | solution.py:355
  62.7 47.1 %collective-permute-start.8 = (bf16[4,2,256,256]{3,2,1,0:T(8,128)(2,1)}, bf16[4,2,256,256]{3,2,1,0:T(8,128)(2,1)S(1)}, u32[]{:S(2)}, u32[]{:S(2)}) collective-permute-start(bf16[4,2,256,256]{3,2,1,0:T(8,128)(2,1)} %get-tuple-element.67.refs_5_), channel_id=1, source_target_pairs={{0,1},{1,0},{2,3},{3,2},{4,5},{5,4},{6,7},{7,6},{8,9},{9,8},{10,11... | collective-permute-start | bytes 3145736 | tf_op jit(solution)/shard_map/ppermute | solution.py:355
  63.9 46.9 %collective-permute-start.9 = (bf16[4,2,256,256]{3,2,1,0:T(8,128)(2,1)}, bf16[4,2,256,256]{3,2,1,0:T(8,128)(2,1)S(1)}, u32[]{:S(2)}, u32[]{:S(2)}) collective-permute-start(bf16[4,2,256,256]{3,2,1,0:T(8,128)(2,1)} %get-tuple-element.65), channel_id=1, source_target_pairs={{0,24},{8,16},{16,8},{24,0},{1,25},{9,17},{17,9},{25,1},{2,26},{10... | collective-permute-start | bytes 3145736 | tf_op jit(solution)/shard_map/ppermute | solution.py:343
  112.1 50.6 %collective-permute-start.10 = (bf16[4,2,256,256]{3,2,1,0:T(8,128)(2,1)}, bf16[4,2,256,256]{3,2,1,0:T(8,128)(2,1)S(1)}, u32[]{:S(2)}, u32[]{:S(2)}) collective-permute-start(bf16[4,2,256,256]{3,2,1,0:T(8,128)(2,1)} %get-tuple-element.68.refs_4_), channel_id=1, source_target_pairs={{0,0},{1,1},{2,8},{3,9},{4,16},{5,17},{6,24},{7,25},{8,2},{9,3},{1... | collective-permute-start | bytes 3145736 | tf_op jit(solution)/shard_map/ppermute | solution.py:352
  116.3 47.2 %collective-permute-start.11 = (bf16[4,2,256,256]{3,2,1,0:T(8,128)(2,1)}, bf16[4,2,256,256]{3,2,1,0:T(8,128)(2,1)S(1)}, u32[]{:S(2)}, u32[]{:S(2)}) collective-permute-start(bf16[4,2,256,256]{3,2,1,0:T(8,128)(2,1)} %get-tuple-element.69), channel_id=1, source_target_pairs={{0,4},{1,5},{2,12},{3,13},{4,20},{5,21},{6,28},{7,29},{8,6},{9,7},... | collective-permute-start | bytes 3145736 | tf_op jit(solution)/shard_map/ppermute | solution.py:352
  117.1 46.4 %collective-permute-start.12 = (bf16[4,2,256,256]{3,2,1,0:T(8,128)(2,1)}, bf16[4,2,256,256]{3,2,1,0:T(8,128)(2,1)S(1)}, u32[]{:S(2)}, u32[]{:S(2)}) collective-permute-start(bf16[4,2,256,256]{3,2,1,0:T(8,128)(2,1)} %get-tuple-element.70.refs_4_), channel_id=1, source_target_pairs={{0,1},{1,0},{2,3},{3,2},{4,5},{5,4},{6,7},{7,6},{8,9},{9,8},{10,11... | collective-permute-start | bytes 3145736 | tf_op jit(solution)/shard_map/ppermute | solution.py:355
  117.4 46.2 %collective-permute-start.13 = (bf16[4,2,256,256]{3,2,1,0:T(8,128)(2,1)}, bf16[4,2,256,256]{3,2,1,0:T(8,128)(2,1)S(1)}, u32[]{:S(2)}, u32[]{:S(2)}) collective-permute-start(bf16[4,2,256,256]{3,2,1,0:T(8,128)(2,1)} %get-tuple-element.71.refs_6_), channel_id=1, source_target_pairs={{0,1},{1,0},{2,3},{3,2},{4,5},{5,4},{6,7},{7,6},{8,9},{9,8},{10,11... | collective-permute-start | bytes 3145736 | tf_op jit(solution)/shard_map/ppermute | solution.py:355
  118.6 45.9 %collective-permute-start.14 = (bf16[4,2,256,256]{3,2,1,0:T(8,128)(2,1)}, bf16[4,2,256,256]{3,2,1,0:T(8,128)(2,1)S(1)}, u32[]{:S(2)}, u32[]{:S(2)}) collective-permute-start(bf16[4,2,256,256]{3,2,1,0:T(8,128)(2,1)} %get-tuple-element.69), channel_id=1, source_target_pairs={{0,16},{8,24},{16,0},{24,8},{1,17},{9,25},{17,1},{25,9},{2,18},{10... | collective-permute-start | bytes 3145736 | tf_op jit(solution)/shard_map/ppermute | solution.py:343
  165.8 47.3 %collective-permute-start.15 = (bf16[4,2,256,256]{3,2,1,0:T(8,128)(2,1)}, bf16[4,2,256,256]{3,2,1,0:T(8,128)(2,1)S(1)}, u32[]{:S(2)}, u32[]{:S(2)}) collective-permute-start(bf16[4,2,256,256]{3,2,1,0:T(8,128)(2,1)} %get-tuple-element.72.refs_2_), channel_id=1, source_target_pairs={{0,2},{1,3},{2,10},{3,11},{4,18},{5,19},{6,26},{7,27},{8,0},{9,1},... | collective-permute-start | bytes 3145736 | tf_op jit(solution)/shard_map/ppermute | solution.py:352
  168.7 47.7 %collective-permute-start.16 = (bf16[4,2,256,256]{3,2,1,0:T(8,128)(2,1)}, bf16[4,2,256,256]{3,2,1,0:T(8,128)(2,1)S(1)}, u32[]{:S(2)}, u32[]{:S(2)}) collective-permute-start(bf16[4,2,256,256]{3,2,1,0:T(8,128)(2,1)} %get-tuple-element.73), channel_id=1, source_target_pairs={{0,6},{1,7},{2,14},{3,15},{4,22},{5,23},{6,30},{7,31},{8,4},{9,5},... | collective-permute-start | bytes 3145736 | tf_op jit(solution)/shard_map/ppermute | solution.py:352
  168.8 47.7 %collective-permute-start.17 = (bf16[4,2,256,256]{3,2,1,0:T(8,128)(2,1)}, bf16[4,2,256,256]{3,2,1,0:T(8,128)(2,1)S(1)}, u32[]{:S(2)}, u32[]{:S(2)}) collective-permute-start(bf16[4,2,256,256]{3,2,1,0:T(8,128)(2,1)} %get-tuple-element.74.refs_7_), channel_id=1, source_target_pairs={{0,1},{1,0},{2,3},{3,2},{4,5},{5,4},{6,7},{7,6},{8,9},{9,8},{10,11... | collective-permute-start | bytes 3145736 | tf_op jit(solution)/shard_map/ppermute | solution.py:355
  169.0 47.5 %collective-permute-start.18 = (bf16[4,2,256,256]{3,2,1,0:T(8,128)(2,1)}, bf16[4,2,256,256]{3,2,1,0:T(8,128)(2,1)}, u32[]{:S(2)}, u32[]{:S(2)}) collective-permute-start(bf16[4,2,256,256]{3,2,1,0:T(8,128)(2,1)} %get-tuple-element.75.refs_9_), channel_id=1, source_target_pairs={{0,1},{1,0},{2,3},{3,2},{4,5},{5,4},{6,7},{7,6},{8,9},{9,8},{10,11... | collective-permute-start | bytes 3145736 | tf_op jit(solution)/shard_map/ppermute | solution.py:355
  170.2 46.2 %collective-permute-start.19 = (bf16[4,2,256,256]{3,2,1,0:T(8,128)(2,1)}, bf16[4,2,256,256]{3,2,1,0:T(8,128)(2,1)}, u32[]{:S(2)}, u32[]{:S(2)}) collective-permute-start(bf16[4,2,256,256]{3,2,1,0:T(8,128)(2,1)} %get-tuple-element.73), channel_id=1, source_target_pairs={{0,24},{8,16},{16,8},{24,0},{1,25},{9,17},{17,9},{25,1},{2,26},{10... | collective-permute-start | bytes 3145736 | tf_op jit(solution)/shard_map/ppermute | solution.py:343
  217.8 48.1 %collective-permute-start.20 = (bf16[4,8,256,256]{3,2,1,0:T(8,128)(2,1)}, bf16[4,8,256,256]{3,2,1,0:T(8,128)(2,1)S(1)}, u32[]{:S(2)}, u32[]{:S(2)}) collective-permute-start(bf16[4,8,256,256]{3,2,1,0:T(8,128)(2,1)} %get-tuple-element.76), channel_id=1, source_target_pairs={{0,16},{1,17},{10,26},{11,27},{20,4},{21,5},{30,14},{31,15}} | collective-permute-start | bytes 12582920 | tf_op jit(solution)/shard_map/ppermute | solution.py:363
  218.7 4.2 collective-permute-start.23
  218.8 24.6 %collective-permute-start.21 = (bf16[4,2,256,256]{3,2,1,0:T(8,128)(2,1)}, bf16[4,2,256,256]{3,2,1,0:T(8,128)(2,1)S(1)}, u32[]{:S(2)}, u32[]{:S(2)}) collective-permute-start(bf16[4,2,256,256]{3,2,1,0:T(8,128)(2,1)} %get-tuple-element.77.refs_8_), channel_id=1, source_target_pairs={{0,1},{1,0},{2,3},{3,2},{4,5},{5,4},{6,7},{7,6},{8,9},{9,8},{10,11... | collective-permute-start | bytes 3145736 | tf_op jit(solution)/shard_map/ppermute | solution.py:355
  219.1 46.8 %collective-permute-start.22 = (bf16[4,2,256,256]{3,2,1,0:T(8,128)(2,1)}, bf16[4,2,256,256]{3,2,1,0:T(8,128)(2,1)S(1)}, u32[]{:S(2)}, u32[]{:S(2)}) collective-permute-start(bf16[4,2,256,256]{3,2,1,0:T(8,128)(2,1)} %get-tuple-element.78.refs_10_), channel_id=1, source_target_pairs={{0,1},{1,0},{2,3},{3,2},{4,5},{5,4},{6,7},{7,6},{8,9},{9,8},{10,11... | collective-permute-start | bytes 3145736 | tf_op jit(solution)/shard_map/ppermute | solution.py:355
  220.3 53.8 %collective-permute-start = (bf16[4,8,256,256]{3,2,1,0:T(8,128)(2,1)}, bf16[4,8,256,256]{3,2,1,0:T(8,128)(2,1)}, u32[]{:S(2)}, u32[]{:S(2)}) collective-permute-start(bf16[4,8,256,256]{3,2,1,0:T(8,128)(2,1)} %copy-done.9), channel_id=1, source_target_pairs={{0,8},{1,9},{10,2},{11,3},{20,28},{21,29},{30,22},{31,23}} | collective-permute-start | bytes 12582920 | tf_op jit(solution)/shard_map/ppermute | solution.py:363
  225.4 13.5 %copy-start.92 = (bf16[4,2,256,256]{3,2,1,0:T(8,128)(2,1)}, bf16[4,2,256,256]{3,2,1,0:T(8,128)(2,1)S(1)}, u32[]{:S(2)}) copy-start(bf16[4,2,256,256]{3,2,1,0:T(8,128)(2,1)S(1)} %collective-permute-done.23.refs_5_.refs_4_) | copy-start | bytes 3145732
  243.4 24.6 %copy-start.108 = (bf16[4,2,256,256]{3,2,1,0:T(8,128)(2,1)}, bf16[4,2,256,256]{3,2,1,0:T(8,128)(2,1)S(1)}, u32[]{:S(2)}) copy-start(bf16[4,2,256,256]{3,2,1,0:T(8,128)(2,1)S(1)} %collective-permute-done.21.refs_2_.refs_16_) | copy-start | bytes 3145732
  268.3 9.8 %collective-permute-start.24 = (bf16[4,8,256,256]{3,2,1,0:T(8,128)(2,1)}, bf16[4,8,256,256]{3,2,1,0:T(8,128)(2,1)}, u32[]{:S(2)}, u32[]{:S(2)}) collective-permute-start(bf16[4,8,256,256]{3,2,1,0:T(8,128)(2,1)} %get-tuple-element.80.refs_2_), channel_id=1, source_target_pairs={{16,24},{17,25},{26,18},{27,19},{4,12},{5,13},{14,6},{15,7}} | collective-permute-start | bytes 12582920 | tf_op jit(solution)/shard_map/ppermute | solution.py:363
  269.7 84.6 %collective-permute-start.30 = (bf16[4,8,256,256]{3,2,1,0:T(8,128)(2,1)}, bf16[4,8,256,256]{3,2,1,0:T(8,128)(2,1)}, u32[]{:S(2)}, u32[]{:S(2)}) collective-permute-start(bf16[4,8,256,256]{3,2,1,0:T(8,128)(2,1)} %get-tuple-element.88.refs_1_), channel_id=1, source_target_pairs={{0,16},{1,17},{10,26},{11,27},{20,4},{21,5},{30,14},{31,15}} | collective-permute-start | bytes 12582920 | tf_op jit(solution)/shard_map/ppermute | solution.py:363
  287.9 16.9 %copy-start.105 = (s32[4]{0:T(128)S(1)}, s32[4]{0:T(128)}, u32[]{:S(2)}) copy-start(s32[4]{0:T(128)} %constant.152.clone.crows_ref) | copy-start | bytes 52
  299.6 50.2 %collective-permute-start.25 = (bf16[4,2,256,256]{3,2,1,0:T(8,128)(2,1)}, bf16[4,2,256,256]{3,2,1,0:T(8,128)(2,1)}, u32[]{:S(2)}, u32[]{:S(2)}) collective-permute-start(bf16[4,2,256,256]{3,2,1,0:T(8,128)(2,1)} %get-tuple-element.81.refs_4_), channel_id=1, source_target_pairs={{0,0},{1,1},{2,8},{3,9},{4,16},{5,17},{6,24},{7,25},{8,2},{9,3},{1... | collective-permute-start | bytes 3145736 | tf_op jit(solution)/shard_map/ppermute | solution.py:352
  303.4 48.7 %collective-permute-start.26 = (bf16[4,2,256,256]{3,2,1,0:T(8,128)(2,1)}, bf16[4,2,256,256]{3,2,1,0:T(8,128)(2,1)}, u32[]{:S(2)}, u32[]{:S(2)}) collective-permute-start(bf16[4,2,256,256]{3,2,1,0:T(8,128)(2,1)} %get-tuple-element.84), channel_id=1, source_target_pairs={{0,4},{1,5},{2,12},{3,13},{4,20},{5,21},{6,28},{7,29},{8,6},{9,7},... | collective-permute-start | bytes 3145736 | tf_op jit(solution)/shard_map/ppermute | solution.py:352
  303.6 50.7 %collective-permute-start.27 = (bf16[4,2,256,256]{3,2,1,0:T(8,128)(2,1)}, bf16[4,2,256,256]{3,2,1,0:T(8,128)(2,1)}, u32[]{:S(2)}, u32[]{:S(2)}) collective-permute-start(bf16[4,2,256,256]{3,2,1,0:T(8,128)(2,1)} %get-tuple-element.84), channel_id=1, source_target_pairs={{0,16},{8,24},{16,0},{24,8},{1,17},{9,25},{17,1},{25,9},{2,18},{10... | collective-permute-start | bytes 3145736 | tf_op jit(solution)/shard_map/ppermute | solution.py:343
  354.3 27.0 %copy-start.66 = (bf16[4,2,256,256]{3,2,1,0:T(8,128)(2,1)S(1)}, bf16[4,2,256,256]{3,2,1,0:T(8,128)(2,1)}, u32[]{:S(2)}) copy-start(bf16[4,2,256,256]{3,2,1,0:T(8,128)(2,1)} %get-tuple-element.87.refs_3_.refs_1_) | copy-start | bytes 3145732
  354.3 27.0 %collective-permute-start.31 = (bf16[4,8,256,256]{3,2,1,0:T(8,128)(2,1)}, bf16[4,8,256,256]{3,2,1,0:T(8,128)(2,1)}, u32[]{:S(2)}, u32[]{:S(2)}) collective-permute-start(bf16[4,8,256,256]{3,2,1,0:T(8,128)(2,1)} %get-tuple-element.89.refs_0_), channel_id=1, source_target_pairs={{0,8},{1,9},{10,2},{11,3},{20,28},{21,29},{30,22},{31,23}} | collective-permute-start | bytes 12582920 | tf_op jit(solution)/shard_map/ppermute | solution.py:363
  357.1 24.5 %collective-permute-start.32 = (bf16[4,8,256,256]{3,2,1,0:T(8,128)(2,1)}, bf16[4,8,256,256]{3,2,1,0:T(8,128)(2,1)}, u32[]{:S(2)}, u32[]{:S(2)}) collective-permute-start(bf16[4,8,256,256]{3,2,1,0:T(8,128)(2,1)} %get-tuple-element.90.refs_2_), channel_id=1, source_target_pairs={{16,24},{17,25},{26,18},{27,19},{4,12},{5,13},{14,6},{15,7}} | collective-permute-start | bytes 12582920 | tf_op jit(solution)/shard_map/ppermute | solution.py:363
  358.5 22.8 %collective-permute-start.28 = (bf16[4,2,256,256]{3,2,1,0:T(8,128)(2,1)}, bf16[4,2,256,256]{3,2,1,0:T(8,128)(2,1)}, u32[]{:S(2)}, u32[]{:S(2)}) collective-permute-start(bf16[4,2,256,256]{3,2,1,0:T(8,128)(2,1)} %get-tuple-element.85.refs_5_), channel_id=1, source_target_pairs={{0,8},{8,0},{16,24},{24,16},{1,9},{9,1},{17,25},{25,17},{2,10},{10... | collective-permute-start | bytes 3145736 | tf_op jit(solution)/shard_map/ppermute | solution.py:343
  376.0 47.5 %collective-permute-start.29 = (bf16[4,2,256,256]{3,2,1,0:T(8,128)(2,1)}, bf16[4,2,256,256]{3,2,1,0:T(8,128)(2,1)}, u32[]{:S(2)}, u32[]{:S(2)}) collective-permute-start(bf16[4,2,256,256]{3,2,1,0:T(8,128)(2,1)} %get-tuple-element.86.refs_6_), channel_id=1, source_target_pairs={{0,24},{8,16},{16,8},{24,0},{1,25},{9,17},{17,9},{25,1},{2,26},{10... | collective-permute-start | bytes 3145736 | tf_op jit(solution)/shard_map/ppermute | solution.py:343
  376.0 47.9 %collective-permute-start.33 = (bf16[4,2,256,256]{3,2,1,0:T(8,128)(2,1)}, bf16[4,2,256,256]{3,2,1,0:T(8,128)(2,1)}, u32[]{:S(2)}, u32[]{:S(2)}) collective-permute-start(bf16[4,2,256,256]{3,2,1,0:T(8,128)(2,1)} %get-tuple-element.85.refs_5_), channel_id=1, source_target_pairs={{0,2},{1,3},{2,10},{3,11},{4,18},{5,19},{6,26},{7,27},{8,0},{9,1},... | collective-permute-start | bytes 3145736 | tf_op jit(solution)/shard_map/ppermute | solution.py:352
  381.3 47.1 %collective-permute-start.34 = (bf16[4,2,256,256]{3,2,1,0:T(8,128)(2,1)}, bf16[4,2,256,256]{3,2,1,0:T(8,128)(2,1)}, u32[]{:S(2)}, u32[]{:S(2)}) collective-permute-start(bf16[4,2,256,256]{3,2,1,0:T(8,128)(2,1)} %get-tuple-element.86.refs_6_), channel_id=1, source_target_pairs={{0,6},{1,7},{2,14},{3,15},{4,22},{5,23},{6,30},{7,31},{8,4},{9,5},... | collective-permute-start | bytes 3145736 | tf_op jit(solution)/shard_map/ppermute | solution.py:352
  381.3 47.1 %collective-permute-start.35 = (bf16[4,2,256,256]{3,2,1,0:T(8,128)(2,1)S(1)}, bf16[4,2,256,256]{3,2,1,0:T(8,128)(2,1)}, u32[]{:S(2)}, u32[]{:S(2)}) collective-permute-start(bf16[4,2,256,256]{3,2,1,0:T(8,128)(2,1)S(1)} %copy-done.66), channel_id=1, source_target_pairs={{0,1},{1,0},{2,3},{3,2},{4,5},{5,4},{6,7},{7,6},{8,9},{9,8},{10,11... | collective-permute-start | bytes 3145736 | tf_op jit(solution)/shard_map/ppermute | solution.py:355
  381.6 47.0 %collective-permute-start.36 = (bf16[4,2,256,256]{3,2,1,0:T(8,128)(2,1)}, bf16[4,2,256,256]{3,2,1,0:T(8,128)(2,1)}, u32[]{:S(2)}, u32[]{:S(2)}) collective-permute-start(bf16[4,2,256,256]{3,2,1,0:T(8,128)(2,1)} %get-tuple-element.93.refs_5_.refs_3_), channel_id=1, source_target_pairs={{0,1},{1,0},{2,3},{3,2},{4,5},{5,4},{6,7},{7,6},{8,9},{9,8},{10,11... | collective-permute-start | bytes 3145736 | tf_op jit(solution)/shard_map/ppermute | solution.py:355
  428.6 54.4 %collective-permute-start.40 = (bf16[4,2,256,256]{3,2,1,0:T(8,128)(2,1)}, bf16[4,2,256,256]{3,2,1,0:T(8,128)(2,1)S(1)}, u32[]{:S(2)}, u32[]{:S(2)}) collective-permute-start(bf16[4,2,256,256]{3,2,1,0:T(8,128)(2,1)} %get-tuple-element.99), channel_id=1, source_target_pairs={{0,4},{1,5},{2,12},{3,13},{4,20},{5,21},{6,28},{7,29},{8,6},{9,7},... | collective-permute-start | bytes 3145736 | tf_op jit(solution)/shard_map/ppermute | solution.py:352
  430.1 54.8 %collective-permute-start.41 = (bf16[4,2,256,256]{3,2,1,0:T(8,128)(2,1)}, bf16[4,2,256,256]{3,2,1,0:T(8,128)(2,1)S(1)}, u32[]{:S(2)}, u32[]{:S(2)}) collective-permute-start(bf16[4,2,256,256]{3,2,1,0:T(8,128)(2,1)} %get-tuple-element.99), channel_id=1, source_target_pairs={{0,16},{8,24},{16,0},{24,8},{1,17},{9,25},{17,1},{25,9},{2,18},{10... | collective-permute-start | bytes 3145736 | tf_op jit(solution)/shard_map/ppermute | solution.py:343
  430.7 33.5 %collective-permute-start.37 = (bf16[4,2,256,256]{3,2,1,0:T(8,128)(2,1)}, bf16[4,2,256,256]{3,2,1,0:T(8,128)(2,1)S(1)}, u32[]{:S(2)}, u32[]{:S(2)}) collective-permute-start(bf16[4,2,256,256]{3,2,1,0:T(8,128)(2,1)} %get-tuple-element.96.refs_4_.refs_2_), channel_id=1, source_target_pairs={{0,1},{1,0},{2,3},{3,2},{4,5},{5,4},{6,7},{7,6},{8,9},{9,8},{10,11... | collective-permute-start | bytes 3145736 | tf_op jit(solution)/shard_map/ppermute | solution.py:355
  430.9 44.4 %collective-permute-start.38 = (bf16[4,2,256,256]{3,2,1,0:T(8,128)(2,1)}, bf16[4,2,256,256]{3,2,1,0:T(8,128)(2,1)S(1)}, u32[]{:S(2)}, u32[]{:S(2)}) collective-permute-start(bf16[4,2,256,256]{3,2,1,0:T(8,128)(2,1)} %get-tuple-element.97.refs_6_.refs_4_), channel_id=1, source_target_pairs={{0,1},{1,0},{2,3},{3,2},{4,5},{5,4},{6,7},{7,6},{8,9},{9,8},{10,11... | collective-permute-start | bytes 3145736 | tf_op jit(solution)/shard_map/ppermute | solution.py:355
  432.1 50.8 %collective-permute-start.39 = (bf16[4,2,256,256]{3,2,1,0:T(8,128)(2,1)}, bf16[4,2,256,256]{3,2,1,0:T(8,128)(2,1)S(1)}, u32[]{:S(2)}, u32[]{:S(2)}) collective-permute-start(bf16[4,2,256,256]{3,2,1,0:T(8,128)(2,1)} %get-tuple-element.98.refs_4_), channel_id=1, source_target_pairs={{0,0},{1,1},{2,8},{3,9},{4,16},{5,17},{6,24},{7,25},{8,2},{9,3},{1... | collective-permute-start | bytes 3145736 | tf_op jit(solution)/shard_map/ppermute | solution.py:352
  464.2 26.5 %copy-start.67 = (bf16[4,2,256,256]{3,2,1,0:T(8,128)(2,1)S(1)}, bf16[4,2,256,256]{3,2,1,0:T(8,128)(2,1)}, u32[]{:S(2)}) copy-start(bf16[4,2,256,256]{3,2,1,0:T(8,128)(2,1)} %get-tuple-element.87.refs_3_.refs_1_) | copy-start | bytes 3145732
  464.2 20.7 %copy-start.86 = (bf16[4,2,256,256]{3,2,1,0:T(8,128)(2,1)}, bf16[4,2,256,256]{3,2,1,0:T(8,128)(2,1)S(1)}, u32[]{:S(2)}) copy-start(bf16[4,2,256,256]{3,2,1,0:T(8,128)(2,1)S(1)} %collective-permute-done.37.refs_8_.refs_4_.refs_6_) | copy-start | bytes 3145732
  485.9 49.9 %collective-permute-start.43 = (bf16[4,2,256,256]{3,2,1,0:T(8,128)(2,1)}, bf16[4,2,256,256]{3,2,1,0:T(8,128)(2,1)S(1)}, u32[]{:S(2)}, u32[]{:S(2)}) collective-permute-start(bf16[4,2,256,256]{3,2,1,0:T(8,128)(2,1)} %get-tuple-element.101), channel_id=1, source_target_pairs={{0,6},{1,7},{2,14},{3,15},{4,22},{5,23},{6,30},{7,31},{8,4},{9,5},... | collective-permute-start | bytes 3145736 | tf_op jit(solution)/shard_map/ppermute | solution.py:352
  485.9 52.5 %collective-permute-start.46 = (bf16[4,2,256,256]{3,2,1,0:T(8,128)(2,1)}, bf16[4,2,256,256]{3,2,1,0:T(8,128)(2,1)S(1)}, u32[]{:S(2)}, u32[]{:S(2)}) collective-permute-start(bf16[4,2,256,256]{3,2,1,0:T(8,128)(2,1)} %get-tuple-element.101), channel_id=1, source_target_pairs={{0,24},{8,16},{16,8},{24,0},{1,25},{9,17},{17,9},{25,1},{2,26},{10... | collective-permute-start | bytes 3145736 | tf_op jit(solution)/shard_map/ppermute | solution.py:343
  487.5 48.2 %collective-permute-start.42 = (bf16[4,2,256,256]{3,2,1,0:T(8,128)(2,1)}, bf16[4,2,256,256]{3,2,1,0:T(8,128)(2,1)S(1)}, u32[]{:S(2)}, u32[]{:S(2)}) collective-permute-start(bf16[4,2,256,256]{3,2,1,0:T(8,128)(2,1)} %get-tuple-element.100.refs_2_), channel_id=1, source_target_pairs={{0,2},{1,3},{2,10},{3,11},{4,18},{5,19},{6,26},{7,27},{8,0},{9,1},... | collective-permute-start | bytes 3145736 | tf_op jit(solution)/shard_map/ppermute | solution.py:352
  489.2 46.6 %collective-permute-start.44 = (bf16[4,2,256,256]{3,2,1,0:T(8,128)(2,1)}, bf16[4,2,256,256]{3,2,1,0:T(8,128)(2,1)S(1)}, u32[]{:S(2)}, u32[]{:S(2)}) collective-permute-start(bf16[4,2,256,256]{3,2,1,0:T(8,128)(2,1)} %get-tuple-element.102.refs_15_), channel_id=1, source_target_pairs={{0,1},{1,0},{2,3},{3,2},{4,5},{5,4},{6,7},{7,6},{8,9},{9,8},{10,11... | collective-permute-start | bytes 3145736 | tf_op jit(solution)/shard_map/ppermute | solution.py:355
  489.4 47.4 %collective-permute-start.45 = (bf16[4,2,256,256]{3,2,1,0:T(8,128)(2,1)}, bf16[4,2,256,256]{3,2,1,0:T(8,128)(2,1)S(1)}, u32[]{:S(2)}, u32[]{:S(2)}) collective-permute-start(bf16[4,2,256,256]{3,2,1,0:T(8,128)(2,1)} %get-tuple-element.103.refs_17_), channel_id=1, source_target_pairs={{0,1},{1,0},{2,3},{3,2},{4,5},{5,4},{6,7},{7,6},{8,9},{9,8},{10,11... | collective-permute-start | bytes 3145736 | tf_op jit(solution)/shard_map/ppermute | solution.py:355
  539.4 2.9 collective-permute-start.47
  539.9 54.1 %collective-permute-start.48 = (bf16[4,2,256,256]{3,2,1,0:T(8,128)(2,1)}, bf16[4,2,256,256]{3,2,1,0:T(8,128)(2,1)}, u32[]{:S(2)}, u32[]{:S(2)}) collective-permute-start(bf16[4,2,256,256]{3,2,1,0:T(8,128)(2,1)} %get-tuple-element.105.refs_16_), channel_id=1, source_target_pairs={{0,1},{1,0},{2,3},{3,2},{4,5},{5,4},{6,7},{7,6},{8,9},{9,8},{10,11... | collective-permute-start | bytes 3145736 | tf_op jit(solution)/shard_map/ppermute | solution.py:355
  540.2 19.9 %copy-start.3 = (bf16[4,256,2048]{2,1,0:T(8,128)(2,1)S(1)}, bf16[4,256,2048]{2,1,0:T(8,128)(2,1)}, u32[]{:S(2)}) copy-start(bf16[4,256,2048]{2,1,0:T(8,128)(2,1)} %copy-done.1) | copy-start | bytes 12582916
  540.2 19.9 %copy-start.6 = (bf16[4,256,2048]{2,1,0:T(8,128)(2,1)S(1)}, bf16[4,256,2048]{2,1,0:T(8,128)(2,1)}, u32[]{:S(2)}) copy-start(bf16[4,256,2048]{2,1,0:T(8,128)(2,1)} %copy-done.5) | copy-start | bytes 12582916
  540.2 53.8 %collective-permute-start.49 = (bf16[4,2,256,256]{3,2,1,0:T(8,128)(2,1)}, bf16[4,2,256,256]{3,2,1,0:T(8,128)(2,1)}, u32[]{:S(2)}, u32[]{:S(2)}) collective-permute-start(bf16[4,2,256,256]{3,2,1,0:T(8,128)(2,1)} %get-tuple-element.106.refs_18_), channel_id=1, source_target_pairs={{0,1},{1,0},{2,3},{3,2},{4,5},{5,4},{6,7},{7,6},{8,9},{9,8},{10,11... | collective-permute-start | bytes 3145736 | tf_op jit(solution)/shard_map/ppermute | solution.py:355
  543.9 16.2 %copy-start.79 = (bf16[4,2,256,256]{3,2,1,0:T(8,128)(2,1)S(1)}, bf16[4,2,256,256]{3,2,1,0:T(8,128)(2,1)}, u32[]{:S(2)}) copy-start(bf16[4,2,256,256]{3,2,1,0:T(8,128)(2,1)} %get-tuple-element.106.refs_18_) | copy-start | bytes 3145732
  543.9 16.2 %copy-start.81 = (bf16[4,2,256,256]{3,2,1,0:T(8,128)(2,1)S(1)}, bf16[4,2,256,256]{3,2,1,0:T(8,128)(2,1)}, u32[]{:S(2)}) copy-start(bf16[4,2,256,256]{3,2,1,0:T(8,128)(2,1)} %get-tuple-element.105.refs_16_) | copy-start | bytes 3145732
  562.5 14.9 %copy-start.58 = (bf16[8,4,256,256]{3,2,1,0:T(8,128)(2,1)S(1)}, bf16[8,4,256,256]{3,2,1,0:T(8,128)(2,1)}, u32[]{:S(2)}) copy-start(bf16[8,4,256,256]{3,2,1,0:T(8,128)(2,1)} %copy-done.57) | copy-start | bytes 12582916
  562.5 14.9 %copy-start.61 = (bf16[4,2,256,256]{3,2,1,0:T(8,128)(2,1)S(1)}, bf16[4,2,256,256]{3,2,1,0:T(8,128)(2,1)}, u32[]{:S(2)}) copy-start(bf16[4,2,256,256]{3,2,1,0:T(8,128)(2,1)} %copy-done.59) | copy-start | bytes 3145732
  577.4 16.5 %copy-start.73 = (bf16[4,2,256,256]{3,2,1,0:T(8,128)(2,1)S(1)}, bf16[4,2,256,256]{3,2,1,0:T(8,128)(2,1)}, u32[]{:S(2)}) copy-start(bf16[4,2,256,256]{3,2,1,0:T(8,128)(2,1)} %copy-done.72) | copy-start | bytes 3145732
  577.5 16.5 %copy-start.75 = (bf16[4,2,256,256]{3,2,1,0:T(8,128)(2,1)S(1)}, bf16[4,2,256,256]{3,2,1,0:T(8,128)(2,1)}, u32[]{:S(2)}) copy-start(bf16[4,2,256,256]{3,2,1,0:T(8,128)(2,1)} %copy-done.74) | copy-start | bytes 3145732
  (96 other events, 316.6 us)
